TPU v7x, 32 devices: a whole 2x2x4 slice. The times are simulated.
32 devices in a mesh: pts: 8 (over z, x), rhs: 4 (over y, core).
Axes of the slice: x: 2, y: 2, z: 4, core: 2. Of those that a mesh axis runs over, the one named last changes fastest.
Arguments:
- points: bfloat16 [16384, 32], P('pts'), may hold values from -0.5 to 0.5
- noise_var: float32 [16384], P('pts'), may hold values from 0.5 to 0.6
- right_side: float32 [64, 16384], P('rhs', 'pts'), may hold values from -12 to 12
- pattern: int32 [128, 33], P('pts'), may hold values from 0 to 1, as said below
Outputs:
- solution: float32 [64, 16384], P('rhs', 'pts')
- residual: float32 [64, 16384], P('rhs', 'pts')
- res_image: float32 [64, 16384], P('rhs', 'pts')
Inputs may be any that keep to these rules, and one draw needn't show every extreme that they name: Symmetric: pattern[b, 16 + d] = pattern[b + d, 16 - d]; the centre column is 1; entries naming a block outside 0 to 127 are 0.
All inputs are finite; a program needn't handle non-finite values.
Results may differ from a plain program's by a relative error of at most 0.0036.
Values may be sent and summed in bfloat16 or wider, within the bound.
No kernel may reach another device: no remote copies, remote signals or barrier semaphores. Data moves between devices by JAX's collectives and lax.ppermute only.
A program may use at most 64 MiB of HBM per device.

v0:
```python
import jax
import jax.numpy as jnp
from jax import lax
from jax.sharding import PartitionSpec as P

F = 32
BLK = 128
REACH = 16
ITERS = 2
WIDE = 33
WEXP = 18


group_tiles = 64


def with_halo(cells, sides, width):
    for axis, dim in sides:
        count = lax.axis_size(axis)
        ends = count - 1
        head = lax.slice_in_dim(cells, 0, width, axis=dim)
        tail = lax.slice_in_dim(cells, cells.shape[dim] - width, cells.shape[dim], axis=dim)
        cells = jnp.concatenate(
            [
                lax.ppermute(tail, axis, [(i, (i + 1) % count) for i in range(ends)]),
                cells,
                lax.ppermute(head, axis, [((i + 1) % count, i) for i in range(ends)]),
            ],
            axis=dim,
        )
    return cells


def kernel_block(left_points, right_points, left_squares, right_squares):
    cross_terms = jnp.einsum(
        "gif,gjf->gij", left_points, right_points, preferred_element_type=jnp.float32
    )
    dist_squared = jnp.maximum(
        left_squares[:, :, None] + right_squares[:, None, :] - 2.0 * cross_terms, 0.0
    )
    radius = jnp.sqrt(dist_squared)
    return jnp.maximum(1.0 - radius, 0.0) ** WEXP * (WEXP * radius + 1.0)


def per_device(points, noise_var, right_side, pattern):
    local_rows = points.shape[0]
    block_count = local_rows // BLK
    rim_rows = REACH * BLK
    kernel_scale = 1.0 / (4 * BLK)
    wide_points = with_halo(points, (("pts", 0),), rim_rows)
    wide_squares = jnp.sum(jnp.square(wide_points.astype(jnp.float32)), axis=1)
    point_blocks = wide_points.reshape(-1, BLK, F)
    square_blocks = wide_squares.reshape(-1, BLK)
    flat_mask = pattern.reshape(-1)
    live_count = jnp.sum(flat_mask)
    slot_order = jnp.argsort(1 - flat_mask, stable=True)
    rhs_ranks = lax.axis_size("rhs")
    rhs_index = lax.axis_index("rhs")
    my_slots = lax.dynamic_index_in_dim(
        slot_order.reshape(-1, rhs_ranks), rhs_index, 1, keepdims=False
    )
    my_count = jnp.maximum(live_count - rhs_index + rhs_ranks - 1, 0) // rhs_ranks
    slot_len = -(-my_slots.shape[0] // group_tiles) * group_tiles
    my_slots = jnp.pad(my_slots, (0, slot_len - my_slots.shape[0]))

    def accumulate(wide_vec):
        width = wide_vec.shape[0]
        vec_blocks = wide_vec.reshape(width, -1, BLK)

        def turn(turn_index, running):
            first_slot = turn_index * group_tiles
            slot_ids = lax.dynamic_slice_in_dim(my_slots, first_slot, group_tiles)
            valid_mask = first_slot + jnp.arange(group_tiles, dtype=jnp.int32) < my_count
            home_block = slot_ids // WIDE
            other_block = home_block + slot_ids % WIDE
            profile = kernel_block(
                point_blocks[home_block + REACH],
                point_blocks[other_block],
                square_blocks[home_block + REACH],
                square_blocks[other_block],
            )
            weights = (profile * valid_mask.astype(jnp.float32)[:, None, None]).astype(jnp.bfloat16)
            contribution = jnp.einsum(
                "gij,cgj->cgi",
                weights,
                vec_blocks[:, other_block],
                preferred_element_type=jnp.float32,
            )
            return running.at[:, home_block].add(contribution)

        turns = (my_count + group_tiles - 1) // group_tiles
        summed = lax.fori_loop(0, turns, turn, jnp.zeros((width, block_count, BLK), jnp.float32))
        return summed.reshape(width, local_rows)

    def apply_operator(vector):
        vec_low = vector.astype(jnp.bfloat16)
        wide_vec = with_halo(vec_low, (("pts", 1),), rim_rows)
        wide_all = lax.all_gather(wide_vec, "rhs", axis=0, tiled=True)
        summed = accumulate(wide_all)
        image_part = lax.psum_scatter(summed, "rhs", scatter_dimension=0, tiled=True)
        return noise_var[None, :] * vector + kernel_scale * image_part

    solution = jnp.zeros_like(right_side)
    residual = right_side
    res_image = apply_operator(residual)
    direction = jnp.zeros_like(right_side)
    dir_image = jnp.zeros_like(right_side)
    dir_twice = jnp.zeros_like(right_side)
    norm_prev = None
    step_prev = None
    for iteration in range(ITERS):
        norm_flat, curv_flat = lax.psum(
            (jnp.sum(residual * residual, axis=1), jnp.sum(res_image * residual, axis=1)), "pts"
        )
        norm_now = norm_flat[:, None]
        curvature = curv_flat[:, None]
        square_image = apply_operator(res_image)
        if iteration == 0:
            step_len = norm_now / curvature
            direction = residual
            dir_image = res_image
            dir_twice = square_image
        else:
            mix_ratio = norm_now / norm_prev
            step_len = norm_now / (curvature - mix_ratio * norm_now / step_prev)
            direction = residual + mix_ratio * direction
            dir_image = res_image + mix_ratio * dir_image
            dir_twice = square_image + mix_ratio * dir_twice
        solution = solution + step_len * direction
        residual = residual - step_len * dir_image
        res_image = res_image - step_len * dir_twice
        norm_prev = norm_now
        step_prev = step_len
    return (solution, residual, res_image)


def solution(mesh):
    placed = (P("pts", None), P("pts"), P("rhs", "pts"), P("pts", None))
    return jax.shard_map(
        per_device,
        mesh=mesh,
        in_specs=placed,
        out_specs=(P("rhs", "pts"), P("rhs", "pts"), P("rhs", "pts")),
        check_vma=False,
    )
```

profile of v0, /device:TPU:0, one launch (start us, length us, event | category | flops | bytes accessed | tf_op | source)
XLA Modules:
  0.0 282.4 jit_solution(17270775721972857675)
XLA Ops:
  7.2 0.9 convert_element_type.60
  8.2 4.8 %collective-permute-start = (bf16[16,2048]{1,0:T(8,128)(2,1)S(1)}, bf16[16,2048]{1,0:T(8,128)(2,1)S(1)}, u32[]{:S(2)}, u32[]{:S(2)}) collective-permute-start(bf16[16,2048]{1,0:T(8,128)(2,1)S(1)} %convert_element_type.60), channel_id=1, source_target_pairs={{0,4},{4,8},{8,12},{12,16},{16,20},{20,24},{24,28},{1,5},{5,9},{9,... | collective-permute-start | bytes 196616 | tf_op jit(solution)/shard_map/ppermute | solution.py:25
  13.0 1.3 collective-permute-start.1
  14.3 4.6 %collective-permute-start.2 = (bf16[2048,32]{0,1:T(8,128)(2,1)}, bf16[2048,32]{0,1:T(8,128)(2,1)S(1)}, u32[]{:S(2)}, u32[]{:S(2)}) collective-permute-start(bf16[2048,32]{0,1:T(8,128)(2,1)} %param.10), channel_id=1, source_target_pairs={{0,4},{4,8},{8,12},{12,16},{16,20},{20,24},{24,28},{1,5},{5,9},{9,... | collective-permute-start | bytes 393224 | tf_op jit(solution)/shard_map/ppermute | solution.py:25
  18.9 1.3 collective-permute-start.3
  20.2 1.3 broadcast_subtract_fusion
  22.3 4.4 %sort.17 = (s32[528]{0:T(1024)}, s32[528]{0:T(1024)S(1)}) sort(s32[528]{0:T(1024)S(1)} %sub.102, s32[528]{0:T(1024)S(1)} %iota.28), dimensions={0}, to_apply=%region_3.4 | sort | flops 5280 | bytes 8448 | tf_op jit(solution)/shard_map/jit(argsort)/sort | solution.py:56
  26.6 0.1 reshape.71
  26.8 0.2 dynamic-slice_reduce_fusion
  27.0 8.6 %all_gather.9 = bf16[64,6144]{1,0:T(8,128)(2,1)S(1)} all-gather(bf16[16,6144]{1,0:T(8,128)(2,1)S(1)} %pad_maximum_fusion), channel_id=1, replica_groups=mesh['pts'=8,'rhs'=4] {'rhs'}, dimensions={0}, use_global_device_ids=true | all-gather | bytes 983040 | tf_op jit(solution)/shard_map/all_gather | solution.py:98
  35.6 0.2 copy_bitcast_fusion.2
  35.9 0.8 copy.38
  36.8 0.1 multiply_reduce_fusion
  37.0 21.3 %while.36 = (s32[]{:T(128)}, f32[64,16,128]{2,0,1:T(8,128)S(1)}, s32[]{:T(128)}, s32[192]{0:T(256)S(1)}, bf16[64,48,128]{2,0,1:T(8,128)(2,1)S(1)}, /*index=5*/f3...) while((s32[]{:T(128)}, f32[64,16,128]{2,0,1:T(8,128)S(1)}, ...), condition=%wide.region_7.8_spmd, body=%wide.region_5.7_spmd.sunk | while | flops 218631744 | bytes 14889135 | solution.py:92
  37.0 0.1 compare_select_fusion.15
  37.1 2.2 gather_fusion
  39.3 2.1 gather_fusion.1
  41.4 0.6 gather_fusion.3
  42.0 0.6 gather_fusion.2
  42.6 1.7 gather_fusion.4
  44.3 6.9 %fusion.50 = f32[64,64,128]{2,1,0:T(8,128)} fusion(bf16[64,128,32]{2,1,0:T(8,128)(2,1)} %gather_fusion, bf16[64,128,32]{2,1,0:T(8,128)(2,1)} %gather_fusion.1, f32[64]{0:T(128)S(1)} %compare_convert_fusion.6, f32[64,128]{1,0:T(8,128)S(1)} %gather_fusion.2, f32[64,128]{1,0:T(8,128)S(1)} %gather_fusion.3, bf16[64,64,128]{2,1,0:T(8,128)(2,1)} %gather_fusion.4), kind=kOutput, calls=%fused_computation.19.clone.1 | convolution fusion | flops 218103808 | bytes 4260096 | tf_op jit(solution)/shard_map/while/body/gij,cgj->cgi/dot_general | solution.py:83
  51.2 7.0 %scatter_fusion = f32[64,16,128]{2,0,1:T(8,128)S(1)} fusion(f32[64,16,128]{2,0,1:T(8,128)S(1)} %get-tuple-element.637, s32[64]{0:T(128)S(1)} %get-tuple-element.597, f32[64,64,128]{2,1,0:T(8,128)} %fusion.50), kind=kCustom, calls=%fused_computation.15.clone.1 | custom fusion | flops 524288 | bytes 6291712 | tf_op jit(solution)/shard_map/while/body/scatter-add | solution.py:89
  58.3 0.8 copy_bitcast_fusion.5
  59.1 45.4 %reduce-scatter.4.cloned.1.call-done = f32[16,2048]{1,0:T(8,128)} async-done(((f32[64,2048]{1,0:T(8,128)}), f32[16,2048]{1,0:T(8,128)}) %reduce-scatter.4.cloned.1.call-update) | async-done | bytes 131088 | tf_op jit(solution)/shard_map/reduce_scatter | solution.py:100
  104.5 0.9 fusion.22
  105.5 3.4 %collective-permute-start.4 = (bf16[16,2048]{1,0:T(8,128)(2,1)S(1)}, bf16[16,2048]{1,0:T(8,128)(2,1)S(1)}, u32[]{:S(2)}, u32[]{:S(2)}) collective-permute-start(bf16[16,2048]{1,0:T(8,128)(2,1)S(1)} %get-tuple-element.436), channel_id=1, source_target_pairs={{0,4},{4,8},{8,12},{12,16},{16,20},{20,24},{24,28},{1,5},{5,9},{9,... | collective-permute-start | bytes 196616 | tf_op jit(solution)/shard_map/ppermute | solution.py:25
  108.9 1.3 collective-permute-start.5
  110.2 0.6 collective-permute-done.4
  110.8 4.3 %collective-permute-done.5 = bf16[16,2048]{1,0:T(8,128)(2,1)S(1)} collective-permute-done((bf16[16,2048]{1,0:T(8,128)(2,1)S(1)}, bf16[16,2048]{1,0:T(8,128)(2,1)S(1)}, u32[]{:S(2)}, u32[]{:S(2)}) %collective-permute-start.5) | collective-permute-done | bytes 65568 | tf_op jit(solution)/shard_map/ppermute | solution.py:27
  115.0 7.7 %all_gather.10 = bf16[64,6144]{1,0:T(8,128)(2,1)S(1)} all-gather(bf16[16,6144]{1,0:T(8,128)(2,1)S(1)} %pad_maximum_fusion.1), channel_id=1, replica_groups=mesh['pts'=8,'rhs'=4] {'rhs'}, dimensions={0}, use_global_device_ids=true | all-gather | bytes 983040 | tf_op jit(solution)/shard_map/all_gather | solution.py:98
  122.7 0.2 copy_bitcast_fusion.1
  123.0 21.3 %while.37 = (s32[]{:T(128)}, f32[64,16,128]{2,0,1:T(8,128)S(1)}, s32[]{:T(128)}, s32[192]{0:T(256)S(1)}, bf16[64,48,128]{2,0,1:T(8,128)(2,1)S(1)}, /*index=5*/f3...) while((s32[]{:T(128)}, f32[64,16,128]{2,0,1:T(8,128)S(1)}, ...), condition=%wide.region_15.16_spmd, body=%wide.region_13.15_spmd.sunk | while | flops 218631744 | bytes 14889135 | solution.py:92
  123.0 0.1 compare_select_fusion.17
  123.1 2.2 gather_fusion.5
  125.3 2.1 gather_fusion.6
  127.4 0.6 gather_fusion.8
  128.0 0.6 gather_fusion.7
  128.6 1.7 gather_fusion.9
  130.3 6.9 %fusion.54 = f32[64,64,128]{2,1,0:T(8,128)} fusion(bf16[64,128,32]{2,1,0:T(8,128)(2,1)} %gather_fusion.5, bf16[64,128,32]{2,1,0:T(8,128)(2,1)} %gather_fusion.6, f32[64]{0:T(128)S(1)} %compare_convert_fusion.7, f32[64,128]{1,0:T(8,128)S(1)} %gather_fusion.7, f32[64,128]{1,0:T(8,128)S(1)} %gather_fusion.8, bf16[64,64,128]{2,1,0:T(8,128)(2,1)} %gather_fusion.9), kind=kOutput, calls=%fused_computation.35.clone.1 | convolution fusion | flops 218103808 | bytes 4260096 | tf_op jit(solution)/shard_map/while/body/gij,cgj->cgi/dot_general | solution.py:83
  137.2 7.0 %scatter_fusion.1 = f32[64,16,128]{2,0,1:T(8,128)S(1)} fusion(f32[64,16,128]{2,0,1:T(8,128)S(1)} %get-tuple-element.673, s32[64]{0:T(128)S(1)} %get-tuple-element.609, f32[64,64,128]{2,1,0:T(8,128)} %fusion.54), kind=kCustom, calls=%fused_computation.16.clone.1 | custom fusion | flops 524288 | bytes 6291712 | tf_op jit(solution)/shard_map/while/body/scatter-add | solution.py:89
  144.3 0.8 copy_bitcast_fusion.4
  145.2 0.1 multiply_reduce_fusion.3
  145.3 40.8 %all-reduce.2 = (f32[16]{0:T(128)S(1)}, f32[16]{0:T(128)S(1)}) all-reduce(f32[16]{0:T(128)S(1)} %get-tuple-element.375, f32[16]{0:T(128)S(1)} %get-tuple-element.374), channel_id=1, replica_groups=mesh['pts'=8,'rhs'=4] {'pts'}, use_global_device_ids=true, to_apply=%region_1.0 | all-reduce | flops 32 | bytes 256 | tf_op jit(solution)/shard_map/psum | solution.py:112
  186.1 3.0 %reduce-scatter.6.cloned.1.call-done = f32[16,2048]{1,0:T(8,128)} async-done(((f32[64,2048]{1,0:T(8,128)}), f32[16,2048]{1,0:T(8,128)}) %reduce-scatter.6.cloned.1.call-update) | async-done | bytes 131088 | tf_op jit(solution)/shard_map/reduce_scatter | solution.py:100
  189.1 1.1 multiply_reduce_fusion.1
  190.2 3.4 %collective-permute-start.6 = (bf16[16,2048]{1,0:T(8,128)(2,1)S(1)}, bf16[16,2048]{1,0:T(8,128)(2,1)S(1)}, u32[]{:S(2)}, u32[]{:S(2)}) collective-permute-start(bf16[16,2048]{1,0:T(8,128)(2,1)S(1)} %get-tuple-element.446), channel_id=1, source_target_pairs={{0,4},{4,8},{8,12},{12,16},{16,20},{20,24},{24,28},{1,5},{5,9},{9,... | collective-permute-start | bytes 196616 | tf_op jit(solution)/shard_map/ppermute | solution.py:25
  193.6 1.3 collective-permute-start.7
  194.9 0.6 collective-permute-done.6
  195.5 4.3 %collective-permute-done.7 = bf16[16,2048]{1,0:T(8,128)(2,1)S(1)} collective-permute-done((bf16[16,2048]{1,0:T(8,128)(2,1)S(1)}, bf16[16,2048]{1,0:T(8,128)(2,1)S(1)}, u32[]{:S(2)}, u32[]{:S(2)}) %collective-permute-start.7) | collective-permute-done | bytes 65568 | tf_op jit(solution)/shard_map/ppermute | solution.py:27
  199.8 7.7 %all_gather.11 = bf16[64,6144]{1,0:T(8,128)(2,1)S(1)} all-gather(bf16[16,6144]{1,0:T(8,128)(2,1)S(1)} %pad_maximum_fusion.2), channel_id=1, replica_groups=mesh['pts'=8,'rhs'=4] {'rhs'}, dimensions={0}, use_global_device_ids=true | all-gather | bytes 983040 | tf_op jit(solution)/shard_map/all_gather | solution.py:98
  207.5 0.2 copy_bitcast_fusion
  207.7 21.4 %while.38 = (s32[]{:T(128)}, f32[64,16,128]{2,0,1:T(8,128)S(1)}, s32[]{:T(128)}, s32[192]{0:T(256)S(1)}, bf16[64,48,128]{2,0,1:T(8,128)(2,1)S(1)}, /*index=5*/f3...) while((s32[]{:T(128)}, f32[64,16,128]{2,0,1:T(8,128)S(1)}, ...), condition=%wide.region_21.22_spmd, body=%wide.region_19.21_spmd.sunk | while | flops 218631744 | bytes 14889135 | solution.py:92
  208.0 0.1 compare_select_fusion.19
  208.1 2.2 gather_fusion.10
  210.2 2.1 gather_fusion.11
  212.4 0.6 gather_fusion.13
  212.9 0.6 gather_fusion.12
  213.5 1.7 gather_fusion.14
  215.2 6.9 %fusion.58 = f32[64,64,128]{2,1,0:T(8,128)} fusion(bf16[64,128,32]{2,1,0:T(8,128)(2,1)} %gather_fusion.10, bf16[64,128,32]{2,1,0:T(8,128)(2,1)} %gather_fusion.11, f32[64]{0:T(128)S(1)} %compare_convert_fusion.8, f32[64,128]{1,0:T(8,128)S(1)} %gather_fusion.12, f32[64,128]{1,0:T(8,128)S(1)} %gather_fusion.13, bf16[64,64,128]{2,1,0:T(8,128)(2,1)} %gather_fusion.14), kind=kOutput, calls=%fused_computation.51.clone.1 | convolution fusion | flops 218103808 | bytes 4260096 | tf_op jit(solution)/shard_map/while/body/gij,cgj->cgi/dot_general | solution.py:83
  222.1 7.0 %scatter_fusion.2 = f32[64,16,128]{2,0,1:T(8,128)S(1)} fusion(f32[64,16,128]{2,0,1:T(8,128)S(1)} %get-tuple-element.709, s32[64]{0:T(128)S(1)} %get-tuple-element.621, f32[64,64,128]{2,1,0:T(8,128)} %fusion.58), kind=kCustom, calls=%fused_computation.17.clone.1 | custom fusion | flops 524288 | bytes 6291712 | tf_op jit(solution)/shard_map/while/body/scatter-add | solution.py:89
  229.2 0.8 copy_bitcast_fusion.3
  230.0 40.8 %all-reduce.1 = (f32[16]{0:T(128)S(1)}, f32[16]{0:T(128)S(1)}) all-reduce(f32[16]{0:T(128)S(1)} %get-tuple-element.373, f32[16]{0:T(128)S(1)} %get-tuple-element.372), channel_id=1, replica_groups=mesh['pts'=8,'rhs'=4] {'pts'}, use_global_device_ids=true, to_apply=%region_12.13 | all-reduce | flops 32 | bytes 256 | tf_op jit(solution)/shard_map/psum | solution.py:112
  270.9 3.2 %reduce-scatter.8.cloned.1.call-done = f32[16,2048]{1,0:T(8,128)} async-done(((f32[64,2048]{1,0:T(8,128)}), f32[16,2048]{1,0:T(8,128)}) %reduce-scatter.8.cloned.1.call-update) | async-done | bytes 131088 | tf_op jit(solution)/shard_map/reduce_scatter | solution.py:100
  274.1 1.8 multiply_subtract_fusion
  (44 shorter events, 0.6 us)
Async XLA Ops:
  7.2 28.7 %copy-start.2 = (bf16[2048,32]{0,1:T(8,128)(2,1)S(1)}, bf16[2048,32]{0,1:T(8,128)(2,1)}, u32[]{:S(2)}) copy-start(bf16[2048,32]{0,1:T(8,128)(2,1)} %param.10) | copy-start | bytes 393220
  7.2 97.4 %reduce-scatter.4.cloned.1.call-start = ((), (), s32[]{:S(2)}) async-start(), calls=%async_computation.3 | async-start | bytes 655360 | tf_op jit(solution)/shard_map/reduce_scatter | solution.py:100
  8.2 18.8 %collective-permute-start = (bf16[16,2048]{1,0:T(8,128)(2,1)S(1)}, bf16[16,2048]{1,0:T(8,128)(2,1)S(1)}, u32[]{:S(2)}, u32[]{:S(2)}) collective-permute-start(bf16[16,2048]{1,0:T(8,128)(2,1)S(1)} %convert_element_type.60), channel_id=1, source_target_pairs={{0,4},{4,8},{8,12},{12,16},{16,20},{20,24},{24,28},{1,5},{5,9},{9,... | collective-permute-start | bytes 196616 | tf_op jit(solution)/shard_map/ppermute | solution.py:25
  13.0 14.0 %collective-permute-start.1 = (bf16[16,2048]{1,0:T(8,128)(2,1)S(1)}, bf16[16,2048]{1,0:T(8,128)(2,1)S(1)}, u32[]{:S(2)}, u32[]{:S(2)}) collective-permute-start(bf16[16,2048]{1,0:T(8,128)(2,1)S(1)} %convert_element_type.60), channel_id=1, source_target_pairs={{4,0},{8,4},{12,8},{16,12},{20,16},{24,20},{28,24},{5,1},{9,5},{13... | collective-permute-start | bytes 196616 | tf_op jit(solution)/shard_map/ppermute | solution.py:27
  14.3 21.6 %collective-permute-start.2 = (bf16[2048,32]{0,1:T(8,128)(2,1)}, bf16[2048,32]{0,1:T(8,128)(2,1)S(1)}, u32[]{:S(2)}, u32[]{:S(2)}) collective-permute-start(bf16[2048,32]{0,1:T(8,128)(2,1)} %param.10), channel_id=1, source_target_pairs={{0,4},{4,8},{8,12},{12,16},{16,20},{20,24},{24,28},{1,5},{5,9},{9,... | collective-permute-start | bytes 393224 | tf_op jit(solution)/shard_map/ppermute | solution.py:25
  18.9 17.0 %collective-permute-start.3 = (bf16[2048,32]{0,1:T(8,128)(2,1)}, bf16[2048,32]{0,1:T(8,128)(2,1)S(1)}, u32[]{:S(2)}, u32[]{:S(2)}) collective-permute-start(bf16[2048,32]{0,1:T(8,128)(2,1)} %param.10), channel_id=1, source_target_pairs={{4,0},{8,4},{12,8},{16,12},{20,16},{24,20},{28,24},{5,1},{9,5},{13... | collective-permute-start | bytes 393224 | tf_op jit(solution)/shard_map/ppermute | solution.py:27
  37.0 67.6 %copy-start = (f32[16,2048]{1,0:T(8,128)S(1)}, f32[16,2048]{1,0:T(8,128)}, u32[]{:S(2)}) copy-start(f32[16,2048]{1,0:T(8,128)} %param.12) | copy-start | bytes 393220
  37.0 67.6 %copy-start.3 = (f32[2048]{0:T(1024)S(1)}, f32[2048]{0:T(1024)}, u32[]{:S(2)}) copy-start(f32[2048]{0:T(1024)} %param.11) | copy-start | bytes 24580
  59.1 130.0 %reduce-scatter.6.cloned.1.call-start = ((), (), s32[]{:S(2)}) async-start(), calls=%async_computation.4 | async-start | bytes 655360 | tf_op jit(solution)/shard_map/reduce_scatter | solution.py:100
  105.5 5.3 %collective-permute-start.4 = (bf16[16,2048]{1,0:T(8,128)(2,1)S(1)}, bf16[16,2048]{1,0:T(8,128)(2,1)S(1)}, u32[]{:S(2)}, u32[]{:S(2)}) collective-permute-start(bf16[16,2048]{1,0:T(8,128)(2,1)S(1)} %get-tuple-element.436), channel_id=1, source_target_pairs={{0,4},{4,8},{8,12},{12,16},{16,20},{20,24},{24,28},{1,5},{5,9},{9,... | collective-permute-start | bytes 196616 | tf_op jit(solution)/shard_map/ppermute | solution.py:25
  108.9 6.2 %collective-permute-start.5 = (bf16[16,2048]{1,0:T(8,128)(2,1)S(1)}, bf16[16,2048]{1,0:T(8,128)(2,1)S(1)}, u32[]{:S(2)}, u32[]{:S(2)}) collective-permute-start(bf16[16,2048]{1,0:T(8,128)(2,1)S(1)} %get-tuple-element.436), channel_id=1, source_target_pairs={{4,0},{8,4},{12,8},{16,12},{20,16},{24,20},{28,24},{5,1},{9,5},{13... | collective-permute-start | bytes 196616 | tf_op jit(solution)/shard_map/ppermute | solution.py:27
  145.1 129.0 %reduce-scatter.8.cloned.1.call-start = ((), (), s32[]{:S(2)}) async-start(), calls=%async_computation.5 | async-start | bytes 655360 | tf_op jit(solution)/shard_map/reduce_scatter | solution.py:100
  190.2 5.3 %collective-permute-start.6 = (bf16[16,2048]{1,0:T(8,128)(2,1)S(1)}, bf16[16,2048]{1,0:T(8,128)(2,1)S(1)}, u32[]{:S(2)}, u32[]{:S(2)}) collective-permute-start(bf16[16,2048]{1,0:T(8,128)(2,1)S(1)} %get-tuple-element.446), channel_id=1, source_target_pairs={{0,4},{4,8},{8,12},{12,16},{16,20},{20,24},{24,28},{1,5},{5,9},{9,... | collective-permute-start | bytes 196616 | tf_op jit(solution)/shard_map/ppermute | solution.py:25
  193.6 6.2 %collective-permute-start.7 = (bf16[16,2048]{1,0:T(8,128)(2,1)S(1)}, bf16[16,2048]{1,0:T(8,128)(2,1)S(1)}, u32[]{:S(2)}, u32[]{:S(2)}) collective-permute-start(bf16[16,2048]{1,0:T(8,128)(2,1)S(1)} %get-tuple-element.446), channel_id=1, source_target_pairs={{4,0},{8,4},{12,8},{16,12},{20,16},{24,20},{28,24},{5,1},{9,5},{13... | collective-permute-start | bytes 196616 | tf_op jit(solution)/shard_map/ppermute | solution.py:27
  207.7 66.3 %copy-start.1 = (f32[16,2048]{1,0:T(8,128)S(1)}, f32[16,2048]{1,0:T(8,128)}, u32[]{:S(2)}) copy-start(f32[16,2048]{1,0:T(8,128)} %reduce-scatter.6.cloned.1.call-done) | copy-start | bytes 393220
Sparse Core Ops, SparseCore 0:
  59.2 45.2 reduce-scatter.3
  145.2 43.8 reduce-scatter.5
  230.2 43.8 reduce-scatter.7
where the time goes:
time: 284 us; the launch traced here: 282 us
  blocking collectives  106 us (37%)
  waiting for transfers between devices  61.3 us (22%)
  other arithmetic  32.3 us (11%)
  local copies, waits for them, and re-layouts  26 us (9%)
  starting transfers between devices  21.4 us (8%)
  matrix products  20.7 us (7%)
  between operations  14.7 us (5%)
    psum x2, blocking collectives, per_device(): lax.psum((jnp.sum(residual * residual, axis=1), jnp.sum(res_image * resid...  81.7 us
    reduce_scatter x3, waiting for transfers between devices, apply_operator(): lax.psum_scatter(summed, 'rhs', scatter_dimension=0, tiled=True)  51.6 us
    all_gather x3, blocking collectives, apply_operator(): wide_all = lax.all_gather(wide_vec, 'rhs', axis=0, tiled=True)  24 us
    scatter-add x3, other arithmetic, turn(): return running.at[:, home_block].add(contribution)  21.1 us
    dot_general x3, matrix products, turn(): jnp.einsum('gij,cgj->cgi', weights, vec_blocks[:, other_block], preferred...  20.7 us
    ppermute x4, starting transfers between devices, with_halo(): lax.ppermute(tail, axis, [(i, (i + 1) % count) for i in range(ends)])  16.1 us
    ppermute x4, waiting for transfers between devices, with_halo(): lax.ppermute(head, axis, [((i + 1) % count, i) for i in range(ends)])  8.55 us
    gather x3, local copies, waits for them, and re-layouts, turn(): point_blocks[home_block + REACH]  6.5 us
  transfers between devices with their start and end apart: 11, of which 7 were waited for; matrix products, arithmetic and copies ran while one was open for 2% of the time, Pallas kernels for 0%

commit v1 on v0

v1 whole, which is shorter than its diff:
```python
import functools

import jax
import jax.numpy as jnp
from jax import lax
from jax.experimental import pallas as pl
from jax.experimental.pallas import tpu as pltpu
from jax.sharding import PartitionSpec as P

F = 32
BLK = 128
REACH = 16
WIDE = 33
WEXP = 18
LANES = 128
PACK = LANES // F
GAMMA = float(WEXP) ** (1.0 / (WEXP + 1))
GAMMA_SQ = GAMMA * GAMMA
OFFSET = GAMMA * (WEXP + 1) / WEXP
TINY = 1e-30
SHIFT = 2.0 / (0.5 + 0.6)
SUMS = 9
UNROLL = 4
MIB = 1 << 20

f32 = jnp.float32
bf16 = jnp.bfloat16


def rounded(x):
    return x.astype(bf16).astype(f32)


def three_parts(x):
    high = rounded(x)
    rest = x - high
    middle = rounded(rest)
    return high, middle, rounded(rest - middle)


def spread_features(packed, group):
    source = lax.broadcasted_iota(jnp.int32, (LANES, LANES), 0)
    target = lax.broadcasted_iota(jnp.int32, (LANES, LANES), 1)
    pick = (source == group * F + target % F) & (target < 3 * F)
    return jnp.dot(packed, pick.astype(bf16), preferred_element_type=f32)


def square_parts(features, lane):
    squares = jnp.sum(jnp.where(lane < F, features * features, 0.0), axis=1, keepdims=True)
    return three_parts(GAMMA_SQ * squares)


def left_features(features, lane, parts):
    out = jnp.where(lane < 3 * F, features, jnp.where(lane < 3 * F + 6, 1.0, 0.0))
    for at, part in enumerate(parts):
        out = jnp.where(lane == 3 * F + at, part, out)
    return out


def right_features(features, lane, parts):
    high, middle, low = three_parts((-2.0 * GAMMA_SQ) * features)
    out = jnp.where(lane < F, high, jnp.where(lane < 2 * F, middle, jnp.where(lane < 3 * F, low, 0.0)))
    out = jnp.where((lane >= 3 * F) & (lane < 3 * F + 3), 1.0, out)
    for at, part in enumerate(parts):
        out = jnp.where(lane == 3 * F + 3 + at, part, out)
    return out


def fill_features(packed, left_ref, right_ref):
    rows = packed.shape[0]
    per = rows // BLK
    lane = lax.broadcasted_iota(jnp.int32, (rows, LANES), 1)
    for group in range(PACK):
        features = spread_features(packed, group)
        parts = square_parts(features, lane)
        left = left_features(features, lane, parts).astype(bf16)
        for at in range(per):
            left_ref[group * per + at] = left[at * BLK : (at + 1) * BLK]
        if right_ref is not None:
            right = right_features(features, lane, parts)
            for at in range(per):
                right_ref[group * per + at] = right[at * BLK : (at + 1) * BLK].T.astype(bf16)


def tile_values(left, right):
    scaled = jnp.dot(left, right, preferred_element_type=f32)
    scaled = jnp.maximum(scaled, TINY)
    s = jnp.maximum(GAMMA - scaled * lax.rsqrt(scaled), 0.0)
    s2 = s * s
    s4 = s2 * s2
    s8 = s4 * s4
    s16 = s8 * s8
    return ((s16 * s2) * (OFFSET - s)).astype(bf16)


def make_tiles(count, list_ref, left_ref, right_ref, tiles_ref):
    def step(at, carry):
        for k in range(UNROLL):
            entry = list_ref[at * UNROLL + k]
            slot = entry & 1023
            other = (entry >> 10) & 63
            home = entry >> 16
            tiles_ref[slot] = tile_values(left_ref[other], right_ref[home])
        return carry

    lax.fori_loop(0, (count + UNROLL - 1) // UNROLL, step, 0)


def list_tiles(blocks, low, high, shift, pattern_ref, list_ref, spare):
    def per_home(home, count):
        def per_other(other, count):
            column = other - home + shift
            slot = home * WIDE + column
            list_ref[count] = (((home << 6) + other) << 10) + slot
            return count + pattern_ref[home, column]

        return lax.fori_loop(low(home), high(home), per_other, count)

    count = lax.fori_loop(0, blocks, per_home, 0)
    for k in range(UNROLL - 1):
        list_ref[count + k] = spare
    return count


def prep_kernel(points_ref, vec_ref, out_ref):
    rows = points_ref.shape[0] // PACK
    out_ref[:rows, :] = jnp.concatenate(
        [points_ref[g * rows : (g + 1) * rows, :] for g in range(PACK)], axis=1
    )
    put_blocks(vec_ref[...].astype(bf16), out_ref, rows)


def put_blocks(values, out_ref, first):
    width = values.shape[0]
    for b in range(values.shape[1] // BLK):
        out_ref[first + b * width : first + (b + 1) * width, :] = values[:, b * BLK : (b + 1) * BLK]


def local_kernel(blocks, pattern_ref, own_ref, tiles_ref, right_ref, left_ref, list_ref, dead_ref):
    rows = blocks * BLK // PACK
    spare = blocks * WIDE

    def scan(home, count):
        def per_column(column, count):
            slot = home * WIDE + column
            dead_ref[count] = slot
            return count + 1 - pattern_ref[home, column]

        return lax.fori_loop(0, WIDE, per_column, count)

    dead = lax.fori_loop(0, blocks, scan, 0)

    def clear(at, carry):
        tiles_ref[dead_ref[at]] = jnp.zeros((BLK, BLK), bf16)
        return carry

    lax.fori_loop(0, dead, clear, 0)
    fill_features(own_ref[:rows, :], left_ref, right_ref)
    count = list_tiles(
        blocks, lambda a: 0, lambda a: blocks, REACH, pattern_ref, list_ref, spare
    )
    make_tiles(count, list_ref, left_ref, right_ref, tiles_ref)


def side_kernel(blocks, before_ref, pattern_ref, other_ref, right_ref, tiles_in, tiles_ref, left_ref, list_ref):
    del tiles_in
    rows = blocks * BLK // PACK
    spare = blocks * WIDE
    before = before_ref[0]
    fill_features(other_ref[:rows, :], left_ref, None)
    count = list_tiles(
        blocks,
        lambda a: a * before,
        lambda a: jnp.where(before == 1, blocks, a + 1),
        jnp.where(before == 1, 0, 2 * REACH),
        pattern_ref,
        list_ref,
        spare,
    )
    make_tiles(count, list_ref, left_ref, right_ref, tiles_ref)


def gather_wide(blocks, width, first, before, own, side_a, side_b, wide_ref):
    at_a = jnp.where(before == 1, 0, 2 * blocks)
    at_b = 2 * blocks - at_a
    size = blocks * width
    wide_ref[blocks : 2 * blocks] = own[first : first + size].reshape(blocks, width, LANES)
    wide_ref[pl.ds(at_a, blocks)] = side_a[first : first + size].reshape(blocks, width, LANES)
    wide_ref[pl.ds(at_b, blocks)] = side_b[first : first + size].reshape(blocks, width, LANES)


def products(home, wide_ref, tiles_ref):
    vec = jnp.concatenate([wide_ref[home + o] for o in range(WIDE)], axis=1)
    tiles = tiles_ref[home * WIDE : (home + 1) * WIDE].reshape(WIDE * BLK, BLK)
    return jnp.dot(vec, tiles, preferred_element_type=f32)


def first_kernel(blocks, before_ref, own_ref, a_ref, b_ref, tiles_ref, noise_ref, vec_ref, image_ref, low_ref, wide_ref):
    width = vec_ref.shape[0]
    first = blocks * BLK // PACK
    gather_wide(blocks, width, first, before_ref[0], own_ref, a_ref, b_ref, wide_ref)
    for home in range(blocks):
        cols = slice(home * BLK, (home + 1) * BLK)
        image = noise_ref[:, cols] * vec_ref[:, cols] + products(home, wide_ref, tiles_ref) * (1.0 / (4 * BLK))
        image_ref[:, cols] = image
        low_ref[home * width : (home + 1) * width, :] = image.astype(bf16)


def second_kernel(
    blocks, before_ref, own_ref, a_ref, b_ref, tiles_ref, noise_ref, vec_ref, image_ref, twice_ref, low_ref, sums_ref, wide_ref
):
    width = vec_ref.shape[0]
    gather_wide(blocks, width, 0, before_ref[0], own_ref, a_ref, b_ref, wide_ref)
    totals = [jnp.zeros((width, BLK), f32) for _ in range(SUMS)]
    for home in range(blocks):
        cols = slice(home * BLK, (home + 1) * BLK)
        r = vec_ref[:, cols]
        w = image_ref[:, cols]
        q = noise_ref[:, cols] * w + products(home, wide_ref, tiles_ref) * (1.0 / (4 * BLK))
        twice_ref[:, cols] = q
        u = r - SHIFT * w
        y = w - SHIFT * q
        low_ref[2 * home * width : (2 * home + 1) * width, :] = y.astype(bf16)
        low_ref[(2 * home + 1) * width : (2 * home + 2) * width, :] = q.astype(bf16)
        terms = (r * r, r * w, u * u, u * w, w * w, y * u, q * u, y * w, q * w)
        totals = [total + term for total, term in zip(totals, terms)]
    lane = lax.broadcasted_iota(jnp.int32, (width, LANES), 1)
    out = jnp.zeros((width, LANES), f32)
    for at, total in enumerate(totals):
        out = jnp.where(lane == at, jnp.sum(total, axis=1, keepdims=True), out)
    sums_ref[...] = out


def third_kernel(blocks, before_ref, own_ref, a_ref, b_ref, tiles_ref, out_ref, wide_ref):
    width = out_ref.shape[0]
    gather_wide(blocks, width, 0, before_ref[0], own_ref, a_ref, b_ref, wide_ref)
    for home in range(blocks):
        out_ref[:, home * BLK : (home + 1) * BLK] = products(home, wide_ref, tiles_ref) * (1.0 / (4 * BLK))


def last_kernel(sums_ref, noise_ref, vec_ref, image_ref, twice_ref, prod_ref, x_ref, r_ref, w_ref):
    width = vec_ref.shape[0]
    rr, rw, uu, uw, ww, yu, qu, yw, qw = [sums_ref[:, at : at + 1] for at in range(SUMS)]
    alpha0 = rr / rw
    delta = alpha0 - SHIFT
    norm = uu - 2.0 * delta * uw + delta * delta * ww
    curv = yu - delta * (qu + yw) + delta * delta * qw
    beta = norm / rr
    alpha1 = norm / (curv - beta * norm / alpha0)
    r0, w0, q0 = vec_ref[...], image_ref[...], twice_ref[...]
    r1 = r0 - alpha0 * w0
    w1 = w0 - alpha0 * q0
    q1 = noise_ref[...] * w1 + (prod_ref[:width, :] - delta * prod_ref[width:, :])
    x_ref[...] = alpha0 * r0 + alpha1 * (r1 + beta * r0)
    r_ref[...] = r1 - alpha1 * (w1 + beta * w0)
    w_ref[...] = w1 - alpha1 * (q1 + beta * q0)


def swap_pairs(count, first):
    pairs = []
    for low in range(first, count - 1, 2):
        pairs += [(low, low + 1), (low + 1, low)]
    return pairs


def both_sides(x):
    count = lax.axis_size("pts")
    return (
        lax.ppermute(x, "pts", swap_pairs(count, 0)),
        lax.ppermute(x, "pts", swap_pairs(count, 1)),
    )


def total_over_points(x):
    count = lax.axis_size("pts")
    if count & (count - 1):
        return lax.psum(x, "pts")
    step = 1
    while step < count:
        x = x + lax.ppermute(x, "pts", [(i, i ^ step) for i in range(count)])
        step *= 2
    return x


def near(x):
    return pltpu.with_memory_space_constraint(x, pltpu.VMEM)


VM = pl.BlockSpec(memory_space=pltpu.VMEM)
SM = pl.BlockSpec(memory_space=pltpu.SMEM)


def cost(flops, moved, special=0):
    return pl.CostEstimate(flops=flops, bytes_accessed=moved, transcendentals=special)


def per_device(points, noise_var, right_side, pattern):
    local_rows = points.shape[0]
    width = right_side.shape[0]
    blocks = local_rows // BLK
    slots = blocks * WIDE + 1
    packed_rows = local_rows // PACK
    list_len = blocks * blocks + UNROLL
    before = (lax.axis_index("pts") % 2).astype(jnp.int32).reshape(1)
    noise = noise_var[None, :]
    params = pltpu.CompilerParams(vmem_limit_bytes=40 * MIB)
    tiles_type = pltpu.VMEM((slots, BLK, BLK), bf16)
    full = (width, local_rows)

    payload = pl.pallas_call(
        prep_kernel,
        out_shape=jax.ShapeDtypeStruct((packed_rows + blocks * width, LANES), bf16),
        in_specs=[VM, VM],
        out_specs=VM,
        name="prep",
    )(points, right_side)
    halo_a, halo_b = both_sides(payload)
    tiles, right = pl.pallas_call(
        functools.partial(local_kernel, blocks),
        out_shape=(tiles_type, pltpu.VMEM((blocks, LANES, BLK), bf16)),
        in_specs=[SM, VM],
        out_specs=(VM, VM),
        scratch_shapes=[
            pltpu.VMEM((blocks, BLK, LANES), bf16),
            pltpu.SMEM((list_len,), jnp.int32),
            pltpu.SMEM((blocks * WIDE + 1,), jnp.int32),
        ],
        compiler_params=params,
        cost_estimate=cost(10**9, 10**7),
        name="local_tiles",
    )(pattern, payload)
    for name, halo in (("tiles_a", halo_a), ("tiles_b", halo_b)):
        tiles = pl.pallas_call(
            functools.partial(side_kernel, blocks),
            out_shape=tiles_type,
            in_specs=[SM, SM, VM, VM, VM],
            out_specs=VM,
            scratch_shapes=[
                pltpu.VMEM((blocks, BLK, LANES), bf16),
                pltpu.SMEM((list_len,), jnp.int32),
            ],
            input_output_aliases={4: 0},
            compiler_params=params,
            cost_estimate=cost(10**9, 10**7),
            name=name,
        )(before if name == "tiles_a" else 1 - before, pattern, halo, near(right), near(tiles))

    def wide(rows):
        return [pltpu.VMEM((3 * blocks, rows, LANES), bf16)]

    image, low = pl.pallas_call(
        functools.partial(first_kernel, blocks),
        out_shape=(jax.ShapeDtypeStruct(full, f32), jax.ShapeDtypeStruct((blocks * width, LANES), bf16)),
        in_specs=[SM] + [VM] * 6,
        out_specs=(VM, VM),
        scratch_shapes=wide(width),
        compiler_params=params,
        name="image",
    )(before, payload, halo_a, halo_b, near(tiles), noise, right_side)
    low_a, low_b = both_sides(low)
    twice, low, sums = pl.pallas_call(
        functools.partial(second_kernel, blocks),
        out_shape=(
            jax.ShapeDtypeStruct(full, f32),
            jax.ShapeDtypeStruct((2 * blocks * width, LANES), bf16),
            jax.ShapeDtypeStruct((width, LANES), f32),
        ),
        in_specs=[SM] + [VM] * 7,
        out_specs=(VM, VM, VM),
        scratch_shapes=wide(width),
        compiler_params=params,
        name="twice",
    )(before, low, low_a, low_b, near(tiles), noise, right_side, image)
    low_a, low_b = both_sides(low)
    sums = total_over_points(sums)
    prods = pl.pallas_call(
        functools.partial(third_kernel, blocks),
        out_shape=jax.ShapeDtypeStruct((2 * width, local_rows), f32),
        in_specs=[SM] + [VM] * 4,
        out_specs=VM,
        scratch_shapes=wide(2 * width),
        compiler_params=params,
        name="products",
    )(before, low, low_a, low_b, near(tiles))
    return pl.pallas_call(
        last_kernel,
        out_shape=tuple(jax.ShapeDtypeStruct(full, f32) for _ in range(3)),
        in_specs=[VM] * 6,
        out_specs=(VM, VM, VM),
        compiler_params=params,
        name="update",
    )(sums, noise, right_side, image, twice, prods)


def solution(mesh):
    placed = (P("pts", None), P("pts"), P("rhs", "pts"), P("pts", None))
    return jax.shard_map(
        per_device,
        mesh=mesh,
        in_specs=placed,
        out_specs=(P("rhs", "pts"), P("rhs", "pts"), P("rhs", "pts")),
        check_vma=False,
    )
```

time: 284 us -> 92.8 us (0.33)
  blocking collectives: 106 us -> 0 us
  waiting for transfers between devices: 61.3 us -> 9.5 us
  Pallas kernels: 0 us -> 50.6 us
  other arithmetic: 32.3 us -> 0.71 us
  matrix products: 20.7 us -> 0 us
  local copies, waits for them, and re-layouts: 26 us -> 6.12 us
  between operations: 14.7 us -> 0.77 us
  starting transfers between devices: 21.4 us -> 25.1 us
    psum x2 -> x0, blocking collectives: 81.7 us -> none  [per_device(): lax.psum((jnp.sum(residual * residual, axis=1), jnp.sum(res_image * resid...]
    reduce_scatter x3 -> x0, waiting for transfers between devices: 51.6 us -> none  [apply_operator(): lax.psum_scatter(summed, 'rhs', scatter_dimension=0, tiled=True)]
    pallas_call x0 -> x8, Pallas kernels: none -> 50.6 us  [the longest x1 21.7 us: per_device(): pl.pallas_call(functools.partial(local_kernel, blocks), out_shape=(tiles_...]
    all_gather x3 -> x0, blocking collectives: 24 us -> none  [apply_operator(): wide_all = lax.all_gather(wide_vec, 'rhs', axis=0, tiled=True)]
    gather x15 -> x0, local copies, waits for them, and re-layouts: 21.5 us -> none  [the longest x3 6.5 us: turn(): point_blocks[home_block + REACH]]
    scatter-add x3 -> x0, other arithmetic: 21.1 us -> none  [turn(): return running.at[:, home_block].add(contribution)]
    dot_general x3 -> x0, matrix products: 20.7 us -> none  [turn(): jnp.einsum('gij,cgj->cgi', weights, vec_blocks[:, other_block], preferred...]
    unnamed x10 -> x23, local copies, waits for them, and re-layouts: 0.04 us -> 6.12 us
  transfers between devices with their start and end apart: 11 -> 9, of which waited for: 7 -> 4; matrix products, arithmetic and copies ran while one was open for 2% -> 1% of each run, Pallas kernels for 0% -> 33%
where the time goes in v1:
time: 92.8 us
  Pallas kernels  50.6 us (55%)
  starting transfers between devices  25.1 us (27%)
  waiting for transfers between devices  9.5 us (10%)
  local copies, waits for them, and re-layouts  6.12 us (7%)
    pallas_call x1, Pallas kernels, per_device(): pl.pallas_call(functools.partial(local_kernel, blocks), out_shape=(tiles_...  21.7 us
    ppermute x3, starting transfers between devices, both_sides(): lax.ppermute(x, 'pts', swap_pairs(count, 0))  16.6 us
    pallas_call x2, Pallas kernels, per_device(): pl.pallas_call(functools.partial(side_kernel, blocks), out_shape=tiles_ty...  12.3 us
    ppermute x3, waiting for transfers between devices, total_over_points(): x = x + lax.ppermute(x, 'pts', [(i, i ^ step) for i in range(count)])  7.04 us
    ppermute x3, starting transfers between devices, total_over_points(): x = x + lax.ppermute(x, 'pts', [(i, i ^ step) for i in range(count)])  6.39 us
    unnamed x23, local copies, waits for them, and re-layouts  6.12 us
    pallas_call x1, Pallas kernels, per_device(): pl.pallas_call(functools.partial(third_kernel, blocks), out_shape=jax.Sha...  4.63 us
    pallas_call x1, Pallas kernels, per_device(): pl.pallas_call(functools.partial(first_kernel, blocks), out_shape=(jax.Sh...  4.46 us
  transfers between devices with their start and end apart: 9, of which 4 were waited for; matrix products, arithmetic and copies ran while one was open for 1% of the time, Pallas kernels for 33%

profile of v1, /device:TPU:0, one launch (start us, length us, event | category | flops | bytes accessed | tf_op | source)
XLA Modules:
  0.0 92.8 jit_solution(10987826740959661442)
XLA Ops:
  0.6 1.9 %copy.9.points_ref = bf16[2048,32]{1,0:T(8,128)(2,1)} copy(bf16[2048,32]{0,1:T(8,128)(2,1)} %param.4) | data formatting | bytes 262144 | tf_op args[0]
  2.6 1.9 %prep.1.own_ref = bf16[768,128]{1,0:T(8,128)(2,1)} custom-call(bf16[2048,32]{1,0:T(8,128)(2,1)} %copy.9.points_ref, f32[16,2048]{1,0:T(8,128)} %vec_ref.7), custom_call_target="tpu_custom_call" | custom-call | tf_op jit(solution)/shard_map/prep/pallas_call | solution.py:310
  4.5 2.9 %collective-permute-start = (bf16[768,128]{1,0:T(8,128)(2,1)}, bf16[768,128]{1,0:T(8,128)(2,1)S(1)}, u32[]{:S(2)}, u32[]{:S(2)}) collective-permute-start(bf16[768,128]{1,0:T(8,128)(2,1)} %prep.1.own_ref), channel_id=1, source_target_pairs={{0,4},{4,0},{8,12},{12,8},{16,20},{20,16},{24,28},{28,24},{1,5},{5... | collective-permute-start | bytes 589832 | tf_op jit(solution)/shard_map/ppermute | solution.py:269
  7.4 0.7 collective-permute-start.1
  8.1 21.7 %local_tiles.1 = (bf16[529,128,128]{2,1,0:T(8,128)(2,1)S(1)}, bf16[16,128,128]{2,1,0:T(8,128)(2,1)S(1)}) custom-call(s32[16,33]{1,0:T(8,128)} %pattern_ref.5, bf16[768,128]{1,0:T(8,128)(2,1)} %prep.1.own_ref), custom_call_target="tpu_custom_call" | custom-call | flops 1000000000 | bytes 10000000 | tf_op jit(solution)/shard_map/local_tiles/pallas_call | solution.py:318
  29.7 0.0 collective-permute-done.other_ref.a_ref
  29.8 0.0 copy-start.5
  29.8 0.7 copy-done.5
  30.4 9.4 %tiles_a.1.tiles_in = bf16[529,128,128]{2,1,0:T(8,128)(2,1)S(1)} custom-call(s32[1]{0:T(128)} %bitcast.before_ref, s32[16,33]{1,0:T(8,128)} %pattern_ref.5, bf16[768,128]{1,0:T(8,128)(2,1)} %copy-done.5, bf16[16,128,128]{2,1,0:T(8,128)(2,1)S(1)} %get-tuple-element.10.right_ref, ...), custom_call_target="tpu_custom_call", output_to_operand_aliasing={{}: (4, {})} | custom-call | flops 1000000000 | bytes 10000000 | tf_op jit(solution)/shard_map/tiles_a/pallas_call | solution.py:333
  39.8 0.0 collective-permute-done.1.other_ref.b_ref
  39.9 0.0 copy-start.6
  39.9 0.7 copy-done.6
  40.5 2.9 %tiles_b.1.tiles_ref = bf16[529,128,128]{2,1,0:T(8,128)(2,1)S(1)} custom-call(s32[1]{0:T(128)S(6)} %sub.3.before_ref, s32[16,33]{1,0:T(8,128)} %pattern_ref.5, bf16[768,128]{1,0:T(8,128)(2,1)} %copy-done.6, bf16[16,128,128]{2,1,0:T(8,128)(2,1)S(1)} %get-tuple-element.10.right_ref, ...), custom_call_target="tpu_custom_call", output_to_operand_aliasing={{}: (4, {})} | custom-call | flops 1000000000 | bytes 10000000 | tf_op jit(solution)/shard_map/tiles_b/pallas_call | solution.py:333
  43.5 4.5 %image.1 = (f32[16,2048]{1,0:T(8,128)}, bf16[256,128]{1,0:T(8,128)(2,1)}) custom-call(s32[1]{0:T(128)} %bitcast.before_ref, bf16[768,128]{1,0:T(8,128)(2,1)} %prep.1.own_ref, bf16[768,128]{1,0:T(8,128)(2,1)} %copy-done.5, bf16[768,128]{1,0:T(8,128)(2,1)} %copy-done.6, bf16[529,128,128]{2,1,0:T(8,128)(2,1)S(1)} %tiles_b.1.tiles_ref, f32[1,2048]{1,0:T(1,128)} %bitcast.2, ...), custom_call_target="tpu_custom_call" | custom-call | tf_op jit(solution)/shard_map/image/pallas_call | solution.py:351
  47.9 0.7 collective-permute-start.3
  48.6 7.7 %collective-permute-start.2 = (bf16[256,128]{1,0:T(8,128)(2,1)}, bf16[256,128]{1,0:T(8,128)(2,1)S(1)}, u32[]{:S(2)}, u32[]{:S(2)}) collective-permute-start(bf16[256,128]{1,0:T(8,128)(2,1)} %get-tuple-element.12.own_ref), channel_id=1, source_target_pairs={{0,4},{4,0},{8,12},{12,8},{16,20},{20,16},{24,28},{28,24},{1,5},{5... | collective-permute-start | bytes 196616 | tf_op jit(solution)/shard_map/ppermute | solution.py:269
  56.3 0.0 collective-permute-done.3.b_ref
  56.3 0.0 copy-start.9
  56.3 2.5 %collective-permute-done.2.a_ref = bf16[256,128]{1,0:T(8,128)(2,1)S(1)} collective-permute-done((bf16[256,128]{1,0:T(8,128)(2,1)}, bf16[256,128]{1,0:T(8,128)(2,1)S(1)}, u32[]{:S(2)}, u32[]{:S(2)}) %collective-permute-start.2) | collective-permute-done | bytes 65568 | tf_op jit(solution)/shard_map/ppermute | solution.py:269
  58.7 0.0 copy-start.10
  58.7 0.0 copy-done.9
  58.7 0.6 copy-done.10
  59.3 0.0 copy-start
  59.3 0.0 copy-start.2
  59.4 0.0 copy-start.4
  59.4 4.5 %twice.1 = (f32[16,2048]{1,0:T(8,128)}, bf16[512,128]{1,0:T(8,128)(2,1)}, f32[16,128]{1,0:T(8,128)}) custom-call(s32[1]{0:T(128)} %bitcast.before_ref, bf16[256,128]{1,0:T(8,128)(2,1)} %get-tuple-element.12.own_ref, bf16[256,128]{1,0:T(8,128)(2,1)} %copy-done.10, bf16[256,128]{1,0:T(8,128)(2,1)} %copy-done.9, bf16[529,128,128]{2,1,0:T(8,128)(2,1)S(1)} %tiles_b.1.tiles_ref, ...), custom_call_target="tpu_custom_call" | custom-call | tf_op jit(solution)/shard_map/twice/pallas_call | solution.py:361
  63.8 0.0 copy-start.3
  63.8 0.8 collective-permute-start.8
  64.6 6.0 %collective-permute-start.7 = (bf16[512,128]{1,0:T(8,128)(2,1)}, bf16[512,128]{1,0:T(8,128)(2,1)S(1)}, u32[]{:S(2)}, u32[]{:S(2)}) collective-permute-start(bf16[512,128]{1,0:T(8,128)(2,1)} %get-tuple-element.16.own_ref), channel_id=1, source_target_pairs={{0,4},{4,0},{8,12},{12,8},{16,20},{20,16},{24,28},{28,24},{1,5},{5... | collective-permute-start | bytes 393224 | tf_op jit(solution)/shard_map/ppermute | solution.py:269
  70.6 0.1 collective-permute-start.4
  70.7 3.8 %collective-permute-done.4 = f32[16,128]{1,0:T(8,128)S(1)} collective-permute-done((f32[16,128]{1,0:T(8,128)}, f32[16,128]{1,0:T(8,128)S(1)}, u32[]{:S(2)}, u32[]{:S(2)}) %collective-permute-start.4) | collective-permute-done | bytes 8224 | tf_op jit(solution)/shard_map/ppermute | solution.py:280
  74.5 0.7 add.14
  75.2 2.4 %collective-permute-start.5 = (f32[16,128]{1,0:T(8,128)S(1)}, f32[16,128]{1,0:T(8,128)S(1)}, u32[]{:S(2)}, u32[]{:S(2)}) collective-permute-start(f32[16,128]{1,0:T(8,128)S(1)} %add.14), channel_id=1, source_target_pairs={{0,8},{4,12},{8,0},{12,4},{16,24},{20,28},{24,16},{28,20},{1,9},{5... | collective-permute-start | bytes 24584 | tf_op jit(solution)/shard_map/ppermute | solution.py:280
  77.5 1.6 %collective-permute-done.5 = f32[16,128]{1,0:T(8,128)S(1)} collective-permute-done((f32[16,128]{1,0:T(8,128)S(1)}, f32[16,128]{1,0:T(8,128)S(1)}, u32[]{:S(2)}, u32[]{:S(2)}) %collective-permute-start.5) | collective-permute-done | bytes 8224 | tf_op jit(solution)/shard_map/ppermute | solution.py:280
  79.2 3.9 %collective-permute-start.6 = (f32[16,128]{1,0:T(8,128)S(1)}, f32[16,128]{1,0:T(8,128)S(1)}, u32[]{:S(2)}, u32[]{:S(2)}) collective-permute-start(f32[16,128]{1,0:T(8,128)S(1)} %add.15), channel_id=1, source_target_pairs={{0,16},{4,20},{8,24},{12,28},{16,0},{20,4},{24,8},{28,12},{1,17},{... | collective-permute-start | bytes 24584 | tf_op jit(solution)/shard_map/ppermute | solution.py:280
  83.1 1.6 %collective-permute-done.6 = f32[16,128]{1,0:T(8,128)S(1)} collective-permute-done((f32[16,128]{1,0:T(8,128)S(1)}, f32[16,128]{1,0:T(8,128)S(1)}, u32[]{:S(2)}, u32[]{:S(2)}) %collective-permute-start.6) | collective-permute-done | bytes 8224 | tf_op jit(solution)/shard_map/ppermute | solution.py:280
  84.8 0.0 collective-permute-done.8.b_ref
  84.8 0.0 copy-start.7
  84.8 0.0 collective-permute-done.7.a_ref
  84.8 0.6 copy-done.7
  85.4 0.0 copy-start.8
  85.4 0.6 copy-done.8
  86.0 4.6 %products.1.prod_ref = f32[32,2048]{1,0:T(8,128)} custom-call(s32[1]{0:T(128)} %bitcast.before_ref, bf16[512,128]{1,0:T(8,128)(2,1)} %get-tuple-element.16.own_ref, bf16[512,128]{1,0:T(8,128)(2,1)} %copy-done.8, bf16[512,128]{1,0:T(8,128)(2,1)} %copy-done.7, bf16[529,128,128]{2,1,0:T(8,128)(2,1)S(1)} %tiles_b.1.tiles_ref), custom_call_target="tpu_custom_call" | custom-call | tf_op jit(solution)/shard_map/products/pallas_call | solution.py:376
  90.7 0.0 copy-done
  90.7 0.0 copy-done.2
  90.7 0.0 copy-done.4
  90.7 0.0 copy-done.3
  90.7 0.0 copy-start.1
  90.7 0.9 %copy-done.1 = f32[32,2048]{1,0:T(8,128)S(1)} copy-done((f32[32,2048]{1,0:T(8,128)S(1)}, f32[32,2048]{1,0:T(8,128)}, u32[]{:S(2)}) %copy-start.1) | copy-done | bytes 262168
  91.6 1.1 %update.1 = (f32[16,2048]{1,0:T(8,128)}, f32[16,2048]{1,0:T(8,128)}, f32[16,2048]{1,0:T(8,128)}) custom-call(f32[16,128]{1,0:T(8,128)S(1)} %add.16.sums_ref, f32[1,2048]{1,0:T(1,128)S(1)} %bitcast.4, f32[16,2048]{1,0:T(8,128)S(1)} %copy-done, f32[16,2048]{1,0:T(8,128)S(1)} %copy-done.2, f32[16,2048]{1,0:T(8,128)S(1)} %copy-done.3, f32[32,2048]{1,0:T(8,128)S(1)} %copy-done.1), custom_call_target="tpu_custom_call" | custom-call | tf_op jit(solution)/shard_map/update/pallas_call | solution.py:385
  (2 shorter events, 0.0 us)
Async XLA Ops:
  4.5 25.3 %collective-permute-start = (bf16[768,128]{1,0:T(8,128)(2,1)}, bf16[768,128]{1,0:T(8,128)(2,1)S(1)}, u32[]{:S(2)}, u32[]{:S(2)}) collective-permute-start(bf16[768,128]{1,0:T(8,128)(2,1)} %prep.1.own_ref), channel_id=1, source_target_pairs={{0,4},{4,0},{8,12},{12,8},{16,20},{20,16},{24,28},{28,24},{1,5},{5... | collective-permute-start | bytes 589832 | tf_op jit(solution)/shard_map/ppermute | solution.py:269
  7.4 32.4 %collective-permute-start.1 = (bf16[768,128]{1,0:T(8,128)(2,1)}, bf16[768,128]{1,0:T(8,128)(2,1)S(1)}, u32[]{:S(2)}, u32[]{:S(2)}) collective-permute-start(bf16[768,128]{1,0:T(8,128)(2,1)} %prep.1.own_ref), channel_id=1, source_target_pairs={{4,8},{8,4},{12,16},{16,12},{20,24},{24,20},{5,9},{9,5},{13,17},{1... | collective-permute-start | bytes 589832 | tf_op jit(solution)/shard_map/ppermute | solution.py:270
  29.8 0.7 copy-start.5
  39.9 0.7 copy-start.6
  47.9 8.4 %collective-permute-start.3 = (bf16[256,128]{1,0:T(8,128)(2,1)}, bf16[256,128]{1,0:T(8,128)(2,1)S(1)}, u32[]{:S(2)}, u32[]{:S(2)}) collective-permute-start(bf16[256,128]{1,0:T(8,128)(2,1)} %get-tuple-element.12.own_ref), channel_id=1, source_target_pairs={{4,8},{8,4},{12,16},{16,12},{20,24},{24,20},{5,9},{9,5},{13,17},{1... | collective-permute-start | bytes 196616 | tf_op jit(solution)/shard_map/ppermute | solution.py:270
  48.6 10.2 %collective-permute-start.2 = (bf16[256,128]{1,0:T(8,128)(2,1)}, bf16[256,128]{1,0:T(8,128)(2,1)S(1)}, u32[]{:S(2)}, u32[]{:S(2)}) collective-permute-start(bf16[256,128]{1,0:T(8,128)(2,1)} %get-tuple-element.12.own_ref), channel_id=1, source_target_pairs={{0,4},{4,0},{8,12},{12,8},{16,20},{20,16},{24,28},{28,24},{1,5},{5... | collective-permute-start | bytes 196616 | tf_op jit(solution)/shard_map/ppermute | solution.py:269
  56.3 2.5 %copy-start.9 = (bf16[256,128]{1,0:T(8,128)(2,1)}, bf16[256,128]{1,0:T(8,128)(2,1)S(1)}, u32[]{:S(2)}) copy-start(bf16[256,128]{1,0:T(8,128)(2,1)S(1)} %collective-permute-done.3.b_ref) | copy-start | bytes 196612
  58.7 0.6 copy-start.10
  59.3 31.3 %copy-start = (f32[16,2048]{1,0:T(8,128)S(1)}, f32[16,2048]{1,0:T(8,128)}, u32[]{:S(2)}) copy-start(f32[16,2048]{1,0:T(8,128)} %vec_ref.7) | copy-start | bytes 393220
  59.3 31.3 %copy-start.2 = (f32[16,2048]{1,0:T(8,128)S(1)}, f32[16,2048]{1,0:T(8,128)}, u32[]{:S(2)}) copy-start(f32[16,2048]{1,0:T(8,128)} %get-tuple-element.13.image_ref) | copy-start | bytes 393220
  59.4 31.3 %copy-start.4 = (f32[2048]{0:T(1024)S(1)}, f32[2048]{0:T(1024)}, u32[]{:S(2)}) copy-start(f32[2048]{0:T(1024)} %param.5) | copy-start | bytes 24580
  63.8 26.9 %copy-start.3 = (f32[16,2048]{1,0:T(8,128)S(1)}, f32[16,2048]{1,0:T(8,128)}, u32[]{:S(2)}) copy-start(f32[16,2048]{1,0:T(8,128)} %get-tuple-element.15.twice_ref) | copy-start | bytes 393220
  63.8 20.9 %collective-permute-start.8 = (bf16[512,128]{1,0:T(8,128)(2,1)}, bf16[512,128]{1,0:T(8,128)(2,1)S(1)}, u32[]{:S(2)}, u32[]{:S(2)}) collective-permute-start(bf16[512,128]{1,0:T(8,128)(2,1)} %get-tuple-element.16.own_ref), channel_id=1, source_target_pairs={{4,8},{8,4},{12,16},{16,12},{20,24},{24,20},{5,9},{9,5},{13,17},{1... | collective-permute-start | bytes 393224 | tf_op jit(solution)/shard_map/ppermute | solution.py:270
  64.6 20.2 %collective-permute-start.7 = (bf16[512,128]{1,0:T(8,128)(2,1)}, bf16[512,128]{1,0:T(8,128)(2,1)S(1)}, u32[]{:S(2)}, u32[]{:S(2)}) collective-permute-start(bf16[512,128]{1,0:T(8,128)(2,1)} %get-tuple-element.16.own_ref), channel_id=1, source_target_pairs={{0,4},{4,0},{8,12},{12,8},{16,20},{20,16},{24,28},{28,24},{1,5},{5... | collective-permute-start | bytes 393224 | tf_op jit(solution)/shard_map/ppermute | solution.py:269
  70.6 3.9 %collective-permute-start.4 = (f32[16,128]{1,0:T(8,128)}, f32[16,128]{1,0:T(8,128)S(1)}, u32[]{:S(2)}, u32[]{:S(2)}) collective-permute-start(f32[16,128]{1,0:T(8,128)} %get-tuple-element.14), channel_id=1, source_target_pairs={{0,4},{4,0},{8,12},{12,8},{16,20},{20,16},{24,28},{28,24},{1,5},{5... | collective-permute-start | bytes 24584 | tf_op jit(solution)/shard_map/ppermute | solution.py:280
  75.2 4.0 %collective-permute-start.5 = (f32[16,128]{1,0:T(8,128)S(1)}, f32[16,128]{1,0:T(8,128)S(1)}, u32[]{:S(2)}, u32[]{:S(2)}) collective-permute-start(f32[16,128]{1,0:T(8,128)S(1)} %add.14), channel_id=1, source_target_pairs={{0,8},{4,12},{8,0},{12,4},{16,24},{20,28},{24,16},{28,20},{1,9},{5... | collective-permute-start | bytes 24584 | tf_op jit(solution)/shard_map/ppermute | solution.py:280
  79.2 5.6 %collective-permute-start.6 = (f32[16,128]{1,0:T(8,128)S(1)}, f32[16,128]{1,0:T(8,128)S(1)}, u32[]{:S(2)}, u32[]{:S(2)}) collective-permute-start(f32[16,128]{1,0:T(8,128)S(1)} %add.15), channel_id=1, source_target_pairs={{0,16},{4,20},{8,24},{12,28},{16,0},{20,4},{24,8},{28,12},{1,17},{... | collective-permute-start | bytes 24584 | tf_op jit(solution)/shard_map/ppermute | solution.py:280
  84.8 0.7 copy-start.7
  85.4 0.6 copy-start.8
  90.7 1.0 %copy-start.1 = (f32[32,2048]{1,0:T(8,128)S(1)}, f32[32,2048]{1,0:T(8,128)}, u32[]{:S(2)}) copy-start(f32[32,2048]{1,0:T(8,128)} %products.1.prod_ref) | copy-start | bytes 786436

commit v2 on v0

v2 whole, which is shorter than its diff:
```python
import functools

import jax
import jax.numpy as jnp
from jax import lax
from jax.experimental import pallas as pl
from jax.experimental.pallas import tpu as pltpu
from jax.sharding import PartitionSpec as P

F = 32
BLK = 128
REACH = 16
WEXP = 18
LANES = 128
GAMMA = float(WEXP) ** (1.0 / (WEXP + 1))
GAMMA_SQ = GAMMA * GAMMA
OFFSET = GAMMA * (WEXP + 1) / WEXP
TINY = 1e-30
SCALE = 1.0 / (4 * BLK)
SHIFT = 2.0 / (0.5 + 0.6)
SUMS = 9
UNROLL = 16
TAIL = 4
FIELD = 9
MIB = 1 << 20

f32 = jnp.float32
bf16 = jnp.bfloat16


def rounded(x):
    return x.astype(bf16).astype(f32)


def three_parts(x):
    high = rounded(x)
    rest = x - high
    middle = rounded(rest)
    return high, middle, rounded(rest - middle)


def eight_rows(rows):
    row = lax.broadcasted_iota(jnp.int32, (8, rows[0].shape[1]), 0)
    out = jnp.zeros((8, rows[0].shape[1]), f32)
    for at, value in enumerate(rows):
        out = jnp.where(row == at, value, out)
    return out


def fill_features(points, left_ref, right_ref):
    x = points.astype(f32)
    count = x.shape[1]
    squares = three_parts(GAMMA_SQ * jnp.sum(x * x, axis=0, keepdims=True))
    ones = [jnp.ones((1, count), f32)] * 3
    blank = jnp.zeros((LANES - 3 * F - 8, count), f32)
    left = jnp.concatenate([x, x, x, eight_rows(list(squares) + ones), blank], axis=0).astype(bf16)
    for b in range(count // BLK):
        left_ref[b] = left[:, b * BLK : (b + 1) * BLK].T
    if right_ref is not None:
        cross = three_parts((-2.0 * GAMMA_SQ) * x)
        right = jnp.concatenate(list(cross) + [eight_rows(ones + list(squares)), blank], axis=0).astype(bf16)
        for b in range(count // BLK):
            right_ref[b] = right[:, b * BLK : (b + 1) * BLK]


def tile_values(left, right):
    scaled = jnp.dot(left, right, preferred_element_type=f32)
    scaled = jnp.maximum(scaled, TINY)
    s = jnp.maximum(GAMMA - scaled * lax.rsqrt(scaled), 0.0)
    s2 = s * s
    s4 = s2 * s2
    s8 = s4 * s4
    s16 = s8 * s8
    return ((s16 * s2) * (OFFSET - s)).astype(bf16)


def entry(slot, mirror, other, home):
    return (((((home << 4) + other) << FIELD) + mirror) << FIELD) + slot


def make_tiles(count, list_ref, left_ref, right_ref, tiles_ref, mirrored):
    mask = (1 << FIELD) - 1

    def one(at):
        code = list_ref[at]
        home = code >> (2 * FIELD + 4)
        other = (code >> (2 * FIELD)) & 15
        tile = tile_values(left_ref[other], right_ref[home])
        if mirrored:
            tiles_ref[(code >> FIELD) & mask] = tile.T
        tiles_ref[code & mask] = tile

    def step(at, carry):
        for k in range(UNROLL):
            one(at * UNROLL + k)
        return carry

    def tail(at, carry):
        for k in range(TAIL):
            one(at * TAIL + k)
        return carry

    whole = count // UNROLL
    lax.fori_loop(0, whole, step, 0)
    lax.fori_loop(whole * (UNROLL // TAIL), (count + TAIL - 1) // TAIL, tail, 0)


def local_slot(blocks, home, other):
    return ((home // 2) * blocks + other) * 2 + home % 2


def side_slot(blocks, home, other, after):
    wide = other - 2 * (home // 2) + (blocks if after else 0)
    return ((home // 2) * (blocks + 2) + wide) * 2 + home % 2


def local_entries(blocks):
    return [(a, b, REACH + b - a) for a in range(blocks) for b in range(a, blocks)]


def side_entries(blocks, after):
    if after:
        return [(a, b, 2 * REACH + b - a) for a in range(blocks) for b in range(a + 1)]
    return [(a, b, b - a) for a in range(blocks) for b in range(a, blocks)]


def list_side(blocks, after, pattern_ref, list_ref):
    count = jnp.int32(0)
    for home, other, column in side_entries(blocks, after):
        list_ref[count] = jnp.int32(entry(side_slot(blocks, home, other, after), 0, other, home))
        count = count + pattern_ref[home, column]
    return count


def pad_list(count, list_ref, spare):
    for k in range(TAIL - 1):
        list_ref[count + k] = jnp.int32(entry(spare, spare, 0, 0))


def clear_tiles(count, list_ref, tiles_ref):
    mask = (1 << FIELD) - 1

    def step(at, carry):
        code = list_ref[at]
        tiles_ref[code & mask] = jnp.zeros((BLK, BLK), bf16)
        tiles_ref[(code >> FIELD) & mask] = jnp.zeros((BLK, BLK), bf16)
        return carry

    lax.fori_loop(0, count, step, 0)


def products(vec, tiles_ref, pair, wide):
    tiles = tiles_ref[pair * 2 * wide : (pair + 1) * 2 * wide].reshape(wide, 2, BLK, BLK)
    tiles = jnp.concatenate([tiles[:, 0].reshape(wide * BLK, BLK), tiles[:, 1].reshape(wide * BLK, BLK)], axis=1)
    return jnp.dot(vec, tiles, preferred_element_type=f32)


def pair_cols(pair):
    return slice(pair * 2 * BLK, (pair + 1) * 2 * BLK)


def local_products(blocks, vec, tiles_ref, out_ref):
    for pair in range(blocks // 2):
        out_ref[:, pair_cols(pair)] = products(vec, tiles_ref, pair, blocks)


def gather_sides(blocks, before, side_a, side_b, wide_ref):
    size = blocks * BLK
    at_a = pl.multiple_of(jnp.where(before == 1, 0, size), size)
    at_b = pl.multiple_of(size - at_a, size)
    wide_ref[:, pl.ds(at_a, size)] = side_a
    wide_ref[:, pl.ds(at_b, size)] = side_b


def side_products(blocks, pair, wide_ref, tiles_ref):
    vec = wide_ref[:, pair * 2 * BLK : (pair * 2 + blocks + 2) * BLK]
    return products(vec, tiles_ref, pair, blocks + 2)


def prep_kernel(points_ref, vec_ref, out_ref):
    out_ref[:F, :] = points_ref[...]
    out_ref[F:, :] = vec_ref[...].astype(bf16)


def local_kernel(
    blocks, pattern_ref, own_ref, local_ref, side_ref, right_ref, part_ref, left_ref, list_ref, dead_ref
):
    spare = blocks * blocks
    fill_features(own_ref[:F, :], left_ref, right_ref)
    dead = jnp.int32(0)
    for after in (False, True):
        for home, other, column in side_entries(blocks, after):
            slot = side_slot(blocks, home, other, after)
            dead_ref[dead] = jnp.int32(entry(slot, slot, 0, 0))
            dead = dead + (1 - pattern_ref[home, column])
    clear_tiles(dead, dead_ref, side_ref)
    for pair in range(blocks // 2):
        first = pair * 2 * (blocks + 2)
        side_ref[first + 1] = jnp.zeros((BLK, BLK), bf16)
        side_ref[first + 2 * (blocks + 1)] = jnp.zeros((BLK, BLK), bf16)
    dead = jnp.int32(0)
    count = jnp.int32(0)
    for home, other, column in local_entries(blocks):
        code = jnp.int32(entry(local_slot(blocks, home, other), local_slot(blocks, other, home), other, home))
        live = pattern_ref[home, column]
        dead_ref[dead] = code
        list_ref[count] = code
        dead = dead + (1 - live)
        count = count + live
    pad_list(count, list_ref, spare)
    clear_tiles(dead, dead_ref, local_ref)
    make_tiles(count, list_ref, left_ref, right_ref, local_ref, True)
    local_products(blocks, own_ref[F:, :], local_ref, part_ref)


def make_side(blocks, before, pattern_ref, other_ref, right_ref, tiles_ref, left_ref, list_ref, count_ref):
    fill_features(other_ref[:F, :], left_ref, None)

    @pl.when(before == 1)
    def _():
        count_ref[0] = list_side(blocks, False, pattern_ref, list_ref)

    @pl.when(before == 0)
    def _():
        count_ref[0] = list_side(blocks, True, pattern_ref, list_ref)

    count = count_ref[0]
    pad_list(count, list_ref, blocks * (blocks + 2))
    make_tiles(count, list_ref, left_ref, right_ref, tiles_ref, False)


def side_kernel(blocks, before_ref, pattern_ref, other_ref, right_ref, tiles_in, tiles_ref, left_ref, list_ref, count_ref):
    del tiles_in
    make_side(blocks, before_ref[0], pattern_ref, other_ref, right_ref, tiles_ref, left_ref, list_ref, count_ref)


def first_kernel(
    blocks, before_ref, pattern_ref, a_ref, b_ref, right_ref, tiles_in, part_ref, noise_ref, vec_ref,
    tiles_ref, image_ref, low_ref, left_ref, wide_ref, list_ref, count_ref,
):
    del tiles_in
    before = before_ref[0]
    make_side(blocks, 1 - before, pattern_ref, b_ref, right_ref, tiles_ref, left_ref, list_ref, count_ref)
    gather_sides(blocks, before, a_ref[F:, :], b_ref[F:, :], wide_ref)
    for pair in range(blocks // 2):
        cols = pair_cols(pair)
        total = part_ref[:, cols] + side_products(blocks, pair, wide_ref, tiles_ref)
        image = noise_ref[:, cols] * vec_ref[:, cols] + total * SCALE
        image_ref[:, cols] = image
        low_ref[:, cols] = image.astype(bf16)


def own_kernel(blocks, own_ref, tiles_ref, part_ref):
    local_products(blocks, own_ref[:, : blocks * BLK], tiles_ref, part_ref)


def second_kernel(
    blocks, before_ref, a_ref, b_ref, tiles_ref, part_ref, noise_ref, vec_ref, image_ref,
    twice_ref, low_ref, sums_ref, wide_ref,
):
    width, points = vec_ref.shape
    gather_sides(blocks, before_ref[0], a_ref[...], b_ref[...], wide_ref)
    totals = [jnp.zeros((width, LANES), f32) for _ in range(SUMS)]
    for pair in range(blocks // 2):
        cols = pair_cols(pair)
        r = vec_ref[:, cols]
        w = image_ref[:, cols]
        q = noise_ref[:, cols] * w + (part_ref[:, cols] + side_products(blocks, pair, wide_ref, tiles_ref)) * SCALE
        twice_ref[:, cols] = q
        u = r - SHIFT * w
        y = w - SHIFT * q
        low_ref[:width, cols] = y.astype(bf16)
        low_ref[width:, cols] = q.astype(bf16)
        terms = (r * r, r * w, u * u, u * w, w * w, y * u, q * u, y * w, q * w)
        totals = [total + (term[:, :LANES] + term[:, LANES:]) for total, term in zip(totals, terms)]
    lane = lax.broadcasted_iota(jnp.int32, (width, LANES), 1)
    out = jnp.zeros((width, LANES), f32)
    for at, total in enumerate(totals):
        out = jnp.where(lane == at, jnp.sum(total, axis=1, keepdims=True), out)
    sums_ref[...] = out
    high, middle, low = three_parts(out)
    low_ref[:width, points : points + LANES] = high.astype(bf16)
    low_ref[:width, points + LANES :] = middle.astype(bf16)
    low_ref[width:, points : points + LANES] = low.astype(bf16)
    low_ref[width:, points + LANES :] = jnp.zeros((width, LANES), bf16)


def third_kernel(blocks, before_ref, a_ref, b_ref, tiles_ref, part_ref, out_ref, wide_ref):
    points = blocks * BLK
    gather_sides(blocks, before_ref[0], a_ref[:, :points], b_ref[:, :points], wide_ref)
    for pair in range(blocks // 2):
        cols = pair_cols(pair)
        out_ref[:, cols] = (part_ref[:, cols] + side_products(blocks, pair, wide_ref, tiles_ref)) * SCALE


def last_kernel(sums_ref, noise_ref, vec_ref, image_ref, twice_ref, prod_ref, x_ref, r_ref, w_ref):
    width = vec_ref.shape[0]
    rr, rw, uu, uw, ww, yu, qu, yw, qw = [sums_ref[:, at : at + 1] for at in range(SUMS)]
    alpha0 = rr / rw
    delta = alpha0 - SHIFT
    norm = uu - 2.0 * delta * uw + delta * delta * ww
    curv = yu - delta * (qu + yw) + delta * delta * qw
    beta = norm / rr
    alpha1 = norm / (curv - beta * norm / alpha0)
    r0, w0, q0 = vec_ref[...], image_ref[...], twice_ref[...]
    r1 = r0 - alpha0 * w0
    w1 = w0 - alpha0 * q0
    q1 = noise_ref[...] * w1 + (prod_ref[:width, :] - delta * prod_ref[width:, :])
    x_ref[...] = alpha0 * r0 + alpha1 * (r1 + beta * r0)
    r_ref[...] = r1 - alpha1 * (w1 + beta * w0)
    w_ref[...] = w1 - alpha1 * (q1 + beta * q0)


def swap_pairs(count, first):
    pairs = []
    for low in range(first, count - 1, 2):
        pairs += [(low, low + 1), (low + 1, low)]
    return pairs


def both_sides(x):
    count = lax.axis_size("pts")
    return (
        lax.ppermute(x, "pts", swap_pairs(count, 0)),
        lax.ppermute(x, "pts", swap_pairs(count, 1)),
    )


def total_over_points(own, neighbour, width):
    count = lax.axis_size("pts")
    if count & (count - 1):
        return lax.psum(own, "pts")
    if count == 1:
        return own
    parts = neighbour[:, -2 * LANES :].astype(f32)
    x = own + ((parts[:width, :LANES] + parts[:width, LANES:]) + parts[width:, :LANES])
    step = 2
    while step < count:
        reach = 4 if step * 2 < count else 2
        x = x + sum(
            lax.ppermute(x, "pts", [(i, i ^ (k * step)) for i in range(count)]) for k in range(1, reach)
        )
        step *= reach
    return x


def near(x):
    return pltpu.with_memory_space_constraint(x, pltpu.VMEM)


VM = pl.BlockSpec(memory_space=pltpu.VMEM)
SM = pl.BlockSpec(memory_space=pltpu.SMEM)


def per_device(points, noise_var, right_side, pattern):
    local_rows = points.shape[0]
    width = right_side.shape[0]
    blocks = local_rows // BLK
    assert blocks == REACH
    before = (lax.axis_index("pts") % 2).astype(jnp.int32).reshape(1)
    params = pltpu.CompilerParams(vmem_limit_bytes=20 * MIB)
    full = (width, local_rows)
    local_type = pltpu.VMEM((blocks * blocks + 1, BLK, BLK), bf16)
    side_type = pltpu.VMEM((blocks * (blocks + 2) + 1, BLK, BLK), bf16)
    left_scratch = pltpu.VMEM((blocks, BLK, LANES), bf16)
    list_scratch = pltpu.SMEM((blocks * (blocks + 1) // 2 + TAIL,), jnp.int32)
    count_scratch = pltpu.SMEM((1,), jnp.int32)
    dead_scratch = pltpu.SMEM((blocks * (blocks + 1) + 1,), jnp.int32)

    def wide(rows):
        return pltpu.VMEM((rows, 2 * local_rows), bf16)

    def call(kernel, name, ins, outs, scratch=(), aliases=None, scalars=0, us=2):
        return pl.pallas_call(
            kernel,
            out_shape=outs,
            in_specs=[SM] * scalars + [VM] * (len(ins) - scalars),
            out_specs=jax.tree.map(lambda _: VM, outs, is_leaf=lambda x: hasattr(x, "dtype")),
            scratch_shapes=list(scratch),
            input_output_aliases=aliases or {},
            compiler_params=params,
            cost_estimate=pl.CostEstimate(flops=us * 10**9, bytes_accessed=us * 3 * 10**6, transcendentals=0),
            name=name,
        )(*ins[:scalars], *[near(x) for x in ins[scalars:]])

    noise = noise_var[None, :]
    payload = call(
        prep_kernel, "prep", (points.T, right_side), pltpu.VMEM((F + width, local_rows), bf16)
    )
    halo_a, halo_b = both_sides(payload)
    local_tiles, side_tiles, right, part = call(
        functools.partial(local_kernel, blocks),
        "local_tiles",
        (pattern, payload),
        (local_type, side_type, pltpu.VMEM((blocks, LANES, BLK), bf16), pltpu.VMEM(full, f32)),
        (left_scratch, list_scratch, dead_scratch),
        scalars=1,
        us=8,
    )
    side_tiles = call(
        functools.partial(side_kernel, blocks),
        "side_tiles",
        (before, pattern, halo_a, right, side_tiles),
        side_type,
        (left_scratch, list_scratch, count_scratch),
        {4: 0},
        scalars=2,
        us=5,
    )
    side_tiles, image, low = call(
        functools.partial(first_kernel, blocks),
        "image",
        (before, pattern, halo_a, halo_b, right, side_tiles, part, noise, right_side),
        (side_type, pltpu.VMEM(full, f32), pltpu.VMEM(full, bf16)),
        (left_scratch, wide(width), list_scratch, count_scratch),
        {5: 0},
        scalars=2,
        us=7,
    )
    low_a, low_b = both_sides(low)
    part = call(
        functools.partial(own_kernel, blocks), "own_products", (low, local_tiles), pltpu.VMEM(full, f32)
    )
    low_type = pltpu.VMEM((2 * width, local_rows + 2 * LANES), bf16)
    twice, low, sums = call(
        functools.partial(second_kernel, blocks),
        "twice",
        (before, low_a, low_b, side_tiles, part, noise, right_side, image),
        (pltpu.VMEM(full, f32), low_type, pltpu.VMEM((width, LANES), f32)),
        (wide(width),),
        scalars=1,
    )
    low_a, low_b = both_sides(low)
    sums = total_over_points(sums, low_a, width)
    both = pltpu.VMEM((2 * width, local_rows), f32)
    part = call(functools.partial(own_kernel, blocks), "own_products_both", (low, local_tiles), both)
    prods = call(
        functools.partial(third_kernel, blocks),
        "products",
        (before, low_a, low_b, side_tiles, part),
        both,
        (wide(2 * width),),
        scalars=1,
    )
    out = jax.ShapeDtypeStruct(full, f32)
    return call(last_kernel, "update", (sums, noise, right_side, image, twice, prods), (out, out, out))


def solution(mesh):
    placed = (P("pts", None), P("pts"), P("rhs", "pts"), P("pts", None))
    return jax.shard_map(
        per_device,
        mesh=mesh,
        in_specs=placed,
        out_specs=(P("rhs", "pts"), P("rhs", "pts"), P("rhs", "pts")),
        check_vma=False,
    )
```

time: 284 us -> 81.6 us (0.29)
  blocking collectives: 106 us -> 0 us
  waiting for transfers between devices: 61.3 us -> 5.99 us
  other arithmetic: 32.3 us -> 0.02 us
  Pallas kernels: 0 us -> 22.1 us
  matrix products: 20.7 us -> 0 us
  between operations: 14.7 us -> 0.78 us
  starting transfers between devices: 21.4 us -> 25.2 us
    psum x2 -> x0, blocking collectives: 81.7 us -> none  [per_device(): lax.psum((jnp.sum(residual * residual, axis=1), jnp.sum(res_image * resid...]
    reduce_scatter x3 -> x0, waiting for transfers between devices: 51.6 us -> none  [apply_operator(): lax.psum_scatter(summed, 'rhs', scatter_dimension=0, tiled=True)]
    unnamed x10 -> x38, local copies, waits for them, and re-layouts: 0.04 us -> 27.9 us
    all_gather x3 -> x0, blocking collectives: 24 us -> none  [apply_operator(): wide_all = lax.all_gather(wide_vec, 'rhs', axis=0, tiled=True)]
    pallas_call x0 -> x9, Pallas kernels: none -> 22.1 us  [call(): pl.pallas_call(kernel, out_shape=outs, in_specs=[SM] * scalars + [VM] * (...]
    gather x15 -> x0, local copies, waits for them, and re-layouts: 21.5 us -> none  [the longest x3 6.5 us: turn(): point_blocks[home_block + REACH]]
    scatter-add x3 -> x0, other arithmetic: 21.1 us -> none  [turn(): return running.at[:, home_block].add(contribution)]
    dot_general x3 -> x0, matrix products: 20.7 us -> none  [turn(): jnp.einsum('gij,cgj->cgi', weights, vec_blocks[:, other_block], preferred...]
  transfers between devices with their start and end apart: 11 -> 9, of which waited for: 7 -> 3; matrix products, arithmetic and copies ran while one was open for 2% -> 0% of each run, Pallas kernels for 0% -> 21%
where the time goes in v2:
time: 81.6 us; the launch traced here: 82 us
  local copies, waits for them, and re-layouts  27.9 us (34%)
  starting transfers between devices  25.2 us (31%)
  Pallas kernels  22.1 us (27%)
  waiting for transfers between devices  5.99 us (7%)
    unnamed x38, local copies, waits for them, and re-layouts  27.9 us
    pallas_call x9, Pallas kernels, call(): pl.pallas_call(kernel, out_shape=outs, in_specs=[SM] * scalars + [VM] * (...  22.1 us
    ppermute x3, starting transfers between devices, both_sides(): lax.ppermute(x, 'pts', swap_pairs(count, 0))  17.2 us
    ppermute x3, starting transfers between devices, total_over_points(): lax.ppermute(x, 'pts', [(i, i ^ k * step) for i in range(count)])  5.62 us
    ppermute x3, waiting for transfers between devices, both_sides(): lax.ppermute(x, 'pts', swap_pairs(count, 0))  3.76 us
    ppermute x3, starting transfers between devices, both_sides(): lax.ppermute(x, 'pts', swap_pairs(count, 1))  2.31 us
    ppermute x3, waiting for transfers between devices, total_over_points(): lax.ppermute(x, 'pts', [(i, i ^ k * step) for i in range(count)])  2.23 us
  transfers between devices with their start and end apart: 9, of which 3 were waited for; matrix products, arithmetic and copies ran while one was open for 0% of the time, Pallas kernels for 21%

profile of v2, /device:TPU:0, one launch (start us, length us, event | category | flops | bytes accessed | tf_op | source)
XLA Modules:
  0.0 82.0 jit_solution(11427351271015424200)
XLA Ops:
  0.6 0.0 copy-start.7
  0.6 0.9 %copy-done.7 = f32[16,2048]{1,0:T(8,128)S(1)} copy-done((f32[16,2048]{1,0:T(8,128)S(1)}, f32[16,2048]{1,0:T(8,128)}, u32[]{:S(2)}) %copy-start.7) | copy-done | bytes 131096
  1.5 0.0 copy-start.12
  1.5 0.9 %copy-done.12 = bf16[2048,32]{0,1:T(8,128)(2,1)S(1)} copy-done((bf16[2048,32]{0,1:T(8,128)(2,1)S(1)}, bf16[2048,32]{0,1:T(8,128)(2,1)}, u32[]{:S(2)}) %copy-start.12) | copy-done | bytes 131096
  2.4 0.0 copy-start.10
  2.5 0.7 collective-permute-start.1
  3.1 5.8 %collective-permute-start = (bf16[48,2048]{1,0:T(8,128)(2,1)S(1)}, bf16[48,2048]{1,0:T(8,128)(2,1)S(1)}, u32[]{:S(2)}, u32[]{:S(2)}) collective-permute-start(bf16[48,2048]{1,0:T(8,128)(2,1)S(1)} %prep.1.own_ref), channel_id=1, source_target_pairs={{0,4},{4,0},{8,12},{12,8},{16,20},{20,16},{24,28},{28,24},{1,5},{5... | collective-permute-start | bytes 589832 | tf_op jit(solution)/shard_map/ppermute | solution.py:324
  8.9 0.0 copy-start.9
  8.9 0.7 copy-done.9
  9.6 10.0 %local_tiles.1 = (bf16[257,128,128]{2,1,0:T(8,128)(2,1)S(1)}, bf16[289,128,128]{2,1,0:T(8,128)(2,1)S(1)}, bf16[16,128,128]{2,1,0:T(8,128)(2,1)S(1)}, f32[16,2048]{1,0:T(8,128)S(1)}) custom-call(s32[16,33]{1,0:T(8,128)S(1)} %copy-done.9, bf16[48,2048]{1,0:T(8,128)(2,1)S(1)} %prep.1.own_ref), custom_call_target="tpu_custom_call" | custom-call | flops 8000000000 | bytes 24000000 | tf_op jit(solution)/shard_map/local_tiles/pallas_call | solution.py:374
  19.7 0.0 copy-start
  19.7 3.7 %copy-done = bf16[289,128,128]{2,1,0:T(8,128)(2,1)} copy-done((bf16[289,128,128]{2,1,0:T(8,128)(2,1)}, bf16[289,128,128]{2,1,0:T(8,128)(2,1)S(1)}, u32[]{:S(2)}) %copy-start) | copy-done | bytes 9469976
  23.3 0.0 copy-start.6
  23.3 3.3 %copy-done.6 = bf16[257,128,128]{2,1,0:T(8,128)(2,1)} copy-done((bf16[257,128,128]{2,1,0:T(8,128)(2,1)}, bf16[257,128,128]{2,1,0:T(8,128)(2,1)S(1)}, u32[]{:S(2)}) %copy-start.6) | copy-done | bytes 8421400
  26.7 0.0 collective-permute-done.other_ref.a_ref
  26.7 0.0 copy-done.10
  26.7 0.0 copy-start.1
  26.7 3.7 %copy-done.1 = bf16[289,128,128]{2,1,0:T(8,128)(2,1)S(1)} copy-done((bf16[289,128,128]{2,1,0:T(8,128)(2,1)S(1)}, bf16[289,128,128]{2,1,0:T(8,128)(2,1)}, u32[]{:S(2)}) %copy-start.1) | copy-done | bytes 9469976
  30.4 0.0 copy-start.8
  30.4 0.0 copy-start.11
  30.4 0.0 slice-start.3
  30.4 0.0 slice-start.4
  30.4 2.9 %side_tiles.1.tiles_in = bf16[289,128,128]{2,1,0:T(8,128)(2,1)S(1)} custom-call(s32[1]{0:T(128)} %bitcast.before_ref, s32[16,33]{1,0:T(8,128)S(1)} %copy-done.10, bf16[48,2048]{1,0:T(8,128)(2,1)S(1)} %collective-permute-done.other_ref.a_ref, bf16[16,128,128]{2,1,0:T(8,128)(2,1)S(1)} %get-tuple-element.13.right_ref, ...), custom_call_target="tpu_custom_call", output_to_operand_aliasing={{}: (4, {})} | custom-call | flops 5000000000 | bytes 15000000 | tf_op jit(solution)/shard_map/side_tiles/pallas_call | solution.py:374
  33.2 0.0 copy-start.2
  33.2 3.7 %copy-done.2 = bf16[289,128,128]{2,1,0:T(8,128)(2,1)} copy-done((bf16[289,128,128]{2,1,0:T(8,128)(2,1)}, bf16[289,128,128]{2,1,0:T(8,128)(2,1)S(1)}, u32[]{:S(2)}) %copy-start.2) | copy-done | bytes 9469976
  36.9 0.0 collective-permute-done.1.b_ref
  36.9 0.0 copy-done.8
  36.9 0.0 copy-done.11
  36.9 0.0 copy-start.3
  36.9 3.7 %copy-done.3 = bf16[289,128,128]{2,1,0:T(8,128)(2,1)S(1)} copy-done((bf16[289,128,128]{2,1,0:T(8,128)(2,1)S(1)}, bf16[289,128,128]{2,1,0:T(8,128)(2,1)}, u32[]{:S(2)}) %copy-start.3) | copy-done | bytes 9469976
  40.6 0.0 slice-start.5
  40.6 2.3 %image.1 = (bf16[289,128,128]{2,1,0:T(8,128)(2,1)S(1)}, f32[16,2048]{1,0:T(8,128)S(1)}, bf16[16,2048]{1,0:T(8,128)(2,1)S(1)}) custom-call(s32[1]{0:T(128)} %bitcast.before_ref, s32[16,33]{1,0:T(8,128)S(1)} %copy-done.10, bf16[48,2048]{1,0:T(8,128)(2,1)S(1)} %collective-permute-done.other_ref.a_ref, ...), custom_call_target="tpu_custom_call", output_to_operand_aliasing={{0}: (5, {})} | custom-call | flops 7000000000 | bytes 21000000 | tf_op jit(solution)/shard_map/image/pallas_call | solution.py:374
  42.9 0.0 copy-start.4
  42.9 3.7 %copy-done.4 = bf16[289,128,128]{2,1,0:T(8,128)(2,1)} copy-done((bf16[289,128,128]{2,1,0:T(8,128)(2,1)}, bf16[289,128,128]{2,1,0:T(8,128)(2,1)S(1)}, u32[]{:S(2)}) %copy-start.4) | copy-done | bytes 9469976
  46.5 0.7 collective-permute-start.3
  47.2 7.3 %collective-permute-start.2 = (bf16[16,2048]{1,0:T(8,128)(2,1)S(1)}, bf16[16,2048]{1,0:T(8,128)(2,1)S(1)}, u32[]{:S(2)}, u32[]{:S(2)}) collective-permute-start(bf16[16,2048]{1,0:T(8,128)(2,1)S(1)} %get-tuple-element.16.own_ref), channel_id=1, source_target_pairs={{0,4},{4,0},{8,12},{12,8},{16,20},{20,16},{24,28},{28,24},{1,5},{5... | collective-permute-start | bytes 196616 | tf_op jit(solution)/shard_map/ppermute | solution.py:324
  54.5 0.0 slice-done.3
  54.5 0.0 slice-done.4
  54.5 0.0 slice-done.5
  54.5 0.0 slice-start
  54.5 1.2 %own_products.1.part_ref = f32[16,2048]{1,0:T(8,128)S(1)} custom-call(bf16[16,2048]{1,0:T(8,128)(2,1)S(1)} %get-tuple-element.16.own_ref, bf16[257,128,128]{2,1,0:T(8,128)(2,1)S(1)} %bitcast.6), custom_call_target="tpu_custom_call" | custom-call | flops 2000000000 | bytes 6000000 | tf_op jit(solution)/shard_map/own_products/pallas_call | solution.py:374
  55.7 0.0 collective-permute-done.3.b_ref
  55.7 1.0 %collective-permute-done.2.a_ref = bf16[16,2048]{1,0:T(8,128)(2,1)S(1)} collective-permute-done((bf16[16,2048]{1,0:T(8,128)(2,1)S(1)}, bf16[16,2048]{1,0:T(8,128)(2,1)S(1)}, u32[]{:S(2)}, u32[]{:S(2)}) %collective-permute-start.2) | collective-permute-done | bytes 65568 | tf_op jit(solution)/shard_map/ppermute | solution.py:324
  56.8 0.0 copy-start.5
  56.8 3.7 %copy-done.5 = bf16[289,128,128]{2,1,0:T(8,128)(2,1)S(1)} copy-done((bf16[289,128,128]{2,1,0:T(8,128)(2,1)S(1)}, bf16[289,128,128]{2,1,0:T(8,128)(2,1)}, u32[]{:S(2)}) %copy-start.5) | copy-done | bytes 9469976
  60.4 0.0 slice-start.1
  60.4 0.0 slice-start.2
  60.4 1.5 %twice.1 = (f32[16,2048]{1,0:T(8,128)S(1)}, bf16[32,2304]{1,0:T(8,128)(2,1)S(1)}, f32[16,128]{1,0:T(8,128)S(1)}) custom-call(s32[1]{0:T(128)} %bitcast.before_ref, bf16[16,2048]{1,0:T(8,128)(2,1)S(1)} %collective-permute-done.2.a_ref, bf16[16,2048]{1,0:T(8,128)(2,1)S(1)} %collective-permute-done.3.b_ref, bf16[289,128,128]{2,1,0:T(8,128)(2,1)S(1)} %copy-done.5, ...), custom_call_target="tpu_custom_call" | custom-call | flops 2000000000 | bytes 6000000 | tf_op jit(solution)/shard_map/twice/pallas_call | solution.py:374
  61.9 1.0 %collective-permute-start.8 = (bf16[32,2304]{1,0:T(8,128)(2,1)S(1)}, bf16[32,2304]{1,0:T(8,128)(2,1)S(1)}, u32[]{:S(2)}, u32[]{:S(2)}) collective-permute-start(bf16[32,2304]{1,0:T(8,128)(2,1)S(1)} %get-tuple-element.21.own_ref), channel_id=1, source_target_pairs={{4,8},{8,4},{12,16},{16,12},{20,24},{24,20},{5,9},{9,5},{13,17},{1... | collective-permute-start | bytes 442376 | tf_op jit(solution)/shard_map/ppermute | solution.py:325
  62.9 4.1 %collective-permute-start.4 = (bf16[32,2304]{1,0:T(8,128)(2,1)S(1)}, bf16[32,2304]{1,0:T(8,128)(2,1)S(1)}, u32[]{:S(2)}, u32[]{:S(2)}) collective-permute-start(bf16[32,2304]{1,0:T(8,128)(2,1)S(1)} %get-tuple-element.21.own_ref), channel_id=1, source_target_pairs={{0,4},{4,0},{8,12},{12,8},{16,20},{20,16},{24,28},{28,24},{1,5},{5... | collective-permute-start | bytes 442376 | tf_op jit(solution)/shard_map/ppermute | solution.py:324
  67.0 1.5 %own_products_both.1.part_ref = f32[32,2048]{1,0:T(8,128)S(1)} custom-call(bf16[32,2304]{1,0:T(8,128)(2,1)S(1)} %get-tuple-element.21.own_ref, bf16[257,128,128]{2,1,0:T(8,128)(2,1)S(1)} %bitcast.6), custom_call_target="tpu_custom_call" | custom-call | flops 2000000000 | bytes 6000000 | tf_op jit(solution)/shard_map/own_products_both/pallas_call | solution.py:374
  68.6 2.7 %collective-permute-done.4.a_ref = bf16[32,2304]{1,0:T(8,128)(2,1)S(1)} collective-permute-done((bf16[32,2304]{1,0:T(8,128)(2,1)S(1)}, bf16[32,2304]{1,0:T(8,128)(2,1)S(1)}, u32[]{:S(2)}, u32[]{:S(2)}) %collective-permute-start.4) | collective-permute-done | bytes 147488 | tf_op jit(solution)/shard_map/ppermute | solution.py:324
  71.3 5.0 %collective-permute-start.7 = (f32[16,128]{1,0:T(8,128)S(1)}, f32[16,128]{1,0:T(8,128)S(1)}, u32[]{:S(2)}, u32[]{:S(2)}) collective-permute-start(f32[16,128]{1,0:T(8,128)S(1)} %fusion), channel_id=1, source_target_pairs={{0,24},{4,28},{8,16},{12,20},{16,8},{20,12},{24,0},{28,4},{1,25},{... | collective-permute-start | bytes 24584 | tf_op jit(solution)/shard_map/ppermute | solution.py:341
  76.3 0.0 collective-permute-start.6
  76.3 0.6 collective-permute-start.5
  76.9 0.0 collective-permute-done.8.b_ref
  76.9 0.0 slice-done
  76.9 0.0 slice-done.1
  76.9 0.0 slice-done.2
  77.0 1.6 %products.1.prod_ref = f32[32,2048]{1,0:T(8,128)S(1)} custom-call(s32[1]{0:T(128)} %bitcast.before_ref, bf16[32,2304]{1,0:T(8,128)(2,1)S(1)} %collective-permute-done.4.a_ref, bf16[32,2304]{1,0:T(8,128)(2,1)S(1)} %collective-permute-done.8.b_ref, bf16[289,128,128]{2,1,0:T(8,128)(2,1)S(1)} %bitcast.4, f32[32,2048]{1,0:T(8,128)S(1)} %own_products_both.1.part_ref), custom_call_target="tpu_custom_call" | custom-call | flops 2000000000 | bytes 6000000 | tf_op jit(solution)/shard_map/products/pallas_call | solution.py:374
  78.6 0.0 collective-permute-done.7
  78.6 2.2 %collective-permute-done.6 = f32[16,128]{1,0:T(8,128)S(1)} collective-permute-done((f32[16,128]{1,0:T(8,128)S(1)}, f32[16,128]{1,0:T(8,128)S(1)}, u32[]{:S(2)}, u32[]{:S(2)}) %collective-permute-start.6) | collective-permute-done | bytes 8224 | tf_op jit(solution)/shard_map/ppermute | solution.py:341
  80.8 0.0 collective-permute-done.5
  80.8 1.2 %update.1 = (f32[16,2048]{1,0:T(8,128)}, f32[16,2048]{1,0:T(8,128)}, f32[16,2048]{1,0:T(8,128)}) custom-call(f32[16,128]{1,0:T(8,128)S(1)} %add_add_fusion.sums_ref, f32[1,2048]{1,0:T(1,128)S(1)} %bitcast.9, f32[16,2048]{1,0:T(8,128)S(1)} %copy-done.8, f32[16,2048]{1,0:T(8,128)S(1)} %get-tuple-element.19.image_ref, ...), custom_call_target="tpu_custom_call" | custom-call | flops 2000000000 | bytes 6000000 | tf_op jit(solution)/shard_map/update/pallas_call | solution.py:374
  (6 shorter events, 0.0 us)
Async XLA Ops:
  0.6 0.9 %copy-start.7 = (f32[16,2048]{1,0:T(8,128)S(1)}, f32[16,2048]{1,0:T(8,128)}, u32[]{:S(2)}) copy-start(f32[16,2048]{1,0:T(8,128)} %vec_ref.7) | copy-start | bytes 393220
  1.5 0.9 %copy-start.12 = (bf16[2048,32]{0,1:T(8,128)(2,1)S(1)}, bf16[2048,32]{0,1:T(8,128)(2,1)}, u32[]{:S(2)}) copy-start(bf16[2048,32]{0,1:T(8,128)(2,1)} %param.4) | copy-start | bytes 393220
  2.4 24.2 %copy-start.10 = (s32[16,33]{1,0:T(8,128)S(1)}, s32[16,33]{1,0:T(8,128)}, u32[]{:S(2)}) copy-start(s32[16,33]{1,0:T(8,128)} %pattern_ref.5) | copy-start | bytes 6340
  2.5 34.4 %collective-permute-start.1 = (bf16[48,2048]{1,0:T(8,128)(2,1)S(1)}, bf16[48,2048]{1,0:T(8,128)(2,1)S(1)}, u32[]{:S(2)}, u32[]{:S(2)}) collective-permute-start(bf16[48,2048]{1,0:T(8,128)(2,1)S(1)} %prep.1.own_ref), channel_id=1, source_target_pairs={{4,8},{8,4},{12,16},{16,12},{20,24},{24,20},{5,9},{9,5},{13,17},{1... | collective-permute-start | bytes 589832 | tf_op jit(solution)/shard_map/ppermute | solution.py:325
  3.1 23.5 %collective-permute-start = (bf16[48,2048]{1,0:T(8,128)(2,1)S(1)}, bf16[48,2048]{1,0:T(8,128)(2,1)S(1)}, u32[]{:S(2)}, u32[]{:S(2)}) collective-permute-start(bf16[48,2048]{1,0:T(8,128)(2,1)S(1)} %prep.1.own_ref), channel_id=1, source_target_pairs={{0,4},{4,0},{8,12},{12,8},{16,20},{20,16},{24,28},{28,24},{1,5},{5... | collective-permute-start | bytes 589832 | tf_op jit(solution)/shard_map/ppermute | solution.py:324
  8.9 0.7 copy-start.9
  19.7 3.7 %copy-start = (bf16[289,128,128]{2,1,0:T(8,128)(2,1)}, bf16[289,128,128]{2,1,0:T(8,128)(2,1)S(1)}, u32[]{:S(2)}) copy-start(bf16[289,128,128]{2,1,0:T(8,128)(2,1)S(1)} %get-tuple-element.14.tiles_in) | copy-start | bytes 28409860
  23.3 3.3 %copy-start.6 = (bf16[257,128,128]{2,1,0:T(8,128)(2,1)}, bf16[257,128,128]{2,1,0:T(8,128)(2,1)S(1)}, u32[]{:S(2)}) copy-start(bf16[257,128,128]{2,1,0:T(8,128)(2,1)S(1)} %get-tuple-element.18.tiles_ref) | copy-start | bytes 25264132
  26.7 3.7 %copy-start.1 = (bf16[289,128,128]{2,1,0:T(8,128)(2,1)S(1)}, bf16[289,128,128]{2,1,0:T(8,128)(2,1)}, u32[]{:S(2)}) copy-start(bf16[289,128,128]{2,1,0:T(8,128)(2,1)} %copy-done) | copy-start | bytes 28409860
  30.4 6.5 %copy-start.8 = (f32[16,2048]{1,0:T(8,128)S(1)}, f32[16,2048]{1,0:T(8,128)}, u32[]{:S(2)}) copy-start(f32[16,2048]{1,0:T(8,128)} %vec_ref.7) | copy-start | bytes 393220
  30.4 6.5 %copy-start.11 = (f32[2048]{0:T(1024)S(1)}, f32[2048]{0:T(1024)}, u32[]{:S(2)}) copy-start(f32[2048]{0:T(1024)} %param.5) | copy-start | bytes 24580
  30.4 24.2 %slice-start.3 = ((s8[8421376]{0:T(1024)(128)(4,1)}), s8[4194304]{0:T(1024)(128)(4,1)S(1)}, s32[]{:S(2)}) async-start(s8[8421376]{0:T(1024)(128)(4,1)} %bitcast.5), calls=%async_computation.3 | async-start | bytes 8388608
  30.4 24.2 %slice-start.4 = ((s8[8421376]{0:T(1024)(128)(4,1)}), s8[4194304]{0:T(1024)(128)(4,1)S(1)}, s32[]{:S(2)}) async-start(s8[8421376]{0:T(1024)(128)(4,1)} %bitcast.5), calls=%async_computation.4 | async-start | bytes 8388608
  33.2 3.7 %copy-start.2 = (bf16[289,128,128]{2,1,0:T(8,128)(2,1)}, bf16[289,128,128]{2,1,0:T(8,128)(2,1)S(1)}, u32[]{:S(2)}) copy-start(bf16[289,128,128]{2,1,0:T(8,128)(2,1)S(1)} %side_tiles.1.tiles_in) | copy-start | bytes 28409860
  36.9 3.7 %copy-start.3 = (bf16[289,128,128]{2,1,0:T(8,128)(2,1)S(1)}, bf16[289,128,128]{2,1,0:T(8,128)(2,1)}, u32[]{:S(2)}) copy-start(bf16[289,128,128]{2,1,0:T(8,128)(2,1)} %copy-done.2) | copy-start | bytes 28409860
  40.6 13.9 %slice-start.5 = ((s8[8421376]{0:T(1024)(128)(4,1)}), s8[32768]{0:T(1024)(128)(4,1)S(1)}, s32[]{:S(2)}) async-start(s8[8421376]{0:T(1024)(128)(4,1)} %bitcast.5), calls=%async_computation.5 | async-start | bytes 65536
  42.9 3.7 %copy-start.4 = (bf16[289,128,128]{2,1,0:T(8,128)(2,1)}, bf16[289,128,128]{2,1,0:T(8,128)(2,1)S(1)}, u32[]{:S(2)}) copy-start(bf16[289,128,128]{2,1,0:T(8,128)(2,1)S(1)} %get-tuple-element.17.tiles_ref) | copy-start | bytes 28409860
  46.5 9.2 %collective-permute-start.3 = (bf16[16,2048]{1,0:T(8,128)(2,1)S(1)}, bf16[16,2048]{1,0:T(8,128)(2,1)S(1)}, u32[]{:S(2)}, u32[]{:S(2)}) collective-permute-start(bf16[16,2048]{1,0:T(8,128)(2,1)S(1)} %get-tuple-element.16.own_ref), channel_id=1, source_target_pairs={{4,8},{8,4},{12,16},{16,12},{20,24},{24,20},{5,9},{9,5},{13,17},{1... | collective-permute-start | bytes 196616 | tf_op jit(solution)/shard_map/ppermute | solution.py:325
  47.2 9.6 %collective-permute-start.2 = (bf16[16,2048]{1,0:T(8,128)(2,1)S(1)}, bf16[16,2048]{1,0:T(8,128)(2,1)S(1)}, u32[]{:S(2)}, u32[]{:S(2)}) collective-permute-start(bf16[16,2048]{1,0:T(8,128)(2,1)S(1)} %get-tuple-element.16.own_ref), channel_id=1, source_target_pairs={{0,4},{4,0},{8,12},{12,8},{16,20},{20,16},{24,28},{28,24},{1,5},{5... | collective-permute-start | bytes 196616 | tf_op jit(solution)/shard_map/ppermute | solution.py:324
  54.5 22.4 %slice-start = ((s8[9469952]{0:T(1024)(128)(4,1)}), s8[4194304]{0:T(1024)(128)(4,1)S(1)}, s32[]{:S(2)}) async-start(s8[9469952]{0:T(1024)(128)(4,1)} %bitcast.3), calls=%async_computation | async-start | bytes 8388608
  56.8 3.7 %copy-start.5 = (bf16[289,128,128]{2,1,0:T(8,128)(2,1)S(1)}, bf16[289,128,128]{2,1,0:T(8,128)(2,1)}, u32[]{:S(2)}) copy-start(bf16[289,128,128]{2,1,0:T(8,128)(2,1)} %copy-done.4) | copy-start | bytes 28409860
  60.4 16.5 %slice-start.1 = ((s8[9469952]{0:T(1024)(128)(4,1)}), s8[4194304]{0:T(1024)(128)(4,1)S(1)}, s32[]{:S(2)}) async-start(s8[9469952]{0:T(1024)(128)(4,1)} %bitcast.3), calls=%async_computation.1 | async-start | bytes 8388608
  60.4 16.5 %slice-start.2 = ((s8[9469952]{0:T(1024)(128)(4,1)}), s8[1081344]{0:T(1024)(128)(4,1)S(1)}, s32[]{:S(2)}) async-start(s8[9469952]{0:T(1024)(128)(4,1)} %bitcast.3), calls=%async_computation.2 | async-start | bytes 2162688
  61.9 15.0 %collective-permute-start.8 = (bf16[32,2304]{1,0:T(8,128)(2,1)S(1)}, bf16[32,2304]{1,0:T(8,128)(2,1)S(1)}, u32[]{:S(2)}, u32[]{:S(2)}) collective-permute-start(bf16[32,2304]{1,0:T(8,128)(2,1)S(1)} %get-tuple-element.21.own_ref), channel_id=1, source_target_pairs={{4,8},{8,4},{12,16},{16,12},{20,24},{24,20},{5,9},{9,5},{13,17},{1... | collective-permute-start | bytes 442376 | tf_op jit(solution)/shard_map/ppermute | solution.py:325
  62.9 8.4 %collective-permute-start.4 = (bf16[32,2304]{1,0:T(8,128)(2,1)S(1)}, bf16[32,2304]{1,0:T(8,128)(2,1)S(1)}, u32[]{:S(2)}, u32[]{:S(2)}) collective-permute-start(bf16[32,2304]{1,0:T(8,128)(2,1)S(1)} %get-tuple-element.21.own_ref), channel_id=1, source_target_pairs={{0,4},{4,0},{8,12},{12,8},{16,20},{20,16},{24,28},{28,24},{1,5},{5... | collective-permute-start | bytes 442376 | tf_op jit(solution)/shard_map/ppermute | solution.py:324
  71.3 7.3 %collective-permute-start.7 = (f32[16,128]{1,0:T(8,128)S(1)}, f32[16,128]{1,0:T(8,128)S(1)}, u32[]{:S(2)}, u32[]{:S(2)}) collective-permute-start(f32[16,128]{1,0:T(8,128)S(1)} %fusion), channel_id=1, source_target_pairs={{0,24},{4,28},{8,16},{12,20},{16,8},{20,12},{24,0},{28,4},{1,25},{... | collective-permute-start | bytes 24584 | tf_op jit(solution)/shard_map/ppermute | solution.py:341
  76.3 4.5 %collective-permute-start.6 = (f32[16,128]{1,0:T(8,128)S(1)}, f32[16,128]{1,0:T(8,128)S(1)}, u32[]{:S(2)}, u32[]{:S(2)}) collective-permute-start(f32[16,128]{1,0:T(8,128)S(1)} %fusion), channel_id=1, source_target_pairs={{0,16},{4,20},{8,24},{12,28},{16,0},{20,4},{24,8},{28,12},{1,17},{... | collective-permute-start | bytes 24584 | tf_op jit(solution)/shard_map/ppermute | solution.py:341
  76.3 4.5 %collective-permute-start.5 = (f32[16,128]{1,0:T(8,128)S(1)}, f32[16,128]{1,0:T(8,128)S(1)}, u32[]{:S(2)}, u32[]{:S(2)}) collective-permute-start(f32[16,128]{1,0:T(8,128)S(1)} %fusion), channel_id=1, source_target_pairs={{0,8},{4,12},{8,0},{12,4},{16,24},{20,28},{24,16},{28,20},{1,9},{5... | collective-permute-start | bytes 24584 | tf_op jit(solution)/shard_map/ppermute | solution.py:341

commit v3 on v2

--- a/solution.py
+++ b/solution.py
@@ -21,7 +21,7 @@
 SUMS = 9
 UNROLL = 16
 TAIL = 4
-FIELD = 9
+FIELD = 10
 MIB = 1 << 20
 
 f32 = jnp.float32
@@ -111,7 +111,11 @@
 
 def side_slot(blocks, home, other, after):
     wide = other - 2 * (home // 2) + (blocks if after else 0)
-    return ((home // 2) * (blocks + 2) + wide) * 2 + home % 2
+    return blocks * blocks + ((home // 2) * (blocks + 2) + wide) * 2 + home % 2
+
+
+def spare_slot(blocks):
+    return 2 * blocks * (blocks + 1)
 
 
 def local_entries(blocks):
@@ -149,8 +153,8 @@
     lax.fori_loop(0, count, step, 0)
 
 
-def products(vec, tiles_ref, pair, wide):
-    tiles = tiles_ref[pair * 2 * wide : (pair + 1) * 2 * wide].reshape(wide, 2, BLK, BLK)
+def products(vec, tiles_ref, first, wide):
+    tiles = tiles_ref[first : first + 2 * wide].reshape(wide, 2, BLK, BLK)
     tiles = jnp.concatenate([tiles[:, 0].reshape(wide * BLK, BLK), tiles[:, 1].reshape(wide * BLK, BLK)], axis=1)
     return jnp.dot(vec, tiles, preferred_element_type=f32)
 
@@ -161,7 +165,7 @@
 
 def local_products(blocks, vec, tiles_ref, out_ref):
     for pair in range(blocks // 2):
-        out_ref[:, pair_cols(pair)] = products(vec, tiles_ref, pair, blocks)
+        out_ref[:, pair_cols(pair)] = products(vec, tiles_ref, pair * 2 * blocks, blocks)
 
 
 def gather_sides(blocks, before, side_a, side_b, wide_ref):
@@ -174,7 +178,7 @@
 
 def side_products(blocks, pair, wide_ref, tiles_ref):
     vec = wide_ref[:, pair * 2 * BLK : (pair * 2 + blocks + 2) * BLK]
-    return products(vec, tiles_ref, pair, blocks + 2)
+    return products(vec, tiles_ref, blocks * blocks + pair * 2 * (blocks + 2), blocks + 2)
 
 
 def prep_kernel(points_ref, vec_ref, out_ref):
@@ -183,9 +187,9 @@
 
 
 def local_kernel(
-    blocks, pattern_ref, own_ref, local_ref, side_ref, right_ref, part_ref, left_ref, list_ref, dead_ref
+    blocks, pattern_ref, own_ref, tiles_ref, right_ref, part_ref, left_ref, list_ref, dead_ref
 ):
-    spare = blocks * blocks
+    spare = spare_slot(blocks)
     fill_features(own_ref[:F, :], left_ref, right_ref)
     dead = jnp.int32(0)
     for after in (False, True):
@@ -193,11 +197,11 @@
             slot = side_slot(blocks, home, other, after)
             dead_ref[dead] = jnp.int32(entry(slot, slot, 0, 0))
             dead = dead + (1 - pattern_ref[home, column])
-    clear_tiles(dead, dead_ref, side_ref)
+    clear_tiles(dead, dead_ref, tiles_ref)
     for pair in range(blocks // 2):
-        first = pair * 2 * (blocks + 2)
-        side_ref[first + 1] = jnp.zeros((BLK, BLK), bf16)
-        side_ref[first + 2 * (blocks + 1)] = jnp.zeros((BLK, BLK), bf16)
+        first = blocks * blocks + pair * 2 * (blocks + 2)
+        tiles_ref[first + 1] = jnp.zeros((BLK, BLK), bf16)
+        tiles_ref[first + 2 * (blocks + 1)] = jnp.zeros((BLK, BLK), bf16)
     dead = jnp.int32(0)
     count = jnp.int32(0)
     for home, other, column in local_entries(blocks):
@@ -208,9 +212,9 @@
         dead = dead + (1 - live)
         count = count + live
     pad_list(count, list_ref, spare)
-    clear_tiles(dead, dead_ref, local_ref)
-    make_tiles(count, list_ref, left_ref, right_ref, local_ref, True)
-    local_products(blocks, own_ref[F:, :], local_ref, part_ref)
+    clear_tiles(dead, dead_ref, tiles_ref)
+    make_tiles(count, list_ref, left_ref, right_ref, tiles_ref, True)
+    local_products(blocks, own_ref[F:, :], tiles_ref, part_ref)
 
 
 def make_side(blocks, before, pattern_ref, other_ref, right_ref, tiles_ref, left_ref, list_ref, count_ref):
@@ -225,7 +229,7 @@
         count_ref[0] = list_side(blocks, True, pattern_ref, list_ref)
 
     count = count_ref[0]
-    pad_list(count, list_ref, blocks * (blocks + 2))
+    pad_list(count, list_ref, spare_slot(blocks))
     make_tiles(count, list_ref, left_ref, right_ref, tiles_ref, False)
 
 
@@ -358,10 +362,9 @@
     blocks = local_rows // BLK
     assert blocks == REACH
     before = (lax.axis_index("pts") % 2).astype(jnp.int32).reshape(1)
-    params = pltpu.CompilerParams(vmem_limit_bytes=20 * MIB)
+    params = pltpu.CompilerParams(vmem_limit_bytes=12 * MIB)
     full = (width, local_rows)
-    local_type = pltpu.VMEM((blocks * blocks + 1, BLK, BLK), bf16)
-    side_type = pltpu.VMEM((blocks * (blocks + 2) + 1, BLK, BLK), bf16)
+    tiles_type = pltpu.VMEM((spare_slot(blocks) + 1, BLK, BLK), bf16)
     left_scratch = pltpu.VMEM((blocks, BLK, LANES), bf16)
     list_scratch = pltpu.SMEM((blocks * (blocks + 1) // 2 + TAIL,), jnp.int32)
     count_scratch = pltpu.SMEM((1,), jnp.int32)
@@ -379,7 +382,7 @@
             scratch_shapes=list(scratch),
             input_output_aliases=aliases or {},
             compiler_params=params,
-            cost_estimate=pl.CostEstimate(flops=us * 10**9, bytes_accessed=us * 3 * 10**6, transcendentals=0),
+            cost_estimate=pl.CostEstimate(flops=10**9, bytes_accessed=10**7, transcendentals=0),
             name=name,
         )(*ins[:scalars], *[near(x) for x in ins[scalars:]])
 
@@ -388,30 +391,30 @@
         prep_kernel, "prep", (points.T, right_side), pltpu.VMEM((F + width, local_rows), bf16)
     )
     halo_a, halo_b = both_sides(payload)
-    local_tiles, side_tiles, right, part = call(
+    tiles, right, part = call(
         functools.partial(local_kernel, blocks),
         "local_tiles",
         (pattern, payload),
-        (local_type, side_type, pltpu.VMEM((blocks, LANES, BLK), bf16), pltpu.VMEM(full, f32)),
+        (tiles_type, pltpu.VMEM((blocks, LANES, BLK), bf16), pltpu.VMEM(full, f32)),
         (left_scratch, list_scratch, dead_scratch),
         scalars=1,
         us=8,
     )
-    side_tiles = call(
+    tiles = call(
         functools.partial(side_kernel, blocks),
         "side_tiles",
-        (before, pattern, halo_a, right, side_tiles),
-        side_type,
+        (before, pattern, halo_a, right, tiles),
+        tiles_type,
         (left_scratch, list_scratch, count_scratch),
         {4: 0},
         scalars=2,
         us=5,
     )
-    side_tiles, image, low = call(
+    tiles, image, low = call(
         functools.partial(first_kernel, blocks),
         "image",
-        (before, pattern, halo_a, halo_b, right, side_tiles, part, noise, right_side),
-        (side_type, pltpu.VMEM(full, f32), pltpu.VMEM(full, bf16)),
+        (before, pattern, halo_a, halo_b, right, tiles, part, noise, right_side),
+        (tiles_type, pltpu.VMEM(full, f32), pltpu.VMEM(full, bf16)),
         (left_scratch, wide(width), list_scratch, count_scratch),
         {5: 0},
         scalars=2,
@@ -419,13 +422,13 @@
     )
     low_a, low_b = both_sides(low)
     part = call(
-        functools.partial(own_kernel, blocks), "own_products", (low, local_tiles), pltpu.VMEM(full, f32)
+        functools.partial(own_kernel, blocks), "own_products", (low, tiles), pltpu.VMEM(full, f32)
     )
     low_type = pltpu.VMEM((2 * width, local_rows + 2 * LANES), bf16)
     twice, low, sums = call(
         functools.partial(second_kernel, blocks),
         "twice",
-        (before, low_a, low_b, side_tiles, part, noise, right_side, image),
+        (before, low_a, low_b, tiles, part, noise, right_side, image),
         (pltpu.VMEM(full, f32), low_type, pltpu.VMEM((width, LANES), f32)),
         (wide(width),),
         scalars=1,
@@ -433,11 +436,11 @@
     low_a, low_b = both_sides(low)
     sums = total_over_points(sums, low_a, width)
     both = pltpu.VMEM((2 * width, local_rows), f32)
-    part = call(functools.partial(own_kernel, blocks), "own_products_both", (low, local_tiles), both)
+    part = call(functools.partial(own_kernel, blocks), "own_products_both", (low, tiles), both)
     prods = call(
         functools.partial(third_kernel, blocks),
         "products",
-        (before, low_a, low_b, side_tiles, part),
+        (before, low_a, low_b, tiles, part),
         both,
         (wide(2 * width),),
         scalars=1,

time: 81.6 us -> 57.1 us (0.70)
  local copies, waits for them, and re-layouts: 27.9 us -> 2.51 us
  starting transfers between devices: 25.2 us -> 22.2 us
  Pallas kernels: 22.1 us -> 25 us
    unnamed x38 -> x12, local copies, waits for them, and re-layouts: 27.9 us -> 2.51 us
    ppermute x3, starting transfers between devices: 17.2 us -> 14.3 us  [both_sides(): lax.ppermute(x, 'pts', swap_pairs(count, 0))]
    pallas_call x9, Pallas kernels: 22.1 us -> 25 us  [call(): pl.pallas_call(kernel, out_shape=outs, in_specs=[SM] * scalars + [VM] * (...]
  transfers between devices with their start and end apart: 9 -> 9, of which waited for: 3 -> 3; matrix products, arithmetic and copies ran while one was open for 0% -> 0% of each run, Pallas kernels for 21% -> 35%
where the time goes in v3:
time: 57.1 us; the launch traced here: 56.9 us
  Pallas kernels  25 us (44%)
  starting transfers between devices  22.2 us (39%)
  waiting for transfers between devices  6.36 us (11%)
  local copies, waits for them, and re-layouts  2.51 us (4%)
  between operations  0.78 us (1%)
    pallas_call x9, Pallas kernels, call(): pl.pallas_call(kernel, out_shape=outs, in_specs=[SM] * scalars + [VM] * (...  25 us
    ppermute x3, starting transfers between devices, both_sides(): lax.ppermute(x, 'pts', swap_pairs(count, 0))  14.3 us
    ppermute x3, starting transfers between devices, total_over_points(): lax.ppermute(x, 'pts', [(i, i ^ k * step) for i in range(count)])  5.99 us
    ppermute x3, waiting for transfers between devices, both_sides(): lax.ppermute(x, 'pts', swap_pairs(count, 0))  4.09 us
    unnamed x12, local copies, waits for them, and re-layouts  2.51 us
    ppermute x3, waiting for transfers between devices, total_over_points(): lax.ppermute(x, 'pts', [(i, i ^ k * step) for i in range(count)])  2.26 us
    ppermute x3, starting transfers between devices, both_sides(): lax.ppermute(x, 'pts', swap_pairs(count, 1))  1.98 us
  transfers between devices with their start and end apart: 9, of which 3 were waited for; matrix products, arithmetic and copies ran while one was open for 0% of the time, Pallas kernels for 35%

profile of v3, /device:TPU:0, one launch (start us, length us, event | category | flops | bytes accessed | tf_op | source)
XLA Modules:
  0.0 56.9 jit_solution(1721063175944924884)
XLA Ops:
  0.6 0.0 copy-start
  0.6 0.9 %copy-done = f32[16,2048]{1,0:T(8,128)S(1)} copy-done((f32[16,2048]{1,0:T(8,128)S(1)}, f32[16,2048]{1,0:T(8,128)}, u32[]{:S(2)}) %copy-start) | copy-done | bytes 131096
  1.5 0.0 copy-start.5
  1.5 0.9 %copy-done.5 = bf16[2048,32]{0,1:T(8,128)(2,1)S(1)} copy-done((bf16[2048,32]{0,1:T(8,128)(2,1)S(1)}, bf16[2048,32]{0,1:T(8,128)(2,1)}, u32[]{:S(2)}) %copy-start.5) | copy-done | bytes 131096
  2.5 3.0 %collective-permute-start = (bf16[48,2048]{1,0:T(8,128)(2,1)S(1)}, bf16[48,2048]{1,0:T(8,128)(2,1)S(1)}, u32[]{:S(2)}, u32[]{:S(2)}) collective-permute-start(bf16[48,2048]{1,0:T(8,128)(2,1)S(1)} %prep.1.own_ref), channel_id=1, source_target_pairs={{0,4},{4,0},{8,12},{12,8},{16,20},{20,16},{24,28},{28,24},{1,5},{5... | collective-permute-start | bytes 589832 | tf_op jit(solution)/shard_map/ppermute | solution.py:328
  5.5 0.7 %collective-permute-start.1 = (bf16[48,2048]{1,0:T(8,128)(2,1)S(1)}, bf16[48,2048]{1,0:T(8,128)(2,1)S(1)}, u32[]{:S(2)}, u32[]{:S(2)}) collective-permute-start(bf16[48,2048]{1,0:T(8,128)(2,1)S(1)} %prep.1.own_ref), channel_id=1, source_target_pairs={{4,8},{8,4},{12,16},{16,12},{20,24},{24,20},{5,9},{9,5},{13,17},{1... | collective-permute-start | bytes 589832 | tf_op jit(solution)/shard_map/ppermute | solution.py:329
  6.1 0.0 copy-start.3
  6.2 0.7 %copy-done.3 = s32[16,33]{1,0:T(8,128)S(1)} copy-done((s32[16,33]{1,0:T(8,128)S(1)}, s32[16,33]{1,0:T(8,128)}, u32[]{:S(2)}) %copy-start.3) | copy-done | bytes 2136
  6.8 10.5 %local_tiles.1 = (bf16[545,128,128]{2,1,0:T(8,128)(2,1)S(1)}, bf16[16,128,128]{2,1,0:T(8,128)(2,1)S(1)}, f32[16,2048]{1,0:T(8,128)S(1)}) custom-call(s32[16,33]{1,0:T(8,128)S(1)} %copy-done.3, bf16[48,2048]{1,0:T(8,128)(2,1)S(1)} %prep.1.own_ref), custom_call_target="tpu_custom_call" | custom-call | flops 1000000000 | bytes 10000000 | tf_op jit(solution)/shard_map/local_tiles/pallas_call | solution.py:377
  17.4 0.0 collective-permute-done.other_ref.a_ref
  17.4 0.0 copy-start.1
  17.4 0.0 copy-start.2
  17.4 0.0 copy-start.4
  17.4 5.2 %side_tiles.1.tiles_in = bf16[545,128,128]{2,1,0:T(8,128)(2,1)S(1)} custom-call(s32[1]{0:T(128)} %bitcast.before_ref, s32[16,33]{1,0:T(8,128)S(1)} %copy-done.3, bf16[48,2048]{1,0:T(8,128)(2,1)S(1)} %collective-permute-done.other_ref.a_ref, bf16[16,128,128]{2,1,0:T(8,128)(2,1)S(1)} %get-tuple-element.12.right_ref, ...), custom_call_target="tpu_custom_call", output_to_operand_aliasing={{}: (4, {})} | custom-call | flops 1000000000 | bytes 10000000 | tf_op jit(solution)/shard_map/side_tiles/pallas_call | solution.py:377
  22.6 0.0 collective-permute-done.1.b_ref
  22.6 0.0 copy-done.1
  22.6 0.0 copy-done.2
  22.6 0.0 copy-done.4
  22.6 2.3 %image.1 = (bf16[545,128,128]{2,1,0:T(8,128)(2,1)S(1)}, f32[16,2048]{1,0:T(8,128)S(1)}, bf16[16,2048]{1,0:T(8,128)(2,1)S(1)}) custom-call(s32[1]{0:T(128)} %bitcast.before_ref, s32[16,33]{1,0:T(8,128)S(1)} %copy-done.4, bf16[48,2048]{1,0:T(8,128)(2,1)S(1)} %collective-permute-done.other_ref.a_ref, ...), custom_call_target="tpu_custom_call", output_to_operand_aliasing={{0}: (5, {})} | custom-call | flops 1000000000 | bytes 10000000 | tf_op jit(solution)/shard_map/image/pallas_call | solution.py:377
  24.9 0.7 %collective-permute-start.3 = (bf16[16,2048]{1,0:T(8,128)(2,1)S(1)}, bf16[16,2048]{1,0:T(8,128)(2,1)S(1)}, u32[]{:S(2)}, u32[]{:S(2)}) collective-permute-start(bf16[16,2048]{1,0:T(8,128)(2,1)S(1)} %get-tuple-element.15.own_ref), channel_id=1, source_target_pairs={{4,8},{8,4},{12,16},{16,12},{20,24},{24,20},{5,9},{9,5},{13,17},{1... | collective-permute-start | bytes 196616 | tf_op jit(solution)/shard_map/ppermute | solution.py:329
  25.6 8.4 %collective-permute-start.2 = (bf16[16,2048]{1,0:T(8,128)(2,1)S(1)}, bf16[16,2048]{1,0:T(8,128)(2,1)S(1)}, u32[]{:S(2)}, u32[]{:S(2)}) collective-permute-start(bf16[16,2048]{1,0:T(8,128)(2,1)S(1)} %get-tuple-element.15.own_ref), channel_id=1, source_target_pairs={{0,4},{4,0},{8,12},{12,8},{16,20},{20,16},{24,28},{28,24},{1,5},{5... | collective-permute-start | bytes 196616 | tf_op jit(solution)/shard_map/ppermute | solution.py:328
  34.0 1.2 %own_products.1.part_ref = f32[16,2048]{1,0:T(8,128)S(1)} custom-call(bf16[16,2048]{1,0:T(8,128)(2,1)S(1)} %get-tuple-element.15.own_ref, bf16[545,128,128]{2,1,0:T(8,128)(2,1)S(1)} %get-tuple-element.16.tiles_ref), custom_call_target="tpu_custom_call" | custom-call | flops 1000000000 | bytes 10000000 | tf_op jit(solution)/shard_map/own_products/pallas_call | solution.py:377
  35.2 0.0 collective-permute-done.3.b_ref
  35.2 1.0 %collective-permute-done.2.a_ref = bf16[16,2048]{1,0:T(8,128)(2,1)S(1)} collective-permute-done((bf16[16,2048]{1,0:T(8,128)(2,1)S(1)}, bf16[16,2048]{1,0:T(8,128)(2,1)S(1)}, u32[]{:S(2)}, u32[]{:S(2)}) %collective-permute-start.2) | collective-permute-done | bytes 65568 | tf_op jit(solution)/shard_map/ppermute | solution.py:328
  36.2 1.5 %twice.1 = (f32[16,2048]{1,0:T(8,128)S(1)}, bf16[32,2304]{1,0:T(8,128)(2,1)S(1)}, f32[16,128]{1,0:T(8,128)S(1)}) custom-call(s32[1]{0:T(128)} %bitcast.before_ref, bf16[16,2048]{1,0:T(8,128)(2,1)S(1)} %collective-permute-done.2.a_ref, bf16[16,2048]{1,0:T(8,128)(2,1)S(1)} %collective-permute-done.3.b_ref, ...), custom_call_target="tpu_custom_call" | custom-call | flops 1000000000 | bytes 10000000 | tf_op jit(solution)/shard_map/twice/pallas_call | solution.py:377
  37.7 2.9 %collective-permute-start.4 = (bf16[32,2304]{1,0:T(8,128)(2,1)S(1)}, bf16[32,2304]{1,0:T(8,128)(2,1)S(1)}, u32[]{:S(2)}, u32[]{:S(2)}) collective-permute-start(bf16[32,2304]{1,0:T(8,128)(2,1)S(1)} %get-tuple-element.19.own_ref), channel_id=1, source_target_pairs={{0,4},{4,0},{8,12},{12,8},{16,20},{20,16},{24,28},{28,24},{1,5},{5... | collective-permute-start | bytes 442376 | tf_op jit(solution)/shard_map/ppermute | solution.py:328
  40.6 0.7 %collective-permute-start.8 = (bf16[32,2304]{1,0:T(8,128)(2,1)S(1)}, bf16[32,2304]{1,0:T(8,128)(2,1)S(1)}, u32[]{:S(2)}, u32[]{:S(2)}) collective-permute-start(bf16[32,2304]{1,0:T(8,128)(2,1)S(1)} %get-tuple-element.19.own_ref), channel_id=1, source_target_pairs={{4,8},{8,4},{12,16},{16,12},{20,24},{24,20},{5,9},{9,5},{13,17},{1... | collective-permute-start | bytes 442376 | tf_op jit(solution)/shard_map/ppermute | solution.py:329
  41.2 1.5 %own_products_both.1.part_ref = f32[32,2048]{1,0:T(8,128)S(1)} custom-call(bf16[32,2304]{1,0:T(8,128)(2,1)S(1)} %get-tuple-element.19.own_ref, bf16[545,128,128]{2,1,0:T(8,128)(2,1)S(1)} %get-tuple-element.16.tiles_ref), custom_call_target="tpu_custom_call" | custom-call | flops 1000000000 | bytes 10000000 | tf_op jit(solution)/shard_map/own_products_both/pallas_call | solution.py:377
  42.8 3.0 %collective-permute-done.4.a_ref = bf16[32,2304]{1,0:T(8,128)(2,1)S(1)} collective-permute-done((bf16[32,2304]{1,0:T(8,128)(2,1)S(1)}, bf16[32,2304]{1,0:T(8,128)(2,1)S(1)}, u32[]{:S(2)}, u32[]{:S(2)}) %collective-permute-start.4) | collective-permute-done | bytes 147488 | tf_op jit(solution)/shard_map/ppermute | solution.py:328
  45.8 5.3 %collective-permute-start.7 = (f32[16,128]{1,0:T(8,128)S(1)}, f32[16,128]{1,0:T(8,128)S(1)}, u32[]{:S(2)}, u32[]{:S(2)}) collective-permute-start(f32[16,128]{1,0:T(8,128)S(1)} %fusion), channel_id=1, source_target_pairs={{0,24},{4,28},{8,16},{12,20},{16,8},{20,12},{24,0},{28,4},{1,25},{... | collective-permute-start | bytes 24584 | tf_op jit(solution)/shard_map/ppermute | solution.py:345
  51.2 0.0 collective-permute-start.6
  51.2 0.6 %collective-permute-start.5 = (f32[16,128]{1,0:T(8,128)S(1)}, f32[16,128]{1,0:T(8,128)S(1)}, u32[]{:S(2)}, u32[]{:S(2)}) collective-permute-start(f32[16,128]{1,0:T(8,128)S(1)} %fusion), channel_id=1, source_target_pairs={{0,8},{4,12},{8,0},{12,4},{16,24},{20,28},{24,16},{28,20},{1,9},{5... | collective-permute-start | bytes 24584 | tf_op jit(solution)/shard_map/ppermute | solution.py:345
  51.8 0.0 collective-permute-done.8.b_ref
  51.8 1.6 %products.1.prod_ref = f32[32,2048]{1,0:T(8,128)S(1)} custom-call(s32[1]{0:T(128)} %bitcast.before_ref, bf16[32,2304]{1,0:T(8,128)(2,1)S(1)} %collective-permute-done.4.a_ref, bf16[32,2304]{1,0:T(8,128)(2,1)S(1)} %collective-permute-done.8.b_ref, bf16[545,128,128]{2,1,0:T(8,128)(2,1)S(1)} %get-tuple-element.16.tiles_ref, ...), custom_call_target="tpu_custom_call" | custom-call | flops 1000000000 | bytes 10000000 | tf_op jit(solution)/shard_map/products/pallas_call | solution.py:377
  53.4 0.0 collective-permute-done.7
  53.5 2.3 %collective-permute-done.6 = f32[16,128]{1,0:T(8,128)S(1)} collective-permute-done((f32[16,128]{1,0:T(8,128)S(1)}, f32[16,128]{1,0:T(8,128)S(1)}, u32[]{:S(2)}, u32[]{:S(2)}) %collective-permute-start.6) | collective-permute-done | bytes 8224 | tf_op jit(solution)/shard_map/ppermute | solution.py:345
  55.7 0.0 collective-permute-done.5
  55.7 1.2 %update.1 = (f32[16,2048]{1,0:T(8,128)}, f32[16,2048]{1,0:T(8,128)}, f32[16,2048]{1,0:T(8,128)}) custom-call(f32[16,128]{1,0:T(8,128)S(1)} %add_add_fusion.sums_ref, f32[1,2048]{1,0:T(1,128)S(1)} %bitcast.5, f32[16,2048]{1,0:T(8,128)S(1)} %copy-done.1, f32[16,2048]{1,0:T(8,128)S(1)} %get-tuple-element.17.image_ref, ...), custom_call_target="tpu_custom_call" | custom-call | flops 1000000000 | bytes 10000000 | tf_op jit(solution)/shard_map/update/pallas_call | solution.py:377
  (4 shorter events, 0.0 us)
Async XLA Ops:
  0.6 0.9 %copy-start = (f32[16,2048]{1,0:T(8,128)S(1)}, f32[16,2048]{1,0:T(8,128)}, u32[]{:S(2)}) copy-start(f32[16,2048]{1,0:T(8,128)} %vec_ref.7) | copy-start | bytes 393220
  1.5 0.9 %copy-start.5 = (bf16[2048,32]{0,1:T(8,128)(2,1)S(1)}, bf16[2048,32]{0,1:T(8,128)(2,1)}, u32[]{:S(2)}) copy-start(bf16[2048,32]{0,1:T(8,128)(2,1)} %param.4) | copy-start | bytes 393220
  2.5 14.9 %collective-permute-start = (bf16[48,2048]{1,0:T(8,128)(2,1)S(1)}, bf16[48,2048]{1,0:T(8,128)(2,1)S(1)}, u32[]{:S(2)}, u32[]{:S(2)}) collective-permute-start(bf16[48,2048]{1,0:T(8,128)(2,1)S(1)} %prep.1.own_ref), channel_id=1, source_target_pairs={{0,4},{4,0},{8,12},{12,8},{16,20},{20,16},{24,28},{28,24},{1,5},{5... | collective-permute-start | bytes 589832 | tf_op jit(solution)/shard_map/ppermute | solution.py:328
  5.5 17.1 %collective-permute-start.1 = (bf16[48,2048]{1,0:T(8,128)(2,1)S(1)}, bf16[48,2048]{1,0:T(8,128)(2,1)S(1)}, u32[]{:S(2)}, u32[]{:S(2)}) collective-permute-start(bf16[48,2048]{1,0:T(8,128)(2,1)S(1)} %prep.1.own_ref), channel_id=1, source_target_pairs={{4,8},{8,4},{12,16},{16,12},{20,24},{24,20},{5,9},{9,5},{13,17},{1... | collective-permute-start | bytes 589832 | tf_op jit(solution)/shard_map/ppermute | solution.py:329
  6.1 0.7 %copy-start.3 = (s32[16,33]{1,0:T(8,128)S(1)}, s32[16,33]{1,0:T(8,128)}, u32[]{:S(2)}) copy-start(s32[16,33]{1,0:T(8,128)} %pattern_ref.5) | copy-start | bytes 6340
  17.4 5.2 %copy-start.1 = (f32[16,2048]{1,0:T(8,128)S(1)}, f32[16,2048]{1,0:T(8,128)}, u32[]{:S(2)}) copy-start(f32[16,2048]{1,0:T(8,128)} %vec_ref.7) | copy-start | bytes 393220
  17.4 5.2 %copy-start.2 = (f32[2048]{0:T(1024)S(1)}, f32[2048]{0:T(1024)}, u32[]{:S(2)}) copy-start(f32[2048]{0:T(1024)} %param.5) | copy-start | bytes 24580
  17.4 5.2 %copy-start.4 = (s32[16,33]{1,0:T(8,128)S(1)}, s32[16,33]{1,0:T(8,128)}, u32[]{:S(2)}) copy-start(s32[16,33]{1,0:T(8,128)} %pattern_ref.5) | copy-start | bytes 6340
  24.9 10.3 %collective-permute-start.3 = (bf16[16,2048]{1,0:T(8,128)(2,1)S(1)}, bf16[16,2048]{1,0:T(8,128)(2,1)S(1)}, u32[]{:S(2)}, u32[]{:S(2)}) collective-permute-start(bf16[16,2048]{1,0:T(8,128)(2,1)S(1)} %get-tuple-element.15.own_ref), channel_id=1, source_target_pairs={{4,8},{8,4},{12,16},{16,12},{20,24},{24,20},{5,9},{9,5},{13,17},{1... | collective-permute-start | bytes 196616 | tf_op jit(solution)/shard_map/ppermute | solution.py:329
  25.6 10.6 %collective-permute-start.2 = (bf16[16,2048]{1,0:T(8,128)(2,1)S(1)}, bf16[16,2048]{1,0:T(8,128)(2,1)S(1)}, u32[]{:S(2)}, u32[]{:S(2)}) collective-permute-start(bf16[16,2048]{1,0:T(8,128)(2,1)S(1)} %get-tuple-element.15.own_ref), channel_id=1, source_target_pairs={{0,4},{4,0},{8,12},{12,8},{16,20},{20,16},{24,28},{28,24},{1,5},{5... | collective-permute-start | bytes 196616 | tf_op jit(solution)/shard_map/ppermute | solution.py:328
  37.7 8.1 %collective-permute-start.4 = (bf16[32,2304]{1,0:T(8,128)(2,1)S(1)}, bf16[32,2304]{1,0:T(8,128)(2,1)S(1)}, u32[]{:S(2)}, u32[]{:S(2)}) collective-permute-start(bf16[32,2304]{1,0:T(8,128)(2,1)S(1)} %get-tuple-element.19.own_ref), channel_id=1, source_target_pairs={{0,4},{4,0},{8,12},{12,8},{16,20},{20,16},{24,28},{28,24},{1,5},{5... | collective-permute-start | bytes 442376 | tf_op jit(solution)/shard_map/ppermute | solution.py:328
  40.6 11.2 %collective-permute-start.8 = (bf16[32,2304]{1,0:T(8,128)(2,1)S(1)}, bf16[32,2304]{1,0:T(8,128)(2,1)S(1)}, u32[]{:S(2)}, u32[]{:S(2)}) collective-permute-start(bf16[32,2304]{1,0:T(8,128)(2,1)S(1)} %get-tuple-element.19.own_ref), channel_id=1, source_target_pairs={{4,8},{8,4},{12,16},{16,12},{20,24},{24,20},{5,9},{9,5},{13,17},{1... | collective-permute-start | bytes 442376 | tf_op jit(solution)/shard_map/ppermute | solution.py:329
  45.8 7.6 %collective-permute-start.7 = (f32[16,128]{1,0:T(8,128)S(1)}, f32[16,128]{1,0:T(8,128)S(1)}, u32[]{:S(2)}, u32[]{:S(2)}) collective-permute-start(f32[16,128]{1,0:T(8,128)S(1)} %fusion), channel_id=1, source_target_pairs={{0,24},{4,28},{8,16},{12,20},{16,8},{20,12},{24,0},{28,4},{1,25},{... | collective-permute-start | bytes 24584 | tf_op jit(solution)/shard_map/ppermute | solution.py:345
  51.2 4.5 %collective-permute-start.6 = (f32[16,128]{1,0:T(8,128)S(1)}, f32[16,128]{1,0:T(8,128)S(1)}, u32[]{:S(2)}, u32[]{:S(2)}) collective-permute-start(f32[16,128]{1,0:T(8,128)S(1)} %fusion), channel_id=1, source_target_pairs={{0,16},{4,20},{8,24},{12,28},{16,0},{20,4},{24,8},{28,12},{1,17},{... | collective-permute-start | bytes 24584 | tf_op jit(solution)/shard_map/ppermute | solution.py:345
  51.2 4.5 %collective-permute-start.5 = (f32[16,128]{1,0:T(8,128)S(1)}, f32[16,128]{1,0:T(8,128)S(1)}, u32[]{:S(2)}, u32[]{:S(2)}) collective-permute-start(f32[16,128]{1,0:T(8,128)S(1)} %fusion), channel_id=1, source_target_pairs={{0,8},{4,12},{8,0},{12,4},{16,24},{20,28},{24,16},{28,20},{1,9},{5... | collective-permute-start | bytes 24584 | tf_op jit(solution)/shard_map/ppermute | solution.py:345

commit v4 on v3

v4 whole, which is shorter than its diff:
```python
import functools

import jax
import jax.numpy as jnp
from jax import lax
from jax.experimental import pallas as pl
from jax.experimental.pallas import tpu as pltpu
from jax.sharding import PartitionSpec as P

F = 32
BLK = 128
REACH = 16
WEXP = 18
LANES = 128
GAMMA = float(WEXP) ** (1.0 / (WEXP + 1))
GAMMA_SQ = GAMMA * GAMMA
OFFSET = GAMMA * (WEXP + 1) / WEXP
TINY = 1e-30
SCALE = 1.0 / (4 * BLK)
SHIFT = 2.0 / (0.5 + 0.6)
SUMS = 9
STEPS = (32, 16, 8)
FIELD = 10
MIB = 1 << 20

f32 = jnp.float32
bf16 = jnp.bfloat16


def rounded(x):
    return x.astype(bf16).astype(f32)


def three_parts(x):
    high = rounded(x)
    rest = x - high
    middle = rounded(rest)
    return high, middle, rounded(rest - middle)


def eight_rows(rows):
    row = lax.broadcasted_iota(jnp.int32, (8, rows[0].shape[1]), 0)
    out = jnp.zeros((8, rows[0].shape[1]), f32)
    for at, value in enumerate(rows):
        out = jnp.where(row == at, value, out)
    return out


def fill_features(points, left_ref, first, right_ref=None):
    x = points.astype(f32)
    count = x.shape[1]
    squares = three_parts(GAMMA_SQ * jnp.sum(x * x, axis=0, keepdims=True))
    ones = [jnp.ones((1, count), f32)] * 3
    blank = jnp.zeros((LANES - 3 * F - 8, count), f32)
    left = jnp.concatenate([x, x, x, eight_rows(list(squares) + ones), blank], axis=0).astype(bf16)
    for b in range(count // BLK):
        left_ref[first + b] = left[:, b * BLK : (b + 1) * BLK].T
    if right_ref is not None:
        cross = three_parts((-2.0 * GAMMA_SQ) * x)
        right = jnp.concatenate(list(cross) + [eight_rows(ones + list(squares)), blank], axis=0).astype(bf16)
        for b in range(count // BLK):
            right_ref[b] = right[:, b * BLK : (b + 1) * BLK]


def tile_values(left, right):
    scaled = jnp.dot(left, right, preferred_element_type=f32)
    scaled = jnp.maximum(scaled, TINY)
    s = jnp.maximum(GAMMA - scaled * lax.rsqrt(scaled), 0.0)
    s2 = s * s
    s4 = s2 * s2
    s8 = s4 * s4
    s16 = s8 * s8
    return ((s16 * s2) * (OFFSET - s)).astype(bf16)


def entry(slot, mirror, other, home):
    return (((((home << 5) + other) << FIELD) + mirror) << FIELD) + slot


def make_tiles(count, list_ref, left_ref, right_ref, tiles_ref, mirrored):
    mask = (1 << FIELD) - 1

    def one(at):
        code = list_ref[at]
        home = code >> (2 * FIELD + 5)
        other = (code >> (2 * FIELD)) & 31
        tile = tile_values(left_ref[other], right_ref[home])
        if mirrored:
            tiles_ref[(code >> FIELD) & mask] = tile.T
        tiles_ref[code & mask] = tile

    done = jnp.int32(0)
    for size in STEPS:

        def step(at, carry, size=size, done=done):
            for k in range(size):
                one(done + at * size + k)
            return carry

        last = size == STEPS[-1]
        steps = (count - done + (size - 1 if last else 0)) // size
        lax.fori_loop(0, steps, step, 0)
        done = done + steps * size


def local_slot(blocks, home, other):
    return ((home // 2) * blocks + other) * 2 + home % 2


def side_slot(blocks, home, other, after):
    wide = other - 2 * (home // 2) + (blocks if after else 0)
    return blocks * blocks + ((home // 2) * (blocks + 2) + wide) * 2 + home % 2


def spare_slot(blocks):
    return 2 * blocks * (blocks + 1)


def local_entries(blocks):
    return [(a, b, REACH + b - a) for a in range(blocks) for b in range(a, blocks)]


def side_entries(blocks, after):
    if after:
        return [(a, b, 2 * REACH + b - a) for a in range(blocks) for b in range(a + 1)]
    return [(a, b, b - a) for a in range(blocks) for b in range(a, blocks)]


def pad_list(count, list_ref, spare):
    for k in range(STEPS[-1] - 1):
        list_ref[count + k] = jnp.int32(entry(spare, spare, 0, 0))


def clear_tiles(count, list_ref, tiles_ref):
    mask = (1 << FIELD) - 1

    def step(at, carry):
        code = list_ref[at]
        tiles_ref[code & mask] = jnp.zeros((BLK, BLK), bf16)
        tiles_ref[(code >> FIELD) & mask] = jnp.zeros((BLK, BLK), bf16)
        return carry

    lax.fori_loop(0, count, step, 0)


def products(vec, tiles_ref, first, wide):
    tiles = tiles_ref[first : first + 2 * wide].reshape(wide, 2, BLK, BLK)
    tiles = jnp.concatenate([tiles[:, 0].reshape(wide * BLK, BLK), tiles[:, 1].reshape(wide * BLK, BLK)], axis=1)
    return jnp.dot(vec, tiles, preferred_element_type=f32)


def pair_cols(pair):
    return slice(pair * 2 * BLK, (pair + 1) * 2 * BLK)


def local_products(blocks, vec, tiles_ref, out_ref):
    for pair in range(blocks // 2):
        out_ref[:, pair_cols(pair)] = products(vec, tiles_ref, pair * 2 * blocks, blocks)


def gather_sides(blocks, before, side_a, side_b, wide_ref):
    size = blocks * BLK
    at_a = pl.multiple_of(jnp.where(before == 1, 0, size), size)
    at_b = pl.multiple_of(size - at_a, size)
    wide_ref[:, pl.ds(at_a, size)] = side_a
    wide_ref[:, pl.ds(at_b, size)] = side_b


def side_products(blocks, pair, wide_ref, tiles_ref):
    vec = wide_ref[:, pair * 2 * BLK : (pair * 2 + blocks + 2) * BLK]
    return products(vec, tiles_ref, blocks * blocks + pair * 2 * (blocks + 2), blocks + 2)


def odd_place():
    return lax.rem(lax.axis_index("pts"), 2)


def prep_kernel(points_ref, vec_ref, out_ref, wide_ref, sems):
    points_copy = pltpu.make_async_copy(points_ref, out_ref.at[:F], sems.at[0])
    vec_copy = pltpu.make_async_copy(vec_ref, wide_ref, sems.at[1])
    vec_copy.start()
    points_copy.start()
    vec_copy.wait()
    out_ref[F:, :] = wide_ref[...].astype(bf16)
    points_copy.wait()


def local_kernel(
    blocks, pattern_ref, own_ref, tiles_ref, right_ref, part_ref, left_ref, listed_ref, list_ref, dead_ref, sem
):
    pattern_copy = pltpu.make_async_copy(pattern_ref, listed_ref, sem)
    pattern_copy.start()
    fill_features(own_ref[:F, :], left_ref, 0, right_ref)
    first = blocks * blocks
    for pair in range(blocks // 2):

        def clear(at, carry, start=first + pair * 2 * (blocks + 2)):
            tiles_ref[pl.ds(start + at * 4, 4)] = jnp.zeros((4, BLK, BLK), bf16)
            return carry

        lax.fori_loop(0, (blocks + 2) // 2, clear, 0)
    pattern_copy.wait()
    dead = jnp.int32(0)
    count = jnp.int32(0)
    for home, other, column in local_entries(blocks):
        code = jnp.int32(entry(local_slot(blocks, home, other), local_slot(blocks, other, home), other, home))
        live = listed_ref[home, column]
        dead_ref[dead] = code
        list_ref[count] = code
        dead = dead + (1 - live)
        count = count + live
    pad_list(count, list_ref, spare_slot(blocks))
    clear_tiles(dead, dead_ref, tiles_ref)
    make_tiles(count, list_ref, left_ref, right_ref, tiles_ref, True)
    local_products(blocks, own_ref[F:, :], tiles_ref, part_ref)


def first_kernel(
    blocks, pattern_ref, a_ref, b_ref, right_ref, tiles_in, part_ref, noise_ref, vec_ref,
    tiles_ref, image_ref, low_ref, left_ref, wide_ref, listed_ref, list_ref, sem,
):
    del tiles_in
    pattern_copy = pltpu.make_async_copy(pattern_ref, listed_ref, sem)
    pattern_copy.start()
    before = odd_place()
    fill_features(a_ref[:F, :], left_ref, (1 - before) * blocks)
    fill_features(b_ref[:F, :], left_ref, before * blocks)
    gather_sides(blocks, before, a_ref[F:, :], b_ref[F:, :], wide_ref)
    pattern_copy.wait()
    count = jnp.int32(0)
    for after in (False, True):
        for home, other, column in side_entries(blocks, after):
            slot = side_slot(blocks, home, other, after)
            list_ref[count] = jnp.int32(entry(slot, 0, other + (blocks if after else 0), home))
            count = count + listed_ref[home, column]
    pad_list(count, list_ref, spare_slot(blocks))
    make_tiles(count, list_ref, left_ref, right_ref, tiles_ref, False)
    for pair in range(blocks // 2):
        cols = pair_cols(pair)
        total = part_ref[:, cols] + side_products(blocks, pair, wide_ref, tiles_ref)
        image = noise_ref[:, cols] * vec_ref[:, cols] + total * SCALE
        image_ref[:, cols] = image
        low_ref[:, cols] = image.astype(bf16)


def own_kernel(blocks, own_ref, tiles_ref, part_ref):
    local_products(blocks, own_ref[...], tiles_ref, part_ref)


def second_kernel(
    blocks, a_ref, b_ref, tiles_ref, part_ref, noise_ref, vec_ref, image_ref,
    twice_ref, low_ref, sums_ref, wide_ref,
):
    width = vec_ref.shape[0]
    gather_sides(blocks, odd_place(), a_ref[...], b_ref[...], wide_ref)
    totals = [jnp.zeros((width, LANES), f32) for _ in range(SUMS)]
    for pair in range(blocks // 2):
        cols = pair_cols(pair)
        r = vec_ref[:, cols]
        w = image_ref[:, cols]
        q = noise_ref[:, cols] * w + (part_ref[:, cols] + side_products(blocks, pair, wide_ref, tiles_ref)) * SCALE
        twice_ref[:, cols] = q
        u = r - SHIFT * w
        y = w - SHIFT * q
        low_ref[:width, cols] = y.astype(bf16)
        low_ref[width:, cols] = q.astype(bf16)
        terms = (r * r, r * w, u * u, u * w, w * w, y * u, q * u, y * w, q * w)
        totals = [total + (term[:, :LANES] + term[:, LANES:]) for total, term in zip(totals, terms)]
    lane = lax.broadcasted_iota(jnp.int32, (width, LANES), 1)
    out = jnp.zeros((width, LANES), f32)
    for at, total in enumerate(totals):
        out = jnp.where(lane == at, jnp.sum(total, axis=1, keepdims=True), out)
    sums_ref[...] = out


def third_kernel(blocks, a_ref, b_ref, tiles_ref, part_ref, out_ref, wide_ref):
    gather_sides(blocks, odd_place(), a_ref[...], b_ref[...], wide_ref)
    for pair in range(blocks // 2):
        cols = pair_cols(pair)
        out_ref[:, cols] = (part_ref[:, cols] + side_products(blocks, pair, wide_ref, tiles_ref)) * SCALE


def last_kernel(sums_ref, noise_ref, vec_ref, image_ref, twice_ref, prod_ref, x_ref, r_ref, w_ref):
    width = vec_ref.shape[0]
    rr, rw, uu, uw, ww, yu, qu, yw, qw = [sums_ref[:, at : at + 1] for at in range(SUMS)]
    alpha0 = rr / rw
    delta = alpha0 - SHIFT
    norm = uu - 2.0 * delta * uw + delta * delta * ww
    curv = yu - delta * (qu + yw) + delta * delta * qw
    beta = norm / rr
    alpha1 = norm / (curv - beta * norm / alpha0)
    r0, w0, q0 = vec_ref[...], image_ref[...], twice_ref[...]
    r1 = r0 - alpha0 * w0
    w1 = w0 - alpha0 * q0
    q1 = noise_ref[...] * w1 + (prod_ref[:width, :] - delta * prod_ref[width:, :])
    x_ref[...] = alpha0 * r0 + alpha1 * (r1 + beta * r0)
    r_ref[...] = r1 - alpha1 * (w1 + beta * w0)
    w_ref[...] = w1 - alpha1 * (q1 + beta * q0)


def swap_pairs(count, first):
    pairs = []
    for low in range(first, count - 1, 2):
        pairs += [(low, low + 1), (low + 1, low)]
    return pairs


def both_sides(x):
    count = lax.axis_size("pts")
    return (
        lax.ppermute(x, "pts", swap_pairs(count, 0)),
        lax.ppermute(x, "pts", swap_pairs(count, 1)),
    )


def total_over_points(x):
    count = lax.axis_size("pts")
    if count & (count - 1):
        return lax.psum(x, "pts")
    step = count
    while step > 1:
        size = 4 if step > 4 else 2
        step //= size
        x = x + sum(
            lax.ppermute(x, "pts", [(i, i ^ (k * step)) for i in range(count)]) for k in range(1, size)
        )
    return x


VM = pl.BlockSpec(memory_space=pltpu.VMEM)
FAR = pl.BlockSpec(memory_space=pltpu.HBM)


def per_device(points, noise_var, right_side, pattern):
    local_rows = points.shape[0]
    width = right_side.shape[0]
    blocks = local_rows // BLK
    assert blocks == REACH
    params = pltpu.CompilerParams(vmem_limit_bytes=12 * MIB)
    full = (width, local_rows)
    tiles_type = pltpu.VMEM((spare_slot(blocks) + 1, BLK, BLK), bf16)
    pairs = blocks * (blocks + 1) // 2
    listed = pltpu.SMEM(pattern.shape, jnp.int32)
    copied = pltpu.SemaphoreType.DMA(())

    def left(count):
        return pltpu.VMEM((count * blocks, BLK, LANES), bf16)

    def numbers(count):
        return pltpu.SMEM((count + STEPS[-1],), jnp.int32)

    def wide(rows):
        return pltpu.VMEM((rows, 2 * local_rows), bf16)

    def call(kernel, name, ins, outs, scratch=(), aliases=None, far=0):
        return pl.pallas_call(
            kernel,
            out_shape=outs,
            in_specs=[FAR] * far + [VM] * (len(ins) - far),
            out_specs=jax.tree.map(lambda _: VM, outs, is_leaf=lambda x: hasattr(x, "dtype")),
            scratch_shapes=list(scratch),
            input_output_aliases=aliases or {},
            compiler_params=params,
            cost_estimate=pl.CostEstimate(flops=10**9, bytes_accessed=10**7, transcendentals=0),
            name=name,
        )(*[pltpu.with_memory_space_constraint(x, pltpu.HBM) for x in ins[:far]], *[pltpu.with_memory_space_constraint(x, pltpu.VMEM) for x in ins[far:]])

    noise = noise_var[None, :]
    payload = call(
        prep_kernel,
        "prep",
        (points.T, right_side),
        pltpu.VMEM((F + width, local_rows), bf16),
        (pltpu.VMEM(full, f32), pltpu.SemaphoreType.DMA((2,))),
        far=2,
    )
    halo_a, halo_b = both_sides(payload)
    tiles, right, part = call(
        functools.partial(local_kernel, blocks),
        "local_tiles",
        (pattern, payload),
        (tiles_type, pltpu.VMEM((blocks, LANES, BLK), bf16), pltpu.VMEM(full, f32)),
        (left(1), listed, numbers(pairs), numbers(pairs), copied),
        far=1,
    )
    tiles, image, low = call(
        functools.partial(first_kernel, blocks),
        "image",
        (pattern, halo_a, halo_b, right, tiles, part, noise, right_side),
        (tiles_type, pltpu.VMEM(full, f32), pltpu.VMEM(full, bf16)),
        (left(2), wide(width), listed, numbers(2 * pairs), copied),
        {4: 0},
        far=1,
    )
    low_a, low_b = both_sides(low)
    part = call(
        functools.partial(own_kernel, blocks), "own_products", (low, tiles), pltpu.VMEM(full, f32)
    )
    twice, low, sums = call(
        functools.partial(second_kernel, blocks),
        "twice",
        (low_a, low_b, tiles, part, noise, right_side, image),
        (
            pltpu.VMEM(full, f32),
            pltpu.VMEM((2 * width, local_rows), bf16),
            pltpu.VMEM((width, LANES), f32),
        ),
        (wide(width),),
    )
    low_a, low_b = both_sides(low)
    sums = total_over_points(sums)
    both = pltpu.VMEM((2 * width, local_rows), f32)
    part = call(functools.partial(own_kernel, blocks), "own_products_both", (low, tiles), both)
    prods = call(
        functools.partial(third_kernel, blocks),
        "products",
        (low_a, low_b, tiles, part),
        both,
        (wide(2 * width),),
    )
    out = jax.ShapeDtypeStruct(full, f32)
    return call(last_kernel, "update", (sums, noise, right_side, image, twice, prods), (out, out, out))


def solution(mesh):
    placed = (P("pts", None), P("pts"), P("rhs", "pts"), P("pts", None))
    return jax.shard_map(
        per_device,
        mesh=mesh,
        in_specs=placed,
        out_specs=(P("rhs", "pts"), P("rhs", "pts"), P("rhs", "pts")),
        check_vma=False,
    )
```

time: 57.1 us -> 51.6 us (0.904)
  Pallas kernels: 25 us -> 17.9 us
  starting transfers between devices: 22.2 us -> 26.2 us
  waiting for transfers between devices: 6.36 us -> 4.84 us
  local copies, waits for them, and re-layouts: 2.51 us -> 1.6 us
    pallas_call x9 -> x8, Pallas kernels: 25 us -> 17.9 us  [call(): pl.pallas_call(kernel, out_shape=outs, in_specs=[FAR] * far + [VM] * (len...]
    ppermute x3, starting transfers between devices: 14.3 us -> 19.5 us  [both_sides(): lax.ppermute(x, 'pts', swap_pairs(count, 0))]
    ppermute x3, waiting for transfers between devices: 4.09 us -> 2.48 us  [both_sides(): lax.ppermute(x, 'pts', swap_pairs(count, 0))]
    ppermute x3 -> x4, starting transfers between devices: 5.99 us -> 4.51 us  [total_over_points(): lax.ppermute(x, 'pts', [(i, i ^ k * step) for i in range(count)])]
    unnamed x12 -> x4, local copies, waits for them, and re-layouts: 2.51 us -> 1.6 us
    ppermute x3 -> x4, waiting for transfers between devices: 2.26 us -> 2.35 us  [total_over_points(): lax.ppermute(x, 'pts', [(i, i ^ k * step) for i in range(count)])]
  transfers between devices with their start and end apart: 9 -> 10, of which waited for: 3 -> 3; matrix products, arithmetic and copies ran while one was open for 0% -> 0% of each run, Pallas kernels for 35% -> 17%
where the time goes in v4:
time: 51.6 us; the launch traced here: 51.3 us
  starting transfers between devices  26.2 us (51%)
  Pallas kernels  17.9 us (35%)
  waiting for transfers between devices  4.84 us (9%)
  local copies, waits for them, and re-layouts  1.6 us (3%)
  between operations  0.72 us (1%)
    ppermute x3, starting transfers between devices, both_sides(): lax.ppermute(x, 'pts', swap_pairs(count, 0))  19.5 us
    pallas_call x8, Pallas kernels, call(): pl.pallas_call(kernel, out_shape=outs, in_specs=[FAR] * far + [VM] * (len...  17.9 us
    ppermute x4, starting transfers between devices, total_over_points(): lax.ppermute(x, 'pts', [(i, i ^ k * step) for i in range(count)])  4.51 us
    ppermute x3, waiting for transfers between devices, both_sides(): lax.ppermute(x, 'pts', swap_pairs(count, 0))  2.48 us
    ppermute x4, waiting for transfers between devices, total_over_points(): lax.ppermute(x, 'pts', [(i, i ^ k * step) for i in range(count)])  2.35 us
    ppermute x3, starting transfers between devices, both_sides(): lax.ppermute(x, 'pts', swap_pairs(count, 1))  2.18 us
    unnamed x4, local copies, waits for them, and re-layouts  1.6 us
  transfers between devices with their start and end apart: 10, of which 3 were waited for; matrix products, arithmetic and copies ran while one was open for 0% of the time, Pallas kernels for 17%

profile of v4, /device:TPU:0, one launch (start us, length us, event | category | flops | bytes accessed | tf_op | source)
XLA Modules:
  0.0 51.3 jit_solution(9825111313069645950)
XLA Ops:
  0.6 1.0 %prep.1.own_ref = bf16[48,2048]{1,0:T(8,128)(2,1)S(1)} custom-call(bf16[32,2048]{1,0:T(8,128)(2,1)} %bitcast.5, f32[16,2048]{1,0:T(8,128)} %vec_ref.7), custom_call_target="tpu_custom_call" | custom-call | flops 1000000000 | bytes 10000000 | tf_op jit(solution)/shard_map/prep/pallas_call | solution.py:356
  1.6 0.7 %collective-permute-start.1 = (bf16[48,2048]{1,0:T(8,128)(2,1)S(1)}, bf16[48,2048]{1,0:T(8,128)(2,1)S(1)}, u32[]{:S(2)}, u32[]{:S(2)}) collective-permute-start(bf16[48,2048]{1,0:T(8,128)(2,1)S(1)} %prep.1.own_ref), channel_id=1, source_target_pairs={{4,8},{8,4},{12,16},{16,12},{20,24},{24,20},{5,9},{9,5},{13,17},{1... | collective-permute-start | bytes 589832 | tf_op jit(solution)/shard_map/ppermute | solution.py:312
  2.3 5.8 %collective-permute-start = (bf16[48,2048]{1,0:T(8,128)(2,1)S(1)}, bf16[48,2048]{1,0:T(8,128)(2,1)S(1)}, u32[]{:S(2)}, u32[]{:S(2)}) collective-permute-start(bf16[48,2048]{1,0:T(8,128)(2,1)S(1)} %prep.1.own_ref), channel_id=1, source_target_pairs={{0,4},{4,0},{8,12},{12,8},{16,20},{20,16},{24,28},{28,24},{1,5},{5... | collective-permute-start | bytes 589832 | tf_op jit(solution)/shard_map/ppermute | solution.py:311
  8.1 6.2 %local_tiles.1 = (bf16[545,128,128]{2,1,0:T(8,128)(2,1)S(1)}, bf16[16,128,128]{2,1,0:T(8,128)(2,1)S(1)}, f32[16,2048]{1,0:T(8,128)S(1)}) custom-call(s32[16,33]{1,0:T(8,128)} %pattern_ref.3, bf16[48,2048]{1,0:T(8,128)(2,1)S(1)} %prep.1.own_ref), custom_call_target="tpu_custom_call" | custom-call | flops 1000000000 | bytes 10000000 | tf_op jit(solution)/shard_map/local_tiles/pallas_call | solution.py:356
  14.3 0.0 collective-permute-done.1.b_ref
  14.3 1.4 %collective-permute-done.a_ref = bf16[48,2048]{1,0:T(8,128)(2,1)S(1)} collective-permute-done((bf16[48,2048]{1,0:T(8,128)(2,1)S(1)}, bf16[48,2048]{1,0:T(8,128)(2,1)S(1)}, u32[]{:S(2)}, u32[]{:S(2)}) %collective-permute-start) | collective-permute-done | bytes 196640 | tf_op jit(solution)/shard_map/ppermute | solution.py:311
  15.7 0.0 copy-start
  15.7 0.9 %copy-done = f32[16,2048]{1,0:T(8,128)S(1)} copy-done((f32[16,2048]{1,0:T(8,128)S(1)}, f32[16,2048]{1,0:T(8,128)}, u32[]{:S(2)}) %copy-start) | copy-done | bytes 131096
  16.6 0.0 copy-start.1
  16.6 0.7 %copy-done.1 = f32[2048]{0:T(1024)S(1)} copy-done((f32[2048]{0:T(1024)S(1)}, f32[2048]{0:T(1024)}, u32[]{:S(2)}) %copy-start.1) | copy-done | bytes 8216
  17.3 3.8 %image.1 = (bf16[545,128,128]{2,1,0:T(8,128)(2,1)S(1)}, f32[16,2048]{1,0:T(8,128)S(1)}, bf16[16,2048]{1,0:T(8,128)(2,1)S(1)}) custom-call(s32[16,33]{1,0:T(8,128)} %pattern_ref.3, bf16[48,2048]{1,0:T(8,128)(2,1)S(1)} %collective-permute-done.a_ref, bf16[48,2048]{1,0:T(8,128)(2,1)S(1)} %collective-permute-done.1.b_ref, ...), custom_call_target="tpu_custom_call", output_to_operand_aliasing={{0}: (4, {})} | custom-call | flops 1000000000 | bytes 10000000 | tf_op jit(solution)/shard_map/image/pallas_call | solution.py:356
  21.1 0.7 %collective-permute-start.3 = (bf16[16,2048]{1,0:T(8,128)(2,1)S(1)}, bf16[16,2048]{1,0:T(8,128)(2,1)S(1)}, u32[]{:S(2)}, u32[]{:S(2)}) collective-permute-start(bf16[16,2048]{1,0:T(8,128)(2,1)S(1)} %get-tuple-element.15.own_ref), channel_id=1, source_target_pairs={{4,8},{8,4},{12,16},{16,12},{20,24},{24,20},{5,9},{9,5},{13,17},{1... | collective-permute-start | bytes 196616 | tf_op jit(solution)/shard_map/ppermute | solution.py:312
  21.8 10.1 %collective-permute-start.2 = (bf16[16,2048]{1,0:T(8,128)(2,1)S(1)}, bf16[16,2048]{1,0:T(8,128)(2,1)S(1)}, u32[]{:S(2)}, u32[]{:S(2)}) collective-permute-start(bf16[16,2048]{1,0:T(8,128)(2,1)S(1)} %get-tuple-element.15.own_ref), channel_id=1, source_target_pairs={{0,4},{4,0},{8,12},{12,8},{16,20},{20,16},{24,28},{28,24},{1,5},{5... | collective-permute-start | bytes 196616 | tf_op jit(solution)/shard_map/ppermute | solution.py:311
  31.9 1.2 %own_products.1.part_ref = f32[16,2048]{1,0:T(8,128)S(1)} custom-call(bf16[16,2048]{1,0:T(8,128)(2,1)S(1)} %get-tuple-element.15.own_ref, bf16[545,128,128]{2,1,0:T(8,128)(2,1)S(1)} %get-tuple-element.16.tiles_ref), custom_call_target="tpu_custom_call" | custom-call | flops 1000000000 | bytes 10000000 | tf_op jit(solution)/shard_map/own_products/pallas_call | solution.py:356
  33.1 0.0 collective-permute-done.3.b_ref
  33.1 1.0 %collective-permute-done.2.a_ref = bf16[16,2048]{1,0:T(8,128)(2,1)S(1)} collective-permute-done((bf16[16,2048]{1,0:T(8,128)(2,1)S(1)}, bf16[16,2048]{1,0:T(8,128)(2,1)S(1)}, u32[]{:S(2)}, u32[]{:S(2)}) %collective-permute-start.2) | collective-permute-done | bytes 65568 | tf_op jit(solution)/shard_map/ppermute | solution.py:311
  34.1 1.4 %twice.1 = (f32[16,2048]{1,0:T(8,128)S(1)}, bf16[32,2048]{1,0:T(8,128)(2,1)S(1)}, f32[16,128]{1,0:T(8,128)S(1)}) custom-call(bf16[16,2048]{1,0:T(8,128)(2,1)S(1)} %collective-permute-done.2.a_ref, bf16[16,2048]{1,0:T(8,128)(2,1)S(1)} %collective-permute-done.3.b_ref, bf16[545,128,128]{2,1,0:T(8,128)(2,1)S(1)} %get-tuple-element.16.tiles_ref, ...), custom_call_target="tpu_custom_call" | custom-call | flops 1000000000 | bytes 10000000 | tf_op jit(solution)/shard_map/twice/pallas_call | solution.py:356
  35.5 2.4 %collective-permute-start.6 = (f32[16,128]{1,0:T(8,128)S(1)}, f32[16,128]{1,0:T(8,128)S(1)}, u32[]{:S(2)}, u32[]{:S(2)}) collective-permute-start(f32[16,128]{1,0:T(8,128)S(1)} %get-tuple-element.18), channel_id=1, source_target_pairs={{0,24},{4,28},{8,16},{12,20},{16,8},{20,12},{24,0},{28,4},{1,25},{... | collective-permute-start | bytes 24584 | tf_op jit(solution)/shard_map/ppermute | solution.py:325
  38.0 0.9 %collective-permute-start.5 = (f32[16,128]{1,0:T(8,128)S(1)}, f32[16,128]{1,0:T(8,128)S(1)}, u32[]{:S(2)}, u32[]{:S(2)}) collective-permute-start(f32[16,128]{1,0:T(8,128)S(1)} %get-tuple-element.18), channel_id=1, source_target_pairs={{0,16},{4,20},{8,24},{12,28},{16,0},{20,4},{24,8},{28,12},{1,17},{... | collective-permute-start | bytes 24584 | tf_op jit(solution)/shard_map/ppermute | solution.py:325
  38.9 1.1 %collective-permute-start.4 = (f32[16,128]{1,0:T(8,128)S(1)}, f32[16,128]{1,0:T(8,128)S(1)}, u32[]{:S(2)}, u32[]{:S(2)}) collective-permute-start(f32[16,128]{1,0:T(8,128)S(1)} %get-tuple-element.18), channel_id=1, source_target_pairs={{0,8},{4,12},{8,0},{12,4},{16,24},{20,28},{24,16},{28,20},{1,9},{5... | collective-permute-start | bytes 24584 | tf_op jit(solution)/shard_map/ppermute | solution.py:325
  40.0 0.8 %collective-permute-start.9 = (bf16[32,2048]{1,0:T(8,128)(2,1)S(1)}, bf16[32,2048]{1,0:T(8,128)(2,1)S(1)}, u32[]{:S(2)}, u32[]{:S(2)}) collective-permute-start(bf16[32,2048]{1,0:T(8,128)(2,1)S(1)} %get-tuple-element.20.own_ref), channel_id=1, source_target_pairs={{4,8},{8,4},{12,16},{16,12},{20,24},{24,20},{5,9},{9,5},{13,17},{1... | collective-permute-start | bytes 393224 | tf_op jit(solution)/shard_map/ppermute | solution.py:312
  40.8 3.7 %collective-permute-start.8 = (bf16[32,2048]{1,0:T(8,128)(2,1)S(1)}, bf16[32,2048]{1,0:T(8,128)(2,1)S(1)}, u32[]{:S(2)}, u32[]{:S(2)}) collective-permute-start(bf16[32,2048]{1,0:T(8,128)(2,1)S(1)} %get-tuple-element.20.own_ref), channel_id=1, source_target_pairs={{0,4},{4,0},{8,12},{12,8},{16,20},{20,16},{24,28},{28,24},{1,5},{5... | collective-permute-start | bytes 393224 | tf_op jit(solution)/shard_map/ppermute | solution.py:311
  44.5 0.0 collective-permute-done.6
  44.5 0.0 collective-permute-done.5
  44.5 0.0 collective-permute-done.4
  44.5 0.1 collective-permute-start.7
  44.6 1.5 %own_products_both.1.part_ref = f32[32,2048]{1,0:T(8,128)S(1)} custom-call(bf16[32,2048]{1,0:T(8,128)(2,1)S(1)} %get-tuple-element.20.own_ref, bf16[545,128,128]{2,1,0:T(8,128)(2,1)S(1)} %get-tuple-element.16.tiles_ref), custom_call_target="tpu_custom_call" | custom-call | flops 1000000000 | bytes 10000000 | tf_op jit(solution)/shard_map/own_products_both/pallas_call | solution.py:356
  46.1 2.3 %collective-permute-done.7 = f32[16,128]{1,0:T(8,128)S(1)} collective-permute-done((f32[16,128]{1,0:T(8,128)S(1)}, f32[16,128]{1,0:T(8,128)S(1)}, u32[]{:S(2)}, u32[]{:S(2)}) %collective-permute-start.7) | collective-permute-done | bytes 8224 | tf_op jit(solution)/shard_map/ppermute | solution.py:325
  48.5 0.0 collective-permute-done.9.b_ref
  48.5 0.0 collective-permute-done.8.a_ref
  48.5 1.6 %products.1.prod_ref = f32[32,2048]{1,0:T(8,128)S(1)} custom-call(bf16[32,2048]{1,0:T(8,128)(2,1)S(1)} %collective-permute-done.8.a_ref, bf16[32,2048]{1,0:T(8,128)(2,1)S(1)} %collective-permute-done.9.b_ref, bf16[545,128,128]{2,1,0:T(8,128)(2,1)S(1)} %get-tuple-element.16.tiles_ref, f32[32,2048]{1,0:T(8,128)S(1)} %own_products_both.1.part_ref), custom_call_target="tpu_custom_call" | custom-call | flops 1000000000 | bytes 10000000 | tf_op jit(solution)/shard_map/products/pallas_call | solution.py:356
  50.1 1.2 %update.1 = (f32[16,2048]{1,0:T(8,128)}, f32[16,2048]{1,0:T(8,128)}, f32[16,2048]{1,0:T(8,128)}) custom-call(f32[16,128]{1,0:T(8,128)S(1)} %add.15.sums_ref, f32[1,2048]{1,0:T(1,128)S(1)} %bitcast.4, f32[16,2048]{1,0:T(8,128)S(1)} %copy-done, f32[16,2048]{1,0:T(8,128)S(1)} %get-tuple-element.17.image_ref, f32[16,2048]{1,0:T(8,128)S(1)} %get-tuple-element.19.twice_ref, ...), custom_call_target="tpu_custom_call" | custom-call | flops 1000000000 | bytes 10000000 | tf_op jit(solution)/shard_map/update/pallas_call | solution.py:356
  (2 shorter events, 0.0 us)
Async XLA Ops:
  1.6 12.7 %collective-permute-start.1 = (bf16[48,2048]{1,0:T(8,128)(2,1)S(1)}, bf16[48,2048]{1,0:T(8,128)(2,1)S(1)}, u32[]{:S(2)}, u32[]{:S(2)}) collective-permute-start(bf16[48,2048]{1,0:T(8,128)(2,1)S(1)} %prep.1.own_ref), channel_id=1, source_target_pairs={{4,8},{8,4},{12,16},{16,12},{20,24},{24,20},{5,9},{9,5},{13,17},{1... | collective-permute-start | bytes 589832 | tf_op jit(solution)/shard_map/ppermute | solution.py:312
  2.3 13.4 %collective-permute-start = (bf16[48,2048]{1,0:T(8,128)(2,1)S(1)}, bf16[48,2048]{1,0:T(8,128)(2,1)S(1)}, u32[]{:S(2)}, u32[]{:S(2)}) collective-permute-start(bf16[48,2048]{1,0:T(8,128)(2,1)S(1)} %prep.1.own_ref), channel_id=1, source_target_pairs={{0,4},{4,0},{8,12},{12,8},{16,20},{20,16},{24,28},{28,24},{1,5},{5... | collective-permute-start | bytes 589832 | tf_op jit(solution)/shard_map/ppermute | solution.py:311
  15.7 0.9 %copy-start = (f32[16,2048]{1,0:T(8,128)S(1)}, f32[16,2048]{1,0:T(8,128)}, u32[]{:S(2)}) copy-start(f32[16,2048]{1,0:T(8,128)} %vec_ref.7) | copy-start | bytes 393220
  16.6 0.7 %copy-start.1 = (f32[2048]{0:T(1024)S(1)}, f32[2048]{0:T(1024)}, u32[]{:S(2)}) copy-start(f32[2048]{0:T(1024)} %param.5) | copy-start | bytes 24580
  21.1 11.9 %collective-permute-start.3 = (bf16[16,2048]{1,0:T(8,128)(2,1)S(1)}, bf16[16,2048]{1,0:T(8,128)(2,1)S(1)}, u32[]{:S(2)}, u32[]{:S(2)}) collective-permute-start(bf16[16,2048]{1,0:T(8,128)(2,1)S(1)} %get-tuple-element.15.own_ref), channel_id=1, source_target_pairs={{4,8},{8,4},{12,16},{16,12},{20,24},{24,20},{5,9},{9,5},{13,17},{1... | collective-permute-start | bytes 196616 | tf_op jit(solution)/shard_map/ppermute | solution.py:312
  21.8 12.3 %collective-permute-start.2 = (bf16[16,2048]{1,0:T(8,128)(2,1)S(1)}, bf16[16,2048]{1,0:T(8,128)(2,1)S(1)}, u32[]{:S(2)}, u32[]{:S(2)}) collective-permute-start(bf16[16,2048]{1,0:T(8,128)(2,1)S(1)} %get-tuple-element.15.own_ref), channel_id=1, source_target_pairs={{0,4},{4,0},{8,12},{12,8},{16,20},{20,16},{24,28},{28,24},{1,5},{5... | collective-permute-start | bytes 196616 | tf_op jit(solution)/shard_map/ppermute | solution.py:311
  35.5 8.9 %collective-permute-start.6 = (f32[16,128]{1,0:T(8,128)S(1)}, f32[16,128]{1,0:T(8,128)S(1)}, u32[]{:S(2)}, u32[]{:S(2)}) collective-permute-start(f32[16,128]{1,0:T(8,128)S(1)} %get-tuple-element.18), channel_id=1, source_target_pairs={{0,24},{4,28},{8,16},{12,20},{16,8},{20,12},{24,0},{28,4},{1,25},{... | collective-permute-start | bytes 24584 | tf_op jit(solution)/shard_map/ppermute | solution.py:325
  38.0 6.5 %collective-permute-start.5 = (f32[16,128]{1,0:T(8,128)S(1)}, f32[16,128]{1,0:T(8,128)S(1)}, u32[]{:S(2)}, u32[]{:S(2)}) collective-permute-start(f32[16,128]{1,0:T(8,128)S(1)} %get-tuple-element.18), channel_id=1, source_target_pairs={{0,16},{4,20},{8,24},{12,28},{16,0},{20,4},{24,8},{28,12},{1,17},{... | collective-permute-start | bytes 24584 | tf_op jit(solution)/shard_map/ppermute | solution.py:325
  38.9 5.6 %collective-permute-start.4 = (f32[16,128]{1,0:T(8,128)S(1)}, f32[16,128]{1,0:T(8,128)S(1)}, u32[]{:S(2)}, u32[]{:S(2)}) collective-permute-start(f32[16,128]{1,0:T(8,128)S(1)} %get-tuple-element.18), channel_id=1, source_target_pairs={{0,8},{4,12},{8,0},{12,4},{16,24},{20,28},{24,16},{28,20},{1,9},{5... | collective-permute-start | bytes 24584 | tf_op jit(solution)/shard_map/ppermute | solution.py:325
  40.0 8.5 %collective-permute-start.9 = (bf16[32,2048]{1,0:T(8,128)(2,1)S(1)}, bf16[32,2048]{1,0:T(8,128)(2,1)S(1)}, u32[]{:S(2)}, u32[]{:S(2)}) collective-permute-start(bf16[32,2048]{1,0:T(8,128)(2,1)S(1)} %get-tuple-element.20.own_ref), channel_id=1, source_target_pairs={{4,8},{8,4},{12,16},{16,12},{20,24},{24,20},{5,9},{9,5},{13,17},{1... | collective-permute-start | bytes 393224 | tf_op jit(solution)/shard_map/ppermute | solution.py:312
  40.8 7.7 %collective-permute-start.8 = (bf16[32,2048]{1,0:T(8,128)(2,1)S(1)}, bf16[32,2048]{1,0:T(8,128)(2,1)S(1)}, u32[]{:S(2)}, u32[]{:S(2)}) collective-permute-start(bf16[32,2048]{1,0:T(8,128)(2,1)S(1)} %get-tuple-element.20.own_ref), channel_id=1, source_target_pairs={{0,4},{4,0},{8,12},{12,8},{16,20},{20,16},{24,28},{28,24},{1,5},{5... | collective-permute-start | bytes 393224 | tf_op jit(solution)/shard_map/ppermute | solution.py:311
  44.5 4.0 %collective-permute-start.7 = (f32[16,128]{1,0:T(8,128)S(1)}, f32[16,128]{1,0:T(8,128)S(1)}, u32[]{:S(2)}, u32[]{:S(2)}) collective-permute-start(f32[16,128]{1,0:T(8,128)S(1)} %add_add_fusion), channel_id=1, source_target_pairs={{0,4},{4,0},{8,12},{12,8},{16,20},{20,16},{24,28},{28,24},{1,5},{5... | collective-permute-start | bytes 24584 | tf_op jit(solution)/shard_map/ppermute | solution.py:325

commit v5 on v4

--- a/solution.py
+++ b/solution.py
@@ -175,14 +175,17 @@
     return lax.rem(lax.axis_index("pts"), 2)
 
 
-def prep_kernel(points_ref, vec_ref, out_ref, wide_ref, sems):
+def prep_kernel(points_ref, vec_ref, noise_ref, out_ref, near_vec_ref, near_noise_ref, sems):
     points_copy = pltpu.make_async_copy(points_ref, out_ref.at[:F], sems.at[0])
-    vec_copy = pltpu.make_async_copy(vec_ref, wide_ref, sems.at[1])
+    vec_copy = pltpu.make_async_copy(vec_ref, near_vec_ref, sems.at[1])
+    noise_copy = pltpu.make_async_copy(noise_ref, near_noise_ref, sems.at[2])
     vec_copy.start()
     points_copy.start()
+    noise_copy.start()
     vec_copy.wait()
-    out_ref[F:, :] = wide_ref[...].astype(bf16)
+    out_ref[F:, :] = near_vec_ref[...].astype(bf16)
     points_copy.wait()
+    noise_copy.wait()
 
 
 def local_kernel(
@@ -244,7 +247,7 @@
 
 
 def own_kernel(blocks, own_ref, tiles_ref, part_ref):
-    local_products(blocks, own_ref[...], tiles_ref, part_ref)
+    local_products(blocks, own_ref[:, : blocks * BLK], tiles_ref, part_ref)
 
 
 def second_kernel(
@@ -262,8 +265,7 @@
         twice_ref[:, cols] = q
         u = r - SHIFT * w
         y = w - SHIFT * q
-        low_ref[:width, cols] = y.astype(bf16)
-        low_ref[width:, cols] = q.astype(bf16)
+        low_ref[:, cols] = y.astype(bf16)
         terms = (r * r, r * w, u * u, u * w, w * w, y * u, q * u, y * w, q * w)
         totals = [total + (term[:, :LANES] + term[:, LANES:]) for total, term in zip(totals, terms)]
     lane = lax.broadcasted_iota(jnp.int32, (width, LANES), 1)
@@ -271,17 +273,20 @@
     for at, total in enumerate(totals):
         out = jnp.where(lane == at, jnp.sum(total, axis=1, keepdims=True), out)
     sums_ref[...] = out
+    points = blocks * BLK
+    for at, part in enumerate(three_parts(out)):
+        low_ref[:, points + at * LANES : points + (at + 1) * LANES] = part.astype(bf16)
 
 
 def third_kernel(blocks, a_ref, b_ref, tiles_ref, part_ref, out_ref, wide_ref):
-    gather_sides(blocks, odd_place(), a_ref[...], b_ref[...], wide_ref)
+    points = blocks * BLK
+    gather_sides(blocks, odd_place(), a_ref[:, :points], b_ref[:, :points], wide_ref)
     for pair in range(blocks // 2):
         cols = pair_cols(pair)
         out_ref[:, cols] = (part_ref[:, cols] + side_products(blocks, pair, wide_ref, tiles_ref)) * SCALE
 
 
 def last_kernel(sums_ref, noise_ref, vec_ref, image_ref, twice_ref, prod_ref, x_ref, r_ref, w_ref):
-    width = vec_ref.shape[0]
     rr, rw, uu, uw, ww, yu, qu, yw, qw = [sums_ref[:, at : at + 1] for at in range(SUMS)]
     alpha0 = rr / rw
     delta = alpha0 - SHIFT
@@ -292,7 +297,8 @@
     r0, w0, q0 = vec_ref[...], image_ref[...], twice_ref[...]
     r1 = r0 - alpha0 * w0
     w1 = w0 - alpha0 * q0
-    q1 = noise_ref[...] * w1 + (prod_ref[:width, :] - delta * prod_ref[width:, :])
+    share = alpha0 * (1.0 / SHIFT)
+    q1 = noise_ref[...] * w1 + (1.0 - share) * (q0 - noise_ref[...] * w0) + share * prod_ref[...]
     x_ref[...] = alpha0 * r0 + alpha1 * (r1 + beta * r0)
     r_ref[...] = r1 - alpha1 * (w1 + beta * w0)
     w_ref[...] = w1 - alpha1 * (q1 + beta * q0)
@@ -307,18 +313,23 @@
 
 def both_sides(x):
     count = lax.axis_size("pts")
-    return (
-        lax.ppermute(x, "pts", swap_pairs(count, 0)),
-        lax.ppermute(x, "pts", swap_pairs(count, 1)),
-    )
-
-
-def total_over_points(x):
+    b = lax.ppermute(x, "pts", swap_pairs(count, 1))
+    a = lax.ppermute(x, "pts", swap_pairs(count, 0))
+    return a, b
+
+
+def total_over_points(x, neighbour):
     count = lax.axis_size("pts")
     if count & (count - 1):
         return lax.psum(x, "pts")
+    if count == 1:
+        return x
+    high, middle, low = [
+        neighbour[:, neighbour.shape[1] - (3 - k) * LANES :][:, :LANES].astype(f32) for k in range(3)
+    ]
+    x = x + ((high + middle) + low)
     step = count
-    while step > 1:
+    while step > 2:
         size = 4 if step > 4 else 2
         step //= size
         x = x + sum(
@@ -365,14 +376,13 @@
             name=name,
         )(*[pltpu.with_memory_space_constraint(x, pltpu.HBM) for x in ins[:far]], *[pltpu.with_memory_space_constraint(x, pltpu.VMEM) for x in ins[far:]])
 
-    noise = noise_var[None, :]
-    payload = call(
+    payload, vec, noise = call(
         prep_kernel,
         "prep",
-        (points.T, right_side),
-        pltpu.VMEM((F + width, local_rows), bf16),
-        (pltpu.VMEM(full, f32), pltpu.SemaphoreType.DMA((2,))),
-        far=2,
+        (points.T, right_side, noise_var[None, :]),
+        (pltpu.VMEM((F + width, local_rows), bf16), pltpu.VMEM(full, f32), pltpu.VMEM((1, local_rows), f32)),
+        (pltpu.SemaphoreType.DMA((3,)),),
+        far=3,
     )
     halo_a, halo_b = both_sides(payload)
     tiles, right, part = call(
@@ -386,7 +396,7 @@
     tiles, image, low = call(
         functools.partial(first_kernel, blocks),
         "image",
-        (pattern, halo_a, halo_b, right, tiles, part, noise, right_side),
+        (pattern, halo_a, halo_b, right, tiles, part, noise, vec),
         (tiles_type, pltpu.VMEM(full, f32), pltpu.VMEM(full, bf16)),
         (left(2), wide(width), listed, numbers(2 * pairs), copied),
         {4: 0},
@@ -399,27 +409,26 @@
     twice, low, sums = call(
         functools.partial(second_kernel, blocks),
         "twice",
-        (low_a, low_b, tiles, part, noise, right_side, image),
+        (low_a, low_b, tiles, part, noise, vec, image),
         (
             pltpu.VMEM(full, f32),
-            pltpu.VMEM((2 * width, local_rows), bf16),
+            pltpu.VMEM((width, local_rows + 3 * LANES), bf16),
             pltpu.VMEM((width, LANES), f32),
         ),
         (wide(width),),
     )
     low_a, low_b = both_sides(low)
-    sums = total_over_points(sums)
-    both = pltpu.VMEM((2 * width, local_rows), f32)
-    part = call(functools.partial(own_kernel, blocks), "own_products_both", (low, tiles), both)
+    sums = total_over_points(sums, low_a)
+    part = call(functools.partial(own_kernel, blocks), "own_products_last", (low, tiles), pltpu.VMEM(full, f32))
     prods = call(
         functools.partial(third_kernel, blocks),
         "products",
         (low_a, low_b, tiles, part),
-        both,
-        (wide(2 * width),),
+        pltpu.VMEM(full, f32),
+        (wide(width),),
     )
     out = jax.ShapeDtypeStruct(full, f32)
-    return call(last_kernel, "update", (sums, noise, right_side, image, twice, prods), (out, out, out))
+    return call(last_kernel, "update", (sums, noise, vec, image, twice, prods), (out, out, out))
 
 
 def solution(mesh):

time: 51.6 us -> 51.4 us (level)
  Pallas kernels: 17.9 us -> 21.3 us
  starting transfers between devices: 26.2 us -> 24.5 us
  local copies, waits for them, and re-layouts: 1.6 us -> 0 us
  waiting for transfers between devices: 4.84 us -> 4.3 us
    pallas_call x8, Pallas kernels: 17.9 us -> 21.3 us  [call(): pl.pallas_call(kernel, out_shape=outs, in_specs=[FAR] * far + [VM] * (len...]
    ppermute x6, starting transfers between devices: 21.7 us -> 19.8 us  [the longest x3 17.6 us: both_sides(): a = lax.ppermute(x, 'pts', swap_pairs(count, 0))]
    unnamed x4 -> x0, local copies, waits for them, and re-layouts: 1.6 us -> none
    ppermute x4 -> x3, waiting for transfers between devices: 2.35 us -> 2.06 us  [total_over_points(): lax.ppermute(x, 'pts', [(i, i ^ k * step) for i in range(count)])]
    ppermute x4 -> x3, starting transfers between devices: 4.51 us -> 4.67 us  [total_over_points(): lax.ppermute(x, 'pts', [(i, i ^ k * step) for i in range(count)])]
  transfers between devices with their start and end apart: 10 -> 9, of which waited for: 3 -> 3; matrix products, arithmetic and copies ran while one was open for 0% -> 0% of each run, Pallas kernels for 17% -> 23%
where the time goes in v5:
time: 51.4 us; the launch traced here: 50.8 us
  starting transfers between devices  24.5 us (48%)
  Pallas kernels  21.3 us (41%)
  waiting for transfers between devices  4.3 us (8%)
  between operations  0.71 us (1%)
    pallas_call x8, Pallas kernels, call(): pl.pallas_call(kernel, out_shape=outs, in_specs=[FAR] * far + [VM] * (len...  21.3 us
    ppermute x3, starting transfers between devices, both_sides(): a = lax.ppermute(x, 'pts', swap_pairs(count, 0))  17.6 us
    ppermute x3, starting transfers between devices, total_over_points(): lax.ppermute(x, 'pts', [(i, i ^ k * step) for i in range(count)])  4.67 us
    ppermute x3, waiting for transfers between devices, both_sides(): a = lax.ppermute(x, 'pts', swap_pairs(count, 0))  2.24 us
    ppermute x3, starting transfers between devices, both_sides(): b = lax.ppermute(x, 'pts', swap_pairs(count, 1))  2.18 us
    ppermute x3, waiting for transfers between devices, total_over_points(): lax.ppermute(x, 'pts', [(i, i ^ k * step) for i in range(count)])  2.06 us
  transfers between devices with their start and end apart: 9, of which 3 were waited for; matrix products, arithmetic and copies ran while one was open for 0% of the time, Pallas kernels for 23%

profile of v5, /device:TPU:0, one launch (start us, length us, event | category | flops | bytes accessed | tf_op | source)
XLA Modules:
  0.0 50.8 jit_solution(2511753911705847712)
XLA Ops:
  0.6 1.0 %prep.1 = (bf16[48,2048]{1,0:T(8,128)(2,1)S(1)}, f32[16,2048]{1,0:T(8,128)S(1)}, f32[1,2048]{1,0:T(1,128)S(1)}) custom-call(bf16[32,2048]{1,0:T(8,128)(2,1)} %bitcast.2, f32[16,2048]{1,0:T(8,128)} %vec_ref.1, f32[1,2048]{1,0:T(1,128)} %bitcast.3), custom_call_target="tpu_custom_call" | custom-call | flops 1000000000 | bytes 10000000 | tf_op jit(solution)/shard_map/prep/pallas_call | solution.py:367
  1.6 0.7 %collective-permute-start.1 = (bf16[48,2048]{1,0:T(8,128)(2,1)S(1)}, bf16[48,2048]{1,0:T(8,128)(2,1)S(1)}, u32[]{:S(2)}, u32[]{:S(2)}) collective-permute-start(bf16[48,2048]{1,0:T(8,128)(2,1)S(1)} %get-tuple-element.15.own_ref), channel_id=1, source_target_pairs={{4,8},{8,4},{12,16},{16,12},{20,24},{24,20},{5,9},{9,5},{13,17},{1... | collective-permute-start | bytes 589832 | tf_op jit(solution)/shard_map/ppermute | solution.py:316
  2.3 5.8 %collective-permute-start = (bf16[48,2048]{1,0:T(8,128)(2,1)S(1)}, bf16[48,2048]{1,0:T(8,128)(2,1)S(1)}, u32[]{:S(2)}, u32[]{:S(2)}) collective-permute-start(bf16[48,2048]{1,0:T(8,128)(2,1)S(1)} %get-tuple-element.15.own_ref), channel_id=1, source_target_pairs={{0,4},{4,0},{8,12},{12,8},{16,20},{20,16},{24,28},{28,24},{1,5},{5... | collective-permute-start | bytes 589832 | tf_op jit(solution)/shard_map/ppermute | solution.py:317
  8.1 7.9 %local_tiles.1 = (bf16[545,128,128]{2,1,0:T(8,128)(2,1)S(1)}, bf16[16,128,128]{2,1,0:T(8,128)(2,1)S(1)}, f32[16,2048]{1,0:T(8,128)S(1)}) custom-call(s32[16,33]{1,0:T(8,128)} %pattern_ref.3, bf16[48,2048]{1,0:T(8,128)(2,1)S(1)} %get-tuple-element.15.own_ref), custom_call_target="tpu_custom_call" | custom-call | flops 1000000000 | bytes 10000000 | tf_op jit(solution)/shard_map/local_tiles/pallas_call | solution.py:367
  16.0 0.0 collective-permute-done.1.b_ref
  16.0 0.0 collective-permute-done.a_ref
  16.1 6.0 %image.1 = (bf16[545,128,128]{2,1,0:T(8,128)(2,1)S(1)}, f32[16,2048]{1,0:T(8,128)S(1)}, bf16[16,2048]{1,0:T(8,128)(2,1)S(1)}) custom-call(s32[16,33]{1,0:T(8,128)} %pattern_ref.3, bf16[48,2048]{1,0:T(8,128)(2,1)S(1)} %collective-permute-done.a_ref, bf16[48,2048]{1,0:T(8,128)(2,1)S(1)} %collective-permute-done.1.b_ref, ...), custom_call_target="tpu_custom_call", output_to_operand_aliasing={{0}: (4, {})} | custom-call | flops 1000000000 | bytes 10000000 | tf_op jit(solution)/shard_map/image/pallas_call | solution.py:367
  22.1 0.7 %collective-permute-start.3 = (bf16[16,2048]{1,0:T(8,128)(2,1)S(1)}, bf16[16,2048]{1,0:T(8,128)(2,1)S(1)}, u32[]{:S(2)}, u32[]{:S(2)}) collective-permute-start(bf16[16,2048]{1,0:T(8,128)(2,1)S(1)} %get-tuple-element.21.own_ref), channel_id=1, source_target_pairs={{4,8},{8,4},{12,16},{16,12},{20,24},{24,20},{5,9},{9,5},{13,17},{1... | collective-permute-start | bytes 196616 | tf_op jit(solution)/shard_map/ppermute | solution.py:316
  22.8 6.0 %collective-permute-start.2 = (bf16[16,2048]{1,0:T(8,128)(2,1)S(1)}, bf16[16,2048]{1,0:T(8,128)(2,1)S(1)}, u32[]{:S(2)}, u32[]{:S(2)}) collective-permute-start(bf16[16,2048]{1,0:T(8,128)(2,1)S(1)} %get-tuple-element.21.own_ref), channel_id=1, source_target_pairs={{0,4},{4,0},{8,12},{12,8},{16,20},{20,16},{24,28},{28,24},{1,5},{5... | collective-permute-start | bytes 196616 | tf_op jit(solution)/shard_map/ppermute | solution.py:317
  28.8 1.2 %own_products.1.part_ref = f32[16,2048]{1,0:T(8,128)S(1)} custom-call(bf16[16,2048]{1,0:T(8,128)(2,1)S(1)} %get-tuple-element.21.own_ref, bf16[545,128,128]{2,1,0:T(8,128)(2,1)S(1)} %get-tuple-element.22.tiles_ref), custom_call_target="tpu_custom_call" | custom-call | flops 1000000000 | bytes 10000000 | tf_op jit(solution)/shard_map/own_products/pallas_call | solution.py:367
  30.0 0.0 collective-permute-done.3.b_ref
  30.0 1.0 %collective-permute-done.2.a_ref = bf16[16,2048]{1,0:T(8,128)(2,1)S(1)} collective-permute-done((bf16[16,2048]{1,0:T(8,128)(2,1)S(1)}, bf16[16,2048]{1,0:T(8,128)(2,1)S(1)}, u32[]{:S(2)}, u32[]{:S(2)}) %collective-permute-start.2) | collective-permute-done | bytes 65568 | tf_op jit(solution)/shard_map/ppermute | solution.py:317
  31.0 1.5 %twice.1 = (f32[16,2048]{1,0:T(8,128)S(1)}, bf16[16,2432]{1,0:T(8,128)(2,1)S(1)}, f32[16,128]{1,0:T(8,128)S(1)}) custom-call(bf16[16,2048]{1,0:T(8,128)(2,1)S(1)} %collective-permute-done.2.a_ref, bf16[16,2048]{1,0:T(8,128)(2,1)S(1)} %collective-permute-done.3.b_ref, bf16[545,128,128]{2,1,0:T(8,128)(2,1)S(1)} %get-tuple-element.22.tiles_ref, ...), custom_call_target="tpu_custom_call" | custom-call | flops 1000000000 | bytes 10000000 | tf_op jit(solution)/shard_map/twice/pallas_call | solution.py:367
  32.5 0.8 %collective-permute-start.8 = (bf16[16,2432]{1,0:T(8,128)(2,1)S(1)}, bf16[16,2432]{1,0:T(8,128)(2,1)S(1)}, u32[]{:S(2)}, u32[]{:S(2)}) collective-permute-start(bf16[16,2432]{1,0:T(8,128)(2,1)S(1)} %get-tuple-element.25.own_ref), channel_id=1, source_target_pairs={{4,8},{8,4},{12,16},{16,12},{20,24},{24,20},{5,9},{9,5},{13,17},{1... | collective-permute-start | bytes 233480 | tf_op jit(solution)/shard_map/ppermute | solution.py:316
  33.4 5.8 %collective-permute-start.4 = (bf16[16,2432]{1,0:T(8,128)(2,1)S(1)}, bf16[16,2432]{1,0:T(8,128)(2,1)S(1)}, u32[]{:S(2)}, u32[]{:S(2)}) collective-permute-start(bf16[16,2432]{1,0:T(8,128)(2,1)S(1)} %get-tuple-element.25.own_ref), channel_id=1, source_target_pairs={{0,4},{4,0},{8,12},{12,8},{16,20},{20,16},{24,28},{28,24},{1,5},{5... | collective-permute-start | bytes 233480 | tf_op jit(solution)/shard_map/ppermute | solution.py:317
  39.2 1.2 %own_products_last.1.part_ref = f32[16,2048]{1,0:T(8,128)S(1)} custom-call(bf16[16,2432]{1,0:T(8,128)(2,1)S(1)} %get-tuple-element.25.own_ref, bf16[545,128,128]{2,1,0:T(8,128)(2,1)S(1)} %get-tuple-element.22.tiles_ref), custom_call_target="tpu_custom_call" | custom-call | flops 1000000000 | bytes 10000000 | tf_op jit(solution)/shard_map/own_products_last/pallas_call | solution.py:367
  40.4 1.2 %collective-permute-done.4.a_ref = bf16[16,2432]{1,0:T(8,128)(2,1)S(1)} collective-permute-done((bf16[16,2432]{1,0:T(8,128)(2,1)S(1)}, bf16[16,2432]{1,0:T(8,128)(2,1)S(1)}, u32[]{:S(2)}, u32[]{:S(2)}) %collective-permute-start.4) | collective-permute-done | bytes 77856 | tf_op jit(solution)/shard_map/ppermute | solution.py:317
  41.6 3.5 %collective-permute-start.7 = (f32[16,128]{1,0:T(8,128)S(1)}, f32[16,128]{1,0:T(8,128)S(1)}, u32[]{:S(2)}, u32[]{:S(2)}) collective-permute-start(f32[16,128]{1,0:T(8,128)S(1)} %add_add_fusion.1), channel_id=1, source_target_pairs={{0,24},{4,28},{8,16},{12,20},{16,8},{20,12},{24,0},{28,4},{1,25},{... | collective-permute-start | bytes 24584 | tf_op jit(solution)/shard_map/ppermute | solution.py:336
  45.1 0.6 %collective-permute-start.6 = (f32[16,128]{1,0:T(8,128)S(1)}, f32[16,128]{1,0:T(8,128)S(1)}, u32[]{:S(2)}, u32[]{:S(2)}) collective-permute-start(f32[16,128]{1,0:T(8,128)S(1)} %add_add_fusion.1), channel_id=1, source_target_pairs={{0,16},{4,20},{8,24},{12,28},{16,0},{20,4},{24,8},{28,12},{1,17},{... | collective-permute-start | bytes 24584 | tf_op jit(solution)/shard_map/ppermute | solution.py:336
  45.7 0.5 collective-permute-start.5
  46.2 0.0 collective-permute-done.8.b_ref
  46.2 1.4 %products.1.prod_ref = f32[16,2048]{1,0:T(8,128)S(1)} custom-call(bf16[16,2432]{1,0:T(8,128)(2,1)S(1)} %collective-permute-done.4.a_ref, bf16[16,2432]{1,0:T(8,128)(2,1)S(1)} %collective-permute-done.8.b_ref, bf16[545,128,128]{2,1,0:T(8,128)(2,1)S(1)} %get-tuple-element.22.tiles_ref, f32[16,2048]{1,0:T(8,128)S(1)} %own_products_last.1.part_ref), custom_call_target="tpu_custom_call" | custom-call | flops 1000000000 | bytes 10000000 | tf_op jit(solution)/shard_map/products/pallas_call | solution.py:367
  47.6 0.0 collective-permute-done.7
  47.6 2.1 %collective-permute-done.6 = f32[16,128]{1,0:T(8,128)S(1)} collective-permute-done((f32[16,128]{1,0:T(8,128)S(1)}, f32[16,128]{1,0:T(8,128)S(1)}, u32[]{:S(2)}, u32[]{:S(2)}) %collective-permute-start.6) | collective-permute-done | bytes 8224 | tf_op jit(solution)/shard_map/ppermute | solution.py:336
  49.6 0.0 collective-permute-done.5
  49.7 1.2 %update.1 = (f32[16,2048]{1,0:T(8,128)}, f32[16,2048]{1,0:T(8,128)}, f32[16,2048]{1,0:T(8,128)}) custom-call(f32[16,128]{1,0:T(8,128)S(1)} %add_add_fusion.sums_ref, f32[1,2048]{1,0:T(1,128)S(1)} %get-tuple-element.19.noise_ref, f32[16,2048]{1,0:T(8,128)S(1)} %get-tuple-element.20.vec_ref, f32[16,2048]{1,0:T(8,128)S(1)} %get-tuple-element.23.image_ref, ...), custom_call_target="tpu_custom_call" | custom-call | flops 1000000000 | bytes 10000000 | tf_op jit(solution)/shard_map/update/pallas_call | solution.py:367
  (2 shorter events, 0.0 us)
Async XLA Ops:
  1.6 14.4 %collective-permute-start.1 = (bf16[48,2048]{1,0:T(8,128)(2,1)S(1)}, bf16[48,2048]{1,0:T(8,128)(2,1)S(1)}, u32[]{:S(2)}, u32[]{:S(2)}) collective-permute-start(bf16[48,2048]{1,0:T(8,128)(2,1)S(1)} %get-tuple-element.15.own_ref), channel_id=1, source_target_pairs={{4,8},{8,4},{12,16},{16,12},{20,24},{24,20},{5,9},{9,5},{13,17},{1... | collective-permute-start | bytes 589832 | tf_op jit(solution)/shard_map/ppermute | solution.py:316
  2.3 13.7 %collective-permute-start = (bf16[48,2048]{1,0:T(8,128)(2,1)S(1)}, bf16[48,2048]{1,0:T(8,128)(2,1)S(1)}, u32[]{:S(2)}, u32[]{:S(2)}) collective-permute-start(bf16[48,2048]{1,0:T(8,128)(2,1)S(1)} %get-tuple-element.15.own_ref), channel_id=1, source_target_pairs={{0,4},{4,0},{8,12},{12,8},{16,20},{20,16},{24,28},{28,24},{1,5},{5... | collective-permute-start | bytes 589832 | tf_op jit(solution)/shard_map/ppermute | solution.py:317
  22.1 7.9 %collective-permute-start.3 = (bf16[16,2048]{1,0:T(8,128)(2,1)S(1)}, bf16[16,2048]{1,0:T(8,128)(2,1)S(1)}, u32[]{:S(2)}, u32[]{:S(2)}) collective-permute-start(bf16[16,2048]{1,0:T(8,128)(2,1)S(1)} %get-tuple-element.21.own_ref), channel_id=1, source_target_pairs={{4,8},{8,4},{12,16},{16,12},{20,24},{24,20},{5,9},{9,5},{13,17},{1... | collective-permute-start | bytes 196616 | tf_op jit(solution)/shard_map/ppermute | solution.py:316
  22.8 8.3 %collective-permute-start.2 = (bf16[16,2048]{1,0:T(8,128)(2,1)S(1)}, bf16[16,2048]{1,0:T(8,128)(2,1)S(1)}, u32[]{:S(2)}, u32[]{:S(2)}) collective-permute-start(bf16[16,2048]{1,0:T(8,128)(2,1)S(1)} %get-tuple-element.21.own_ref), channel_id=1, source_target_pairs={{0,4},{4,0},{8,12},{12,8},{16,20},{20,16},{24,28},{28,24},{1,5},{5... | collective-permute-start | bytes 196616 | tf_op jit(solution)/shard_map/ppermute | solution.py:317
  32.5 13.7 %collective-permute-start.8 = (bf16[16,2432]{1,0:T(8,128)(2,1)S(1)}, bf16[16,2432]{1,0:T(8,128)(2,1)S(1)}, u32[]{:S(2)}, u32[]{:S(2)}) collective-permute-start(bf16[16,2432]{1,0:T(8,128)(2,1)S(1)} %get-tuple-element.25.own_ref), channel_id=1, source_target_pairs={{4,8},{8,4},{12,16},{16,12},{20,24},{24,20},{5,9},{9,5},{13,17},{1... | collective-permute-start | bytes 233480 | tf_op jit(solution)/shard_map/ppermute | solution.py:316
  33.4 8.2 %collective-permute-start.4 = (bf16[16,2432]{1,0:T(8,128)(2,1)S(1)}, bf16[16,2432]{1,0:T(8,128)(2,1)S(1)}, u32[]{:S(2)}, u32[]{:S(2)}) collective-permute-start(bf16[16,2432]{1,0:T(8,128)(2,1)S(1)} %get-tuple-element.25.own_ref), channel_id=1, source_target_pairs={{0,4},{4,0},{8,12},{12,8},{16,20},{20,16},{24,28},{28,24},{1,5},{5... | collective-permute-start | bytes 233480 | tf_op jit(solution)/shard_map/ppermute | solution.py:317
  41.6 6.0 %collective-permute-start.7 = (f32[16,128]{1,0:T(8,128)S(1)}, f32[16,128]{1,0:T(8,128)S(1)}, u32[]{:S(2)}, u32[]{:S(2)}) collective-permute-start(f32[16,128]{1,0:T(8,128)S(1)} %add_add_fusion.1), channel_id=1, source_target_pairs={{0,24},{4,28},{8,16},{12,20},{16,8},{20,12},{24,0},{28,4},{1,25},{... | collective-permute-start | bytes 24584 | tf_op jit(solution)/shard_map/ppermute | solution.py:336
  45.1 4.5 %collective-permute-start.6 = (f32[16,128]{1,0:T(8,128)S(1)}, f32[16,128]{1,0:T(8,128)S(1)}, u32[]{:S(2)}, u32[]{:S(2)}) collective-permute-start(f32[16,128]{1,0:T(8,128)S(1)} %add_add_fusion.1), channel_id=1, source_target_pairs={{0,16},{4,20},{8,24},{12,28},{16,0},{20,4},{24,8},{28,12},{1,17},{... | collective-permute-start | bytes 24584 | tf_op jit(solution)/shard_map/ppermute | solution.py:336
  45.7 3.9 %collective-permute-start.5 = (f32[16,128]{1,0:T(8,128)S(1)}, f32[16,128]{1,0:T(8,128)S(1)}, u32[]{:S(2)}, u32[]{:S(2)}) collective-permute-start(f32[16,128]{1,0:T(8,128)S(1)} %add_add_fusion.1), channel_id=1, source_target_pairs={{0,8},{4,12},{8,0},{12,4},{16,24},{20,28},{24,16},{28,20},{1,9},{5... | collective-permute-start | bytes 24584 | tf_op jit(solution)/shard_map/ppermute | solution.py:336

commit v6 on v5

--- a/solution.py
+++ b/solution.py
@@ -175,69 +175,90 @@
     return lax.rem(lax.axis_index("pts"), 2)
 
 
-def prep_kernel(points_ref, vec_ref, noise_ref, out_ref, near_vec_ref, near_noise_ref, sems):
+def prep_kernel(points_ref, vec_ref, noise_ref, pattern_ref, out_ref, near_vec_ref, near_noise_ref, listed_ref, sems):
     points_copy = pltpu.make_async_copy(points_ref, out_ref.at[:F], sems.at[0])
     vec_copy = pltpu.make_async_copy(vec_ref, near_vec_ref, sems.at[1])
     noise_copy = pltpu.make_async_copy(noise_ref, near_noise_ref, sems.at[2])
     vec_copy.start()
     points_copy.start()
     noise_copy.start()
+    pattern_copy = pltpu.make_async_copy(pattern_ref, listed_ref, sems.at[3])
+    pattern_copy.start()
     vec_copy.wait()
     out_ref[F:, :] = near_vec_ref[...].astype(bf16)
     points_copy.wait()
     noise_copy.wait()
-
-
-def local_kernel(
-    blocks, pattern_ref, own_ref, tiles_ref, right_ref, part_ref, left_ref, listed_ref, list_ref, dead_ref, sem
-):
-    pattern_copy = pltpu.make_async_copy(pattern_ref, listed_ref, sem)
-    pattern_copy.start()
+    pattern_copy.wait()
+
+
+def local_kernel(blocks, listed_ref, own_ref, tiles_ref, right_ref, part_ref, left_ref, list_ref, dead_ref):
     fill_features(own_ref[:F, :], left_ref, 0, right_ref)
-    first = blocks * blocks
     for pair in range(blocks // 2):
-
-        def clear(at, carry, start=first + pair * 2 * (blocks + 2)):
-            tiles_ref[pl.ds(start + at * 4, 4)] = jnp.zeros((4, BLK, BLK), bf16)
-            return carry
-
-        lax.fori_loop(0, (blocks + 2) // 2, clear, 0)
-    pattern_copy.wait()
-    dead = jnp.int32(0)
-    count = jnp.int32(0)
-    for home, other, column in local_entries(blocks):
-        code = jnp.int32(entry(local_slot(blocks, home, other), local_slot(blocks, other, home), other, home))
-        live = listed_ref[home, column]
-        dead_ref[dead] = code
-        list_ref[count] = code
-        dead = dead + (1 - live)
-        count = count + live
+        first = blocks * blocks + pair * 2 * (blocks + 2)
+        tiles_ref[first + 1] = jnp.zeros((BLK, BLK), bf16)
+        tiles_ref[first + 2 * (blocks + 1)] = jnp.zeros((BLK, BLK), bf16)
+    entries = [
+        (entry(local_slot(blocks, home, other), local_slot(blocks, other, home), other, home), home, column)
+        for home, other, column in local_entries(blocks)
+    ]
+    count, dead = scan_entries(entries, listed_ref, list_ref, dead_ref)
     pad_list(count, list_ref, spare_slot(blocks))
     clear_tiles(dead, dead_ref, tiles_ref)
     make_tiles(count, list_ref, left_ref, right_ref, tiles_ref, True)
     local_products(blocks, own_ref[F:, :], tiles_ref, part_ref)
 
 
-def first_kernel(
-    blocks, pattern_ref, a_ref, b_ref, right_ref, tiles_in, part_ref, noise_ref, vec_ref,
-    tiles_ref, image_ref, low_ref, left_ref, wide_ref, listed_ref, list_ref, sem,
+def scan_entries(entries, listed_ref, list_ref, dead_ref):
+    count = jnp.int32(0)
+    dead = jnp.int32(0)
+    for code, home, column in entries:
+        live = listed_ref[home, column]
+        list_ref[count] = jnp.int32(code)
+        dead_ref[dead] = jnp.int32(code)
+        count = count + live
+        dead = dead + (1 - live)
+    return count, dead
+
+
+def make_side(blocks, before, listed_ref, points, right_ref, tiles_ref, left_ref, list_ref, dead_ref, count_ref):
+    fill_features(points, left_ref, 0)
+    for after in (False, True):
+
+        @pl.when(before == (0 if after else 1))
+        def _(after=after):
+            entries = []
+            for home, other, column in side_entries(blocks, after):
+                slot = side_slot(blocks, home, other, after)
+                entries.append((entry(slot, slot, other, home), home, column))
+            count, dead = scan_entries(entries, listed_ref, list_ref, dead_ref)
+            count_ref[0] = count
+            count_ref[1] = dead
+
+    count = count_ref[0]
+    pad_list(count, list_ref, spare_slot(blocks))
+    clear_tiles(count_ref[1], dead_ref, tiles_ref)
+    make_tiles(count, list_ref, left_ref, right_ref, tiles_ref, False)
+
+
+def side_kernel(
+    blocks, listed_ref, b_ref, right_ref, tiles_in, tiles_ref, left_ref, list_ref, dead_ref, count_ref
 ):
     del tiles_in
-    pattern_copy = pltpu.make_async_copy(pattern_ref, listed_ref, sem)
-    pattern_copy.start()
+    make_side(
+        blocks, 1 - odd_place(), listed_ref, b_ref[:F, :], right_ref, tiles_ref, left_ref, list_ref, dead_ref, count_ref
+    )
+
+
+def first_kernel(
+    blocks, listed_ref, a_ref, b_ref, right_ref, tiles_in, part_ref, noise_ref, vec_ref,
+    tiles_ref, image_ref, low_ref, left_ref, list_ref, dead_ref, count_ref, wide_ref,
+):
+    del tiles_in
     before = odd_place()
-    fill_features(a_ref[:F, :], left_ref, (1 - before) * blocks)
-    fill_features(b_ref[:F, :], left_ref, before * blocks)
+    make_side(
+        blocks, before, listed_ref, a_ref[:F, :], right_ref, tiles_ref, left_ref, list_ref, dead_ref, count_ref
+    )
     gather_sides(blocks, before, a_ref[F:, :], b_ref[F:, :], wide_ref)
-    pattern_copy.wait()
-    count = jnp.int32(0)
-    for after in (False, True):
-        for home, other, column in side_entries(blocks, after):
-            slot = side_slot(blocks, home, other, after)
-            list_ref[count] = jnp.int32(entry(slot, 0, other + (blocks if after else 0), home))
-            count = count + listed_ref[home, column]
-    pad_list(count, list_ref, spare_slot(blocks))
-    make_tiles(count, list_ref, left_ref, right_ref, tiles_ref, False)
     for pair in range(blocks // 2):
         cols = pair_cols(pair)
         total = part_ref[:, cols] + side_products(blocks, pair, wide_ref, tiles_ref)
@@ -311,11 +332,16 @@
     return pairs
 
 
+def first_side(x):
+    return lax.ppermute(x, "pts", swap_pairs(lax.axis_size("pts"), 0))
+
+
+def second_side(x):
+    return lax.ppermute(x, "pts", swap_pairs(lax.axis_size("pts"), 1))
+
+
 def both_sides(x):
-    count = lax.axis_size("pts")
-    b = lax.ppermute(x, "pts", swap_pairs(count, 1))
-    a = lax.ppermute(x, "pts", swap_pairs(count, 0))
-    return a, b
+    return first_side(x), second_side(x)
 
 
 def total_over_points(x, neighbour):
@@ -340,6 +366,7 @@
 
 VM = pl.BlockSpec(memory_space=pltpu.VMEM)
 FAR = pl.BlockSpec(memory_space=pltpu.HBM)
+SM = pl.BlockSpec(memory_space=pltpu.SMEM)
 
 
 def per_device(points, noise_var, right_side, pattern):
@@ -351,56 +378,72 @@
     full = (width, local_rows)
     tiles_type = pltpu.VMEM((spare_slot(blocks) + 1, BLK, BLK), bf16)
     pairs = blocks * (blocks + 1) // 2
-    listed = pltpu.SMEM(pattern.shape, jnp.int32)
-    copied = pltpu.SemaphoreType.DMA(())
-
-    def left(count):
-        return pltpu.VMEM((count * blocks, BLK, LANES), bf16)
 
     def numbers(count):
-        return pltpu.SMEM((count + STEPS[-1],), jnp.int32)
-
-    def wide(rows):
-        return pltpu.VMEM((rows, 2 * local_rows), bf16)
-
-    def call(kernel, name, ins, outs, scratch=(), aliases=None, far=0):
+        return pltpu.SMEM((count,), jnp.int32)
+
+    lists = (
+        pltpu.VMEM((blocks, BLK, LANES), bf16),
+        numbers(pairs + STEPS[-1]),
+        numbers(pairs + 1),
+    )
+    wide = pltpu.VMEM((width, 2 * local_rows), bf16)
+
+    def call(kernel, name, ins, outs, scratch=(), aliases=None, spaces=()):
+        spaces = tuple(spaces) + (VM,) * (len(ins) - len(spaces))
         return pl.pallas_call(
             kernel,
             out_shape=outs,
-            in_specs=[FAR] * far + [VM] * (len(ins) - far),
-            out_specs=jax.tree.map(lambda _: VM, outs, is_leaf=lambda x: hasattr(x, "dtype")),
+            in_specs=list(spaces),
+            out_specs=jax.tree.map(
+                lambda x: SM if x.dtype == jnp.int32 else VM, outs, is_leaf=lambda x: hasattr(x, "dtype")
+            ),
             scratch_shapes=list(scratch),
             input_output_aliases=aliases or {},
             compiler_params=params,
             cost_estimate=pl.CostEstimate(flops=10**9, bytes_accessed=10**7, transcendentals=0),
             name=name,
-        )(*[pltpu.with_memory_space_constraint(x, pltpu.HBM) for x in ins[:far]], *[pltpu.with_memory_space_constraint(x, pltpu.VMEM) for x in ins[far:]])
-
-    payload, vec, noise = call(
+        )(*[pltpu.with_memory_space_constraint(x, space.memory_space) for x, space in zip(ins, spaces)])
+
+    payload, vec, noise, listed = call(
         prep_kernel,
         "prep",
-        (points.T, right_side, noise_var[None, :]),
-        (pltpu.VMEM((F + width, local_rows), bf16), pltpu.VMEM(full, f32), pltpu.VMEM((1, local_rows), f32)),
-        (pltpu.SemaphoreType.DMA((3,)),),
-        far=3,
+        (points.T, right_side, noise_var[None, :], pattern),
+        (
+            pltpu.VMEM((F + width, local_rows), bf16),
+            pltpu.VMEM(full, f32),
+            pltpu.VMEM((1, local_rows), f32),
+            pltpu.SMEM(pattern.shape, jnp.int32),
+        ),
+        (pltpu.SemaphoreType.DMA((4,)),),
+        spaces=(FAR,) * 4,
     )
     halo_a, halo_b = both_sides(payload)
     tiles, right, part = call(
         functools.partial(local_kernel, blocks),
         "local_tiles",
-        (pattern, payload),
+        (listed, payload),
         (tiles_type, pltpu.VMEM((blocks, LANES, BLK), bf16), pltpu.VMEM(full, f32)),
-        (left(1), listed, numbers(pairs), numbers(pairs), copied),
-        far=1,
+        lists,
+        spaces=(SM,),
+    )
+    tiles = call(
+        functools.partial(side_kernel, blocks),
+        "side_tiles",
+        (listed, halo_b, right, tiles),
+        tiles_type,
+        lists + (numbers(2),),
+        {3: 0},
+        spaces=(SM,),
     )
     tiles, image, low = call(
         functools.partial(first_kernel, blocks),
         "image",
-        (pattern, halo_a, halo_b, right, tiles, part, noise, vec),
+        (listed, halo_a, halo_b, right, tiles, part, noise, vec),
         (tiles_type, pltpu.VMEM(full, f32), pltpu.VMEM(full, bf16)),
-        (left(2), wide(width), listed, numbers(2 * pairs), copied),
+        lists + (numbers(2), wide),
         {4: 0},
-        far=1,
+        spaces=(SM,),
     )
     low_a, low_b = both_sides(low)
     part = call(
@@ -415,17 +458,19 @@
             pltpu.VMEM((width, local_rows + 3 * LANES), bf16),
             pltpu.VMEM((width, LANES), f32),
         ),
-        (wide(width),),
-    )
-    low_a, low_b = both_sides(low)
+        (wide,),
+    )
+    low_a = first_side(low)
+    part = call(functools.partial(own_kernel, blocks), "own_products_last", (low, tiles), pltpu.VMEM(full, f32))
+    low, part = lax.optimization_barrier((low, part))
+    low_b = second_side(low)
     sums = total_over_points(sums, low_a)
-    part = call(functools.partial(own_kernel, blocks), "own_products_last", (low, tiles), pltpu.VMEM(full, f32))
     prods = call(
         functools.partial(third_kernel, blocks),
         "products",
         (low_a, low_b, tiles, part),
         pltpu.VMEM(full, f32),
-        (wide(width),),
+        (wide,),
     )
     out = jax.ShapeDtypeStruct(full, f32)
     return call(last_kernel, "update", (sums, noise, vec, image, twice, prods), (out, out, out))

time: 51.4 us -> 47.6 us (0.926); the launches traced: 50.8 us -> 47.9 us
  Pallas kernels: 21.3 us -> 19.1 us
  starting transfers between devices: 24.5 us -> 23.6 us
    ppermute x6, starting transfers between devices: 19.8 us -> 16.9 us  [the longest x3 14.7 us: first_side(): return lax.ppermute(x, 'pts', swap_pairs(lax.axis_size('pts'), 0))]
    pallas_call x8 -> x9, Pallas kernels: 21.3 us -> 19.1 us  [call(): pl.pallas_call(kernel, out_shape=outs, in_specs=list(spaces), out_specs=j...]
    ppermute x3, starting transfers between devices: 4.67 us -> 6.78 us  [total_over_points(): lax.ppermute(x, 'pts', [(i, i ^ k * step) for i in range(count)])]
  transfers between devices with their start and end apart: 9 -> 9, of which waited for: 3 -> 5; matrix products, arithmetic and copies ran while one was open for 0% -> 0% of each run, Pallas kernels for 23% -> 23%
where the time goes in v6:
time: 47.6 us; the launch traced here: 47.9 us
  starting transfers between devices  23.6 us (50%)
  Pallas kernels  19.1 us (40%)
  waiting for transfers between devices  4.44 us (9%)
  between operations  0.69 us (1%)
    pallas_call x9, Pallas kernels, call(): pl.pallas_call(kernel, out_shape=outs, in_specs=list(spaces), out_specs=j...  19.1 us
    ppermute x3, starting transfers between devices, first_side(): return lax.ppermute(x, 'pts', swap_pairs(lax.axis_size('pts'), 0))  14.7 us
    ppermute x3, starting transfers between devices, total_over_points(): lax.ppermute(x, 'pts', [(i, i ^ k * step) for i in range(count)])  6.78 us
    ppermute x3, waiting for transfers between devices, total_over_points(): lax.ppermute(x, 'pts', [(i, i ^ k * step) for i in range(count)])  2.55 us
    ppermute x3, starting transfers between devices, second_side(): return lax.ppermute(x, 'pts', swap_pairs(lax.axis_size('pts'), 1))  2.18 us
    ppermute x3, waiting for transfers between devices, first_side(): return lax.ppermute(x, 'pts', swap_pairs(lax.axis_size('pts'), 0))  1.89 us
  transfers between devices with their start and end apart: 9, of which 5 were waited for; matrix products, arithmetic and copies ran while one was open for 0% of the time, Pallas kernels for 23%

profile of v6, /device:TPU:0, one launch (start us, length us, event | category | flops | bytes accessed | tf_op | source)
XLA Modules:
  0.0 47.9 jit_solution(4961009519537936535)
XLA Ops:
  0.6 1.0 %prep.1 = (bf16[48,2048]{1,0:T(8,128)(2,1)S(1)}, f32[16,2048]{1,0:T(8,128)S(1)}, f32[1,2048]{1,0:T(1,128)S(1)}, s32[16,33]{1,0:T(8,128)S(4)}) custom-call(bf16[32,2048]{1,0:T(8,128)(2,1)} %bitcast.2, f32[16,2048]{1,0:T(8,128)} %vec_ref.1, f32[1,2048]{1,0:T(1,128)} %bitcast.3, s32[16,33]{1,0:T(8,128)} %pattern_ref.1), custom_call_target="tpu_custom_call" | custom-call | flops 1000000000 | bytes 10000000 | tf_op jit(solution)/shard_map/prep/pallas_call | solution.py:394
  1.7 0.7 %collective-permute-start.1 = (bf16[48,2048]{1,0:T(8,128)(2,1)S(1)}, bf16[48,2048]{1,0:T(8,128)(2,1)S(1)}, u32[]{:S(2)}, u32[]{:S(2)}) collective-permute-start(bf16[48,2048]{1,0:T(8,128)(2,1)S(1)} %get-tuple-element.19.own_ref), channel_id=1, source_target_pairs={{4,8},{8,4},{12,16},{16,12},{20,24},{24,20},{5,9},{9,5},{13,17},{1... | collective-permute-start | bytes 589832 | tf_op jit(solution)/shard_map/ppermute | solution.py:340
  2.3 5.8 %collective-permute-start = (bf16[48,2048]{1,0:T(8,128)(2,1)S(1)}, bf16[48,2048]{1,0:T(8,128)(2,1)S(1)}, u32[]{:S(2)}, u32[]{:S(2)}) collective-permute-start(bf16[48,2048]{1,0:T(8,128)(2,1)S(1)} %get-tuple-element.19.own_ref), channel_id=1, source_target_pairs={{0,4},{4,0},{8,12},{12,8},{16,20},{20,16},{24,28},{28,24},{1,5},{5... | collective-permute-start | bytes 589832 | tf_op jit(solution)/shard_map/ppermute | solution.py:336
  8.1 5.1 %local_tiles.1 = (bf16[545,128,128]{2,1,0:T(8,128)(2,1)S(1)}, bf16[16,128,128]{2,1,0:T(8,128)(2,1)S(1)}, f32[16,2048]{1,0:T(8,128)S(1)}) custom-call(s32[16,33]{1,0:T(8,128)S(4)} %get-tuple-element.18.listed_ref, bf16[48,2048]{1,0:T(8,128)(2,1)S(1)} %get-tuple-element.19.own_ref), custom_call_target="tpu_custom_call" | custom-call | flops 1000000000 | bytes 10000000 | tf_op jit(solution)/shard_map/local_tiles/pallas_call | solution.py:394
  13.2 0.0 collective-permute-done.1.b_ref
  13.2 2.2 %side_tiles.1.tiles_in = bf16[545,128,128]{2,1,0:T(8,128)(2,1)S(1)} custom-call(s32[16,33]{1,0:T(8,128)S(4)} %get-tuple-element.18.listed_ref, bf16[48,2048]{1,0:T(8,128)(2,1)S(1)} %collective-permute-done.1.b_ref, bf16[16,128,128]{2,1,0:T(8,128)(2,1)S(1)} %get-tuple-element.20.right_ref, ...), custom_call_target="tpu_custom_call", output_to_operand_aliasing={{}: (3, {})} | custom-call | flops 1000000000 | bytes 10000000 | tf_op jit(solution)/shard_map/side_tiles/pallas_call | solution.py:394
  15.4 0.3 collective-permute-done.a_ref
  15.8 4.5 %image.1 = (bf16[545,128,128]{2,1,0:T(8,128)(2,1)S(1)}, f32[16,2048]{1,0:T(8,128)S(1)}, bf16[16,2048]{1,0:T(8,128)(2,1)S(1)}) custom-call(s32[16,33]{1,0:T(8,128)S(4)} %get-tuple-element.18.listed_ref, bf16[48,2048]{1,0:T(8,128)(2,1)S(1)} %collective-permute-done.a_ref, ...), custom_call_target="tpu_custom_call", output_to_operand_aliasing={{0}: (4, {})} | custom-call | flops 1000000000 | bytes 10000000 | tf_op jit(solution)/shard_map/image/pallas_call | solution.py:394
  20.2 0.8 %collective-permute-start.3 = (bf16[16,2048]{1,0:T(8,128)(2,1)S(1)}, bf16[16,2048]{1,0:T(8,128)(2,1)S(1)}, u32[]{:S(2)}, u32[]{:S(2)}) collective-permute-start(bf16[16,2048]{1,0:T(8,128)(2,1)S(1)} %get-tuple-element.25.own_ref), channel_id=1, source_target_pairs={{4,8},{8,4},{12,16},{16,12},{20,24},{24,20},{5,9},{9,5},{13,17},{1... | collective-permute-start | bytes 196616 | tf_op jit(solution)/shard_map/ppermute | solution.py:340
  21.1 6.8 %collective-permute-start.2 = (bf16[16,2048]{1,0:T(8,128)(2,1)S(1)}, bf16[16,2048]{1,0:T(8,128)(2,1)S(1)}, u32[]{:S(2)}, u32[]{:S(2)}) collective-permute-start(bf16[16,2048]{1,0:T(8,128)(2,1)S(1)} %get-tuple-element.25.own_ref), channel_id=1, source_target_pairs={{0,4},{4,0},{8,12},{12,8},{16,20},{20,16},{24,28},{28,24},{1,5},{5... | collective-permute-start | bytes 196616 | tf_op jit(solution)/shard_map/ppermute | solution.py:336
  27.9 1.2 %own_products.1.part_ref = f32[16,2048]{1,0:T(8,128)S(1)} custom-call(bf16[16,2048]{1,0:T(8,128)(2,1)S(1)} %get-tuple-element.25.own_ref, bf16[545,128,128]{2,1,0:T(8,128)(2,1)S(1)} %get-tuple-element.26.tiles_ref), custom_call_target="tpu_custom_call" | custom-call | flops 1000000000 | bytes 10000000 | tf_op jit(solution)/shard_map/own_products/pallas_call | solution.py:394
  29.1 0.0 collective-permute-done.3.b_ref
  29.1 1.0 %collective-permute-done.2.a_ref = bf16[16,2048]{1,0:T(8,128)(2,1)S(1)} collective-permute-done((bf16[16,2048]{1,0:T(8,128)(2,1)S(1)}, bf16[16,2048]{1,0:T(8,128)(2,1)S(1)}, u32[]{:S(2)}, u32[]{:S(2)}) %collective-permute-start.2) | collective-permute-done | bytes 65568 | tf_op jit(solution)/shard_map/ppermute | solution.py:336
  30.1 1.5 %twice.1 = (f32[16,2048]{1,0:T(8,128)S(1)}, bf16[16,2432]{1,0:T(8,128)(2,1)S(1)}, f32[16,128]{1,0:T(8,128)S(1)}) custom-call(bf16[16,2048]{1,0:T(8,128)(2,1)S(1)} %collective-permute-done.2.a_ref, bf16[16,2048]{1,0:T(8,128)(2,1)S(1)} %collective-permute-done.3.b_ref, bf16[545,128,128]{2,1,0:T(8,128)(2,1)S(1)} %get-tuple-element.26.tiles_ref, ...), custom_call_target="tpu_custom_call" | custom-call | flops 1000000000 | bytes 10000000 | tf_op jit(solution)/shard_map/twice/pallas_call | solution.py:394
  31.6 2.1 %collective-permute-start.4 = (bf16[16,2432]{1,0:T(8,128)(2,1)S(1)}, bf16[16,2432]{1,0:T(8,128)(2,1)S(1)}, u32[]{:S(2)}, u32[]{:S(2)}) collective-permute-start(bf16[16,2432]{1,0:T(8,128)(2,1)S(1)} %get-tuple-element.31.own_ref), channel_id=1, source_target_pairs={{0,4},{4,0},{8,12},{12,8},{16,20},{20,16},{24,28},{28,24},{1,5},{5... | collective-permute-start | bytes 233480 | tf_op jit(solution)/shard_map/ppermute | solution.py:336
  33.7 1.2 %own_products_last.1.part_ref = f32[16,2048]{1,0:T(8,128)S(1)} custom-call(bf16[16,2432]{1,0:T(8,128)(2,1)S(1)} %get-tuple-element.31.own_ref, bf16[545,128,128]{2,1,0:T(8,128)(2,1)S(1)} %get-tuple-element.26.tiles_ref), custom_call_target="tpu_custom_call" | custom-call | flops 1000000000 | bytes 10000000 | tf_op jit(solution)/shard_map/own_products_last/pallas_call | solution.py:394
  34.9 0.7 %collective-permute-start.8 = (bf16[16,2432]{1,0:T(8,128)(2,1)S(1)}, bf16[16,2432]{1,0:T(8,128)(2,1)S(1)}, u32[]{:S(2)}, u32[]{:S(2)}) collective-permute-start(bf16[16,2432]{1,0:T(8,128)(2,1)S(1)} %get-tuple-element.31.own_ref), channel_id=1, source_target_pairs={{4,8},{8,4},{12,16},{16,12},{20,24},{24,20},{5,9},{9,5},{13,17},{1... | collective-permute-start | bytes 233480 | tf_op jit(solution)/shard_map/ppermute | solution.py:340
  35.5 0.5 %collective-permute-done.4.a_ref = bf16[16,2432]{1,0:T(8,128)(2,1)S(1)} collective-permute-done((bf16[16,2432]{1,0:T(8,128)(2,1)S(1)}, bf16[16,2432]{1,0:T(8,128)(2,1)S(1)}, u32[]{:S(2)}, u32[]{:S(2)}) %collective-permute-start.4) | collective-permute-done | bytes 77856 | tf_op jit(solution)/shard_map/ppermute | solution.py:336
  36.1 6.1 %collective-permute-start.7 = (f32[16,128]{1,0:T(8,128)S(1)}, f32[16,128]{1,0:T(8,128)S(1)}, u32[]{:S(2)}, u32[]{:S(2)}) collective-permute-start(f32[16,128]{1,0:T(8,128)S(1)} %add_add_fusion.1), channel_id=1, source_target_pairs={{0,24},{4,28},{8,16},{12,20},{16,8},{20,12},{24,0},{28,4},{1,25},{... | collective-permute-start | bytes 24584 | tf_op jit(solution)/shard_map/ppermute | solution.py:362
  42.2 0.0 collective-permute-start.6
  42.2 0.6 %collective-permute-start.5 = (f32[16,128]{1,0:T(8,128)S(1)}, f32[16,128]{1,0:T(8,128)S(1)}, u32[]{:S(2)}, u32[]{:S(2)}) collective-permute-start(f32[16,128]{1,0:T(8,128)S(1)} %add_add_fusion.1), channel_id=1, source_target_pairs={{0,8},{4,12},{8,0},{12,4},{16,24},{20,28},{24,16},{28,20},{1,9},{5... | collective-permute-start | bytes 24584 | tf_op jit(solution)/shard_map/ppermute | solution.py:362
  42.9 0.0 collective-permute-done.8.b_ref
  42.9 1.4 %products.1.prod_ref = f32[16,2048]{1,0:T(8,128)S(1)} custom-call(bf16[16,2432]{1,0:T(8,128)(2,1)S(1)} %collective-permute-done.4.a_ref, bf16[16,2432]{1,0:T(8,128)(2,1)S(1)} %collective-permute-done.8.b_ref, bf16[545,128,128]{2,1,0:T(8,128)(2,1)S(1)} %get-tuple-element.26.tiles_ref, f32[16,2048]{1,0:T(8,128)S(1)} %own_products_last.1.part_ref), custom_call_target="tpu_custom_call" | custom-call | flops 1000000000 | bytes 10000000 | tf_op jit(solution)/shard_map/products/pallas_call | solution.py:394
  44.2 0.4 collective-permute-done.7
  44.6 2.1 %collective-permute-done.6 = f32[16,128]{1,0:T(8,128)S(1)} collective-permute-done((f32[16,128]{1,0:T(8,128)S(1)}, f32[16,128]{1,0:T(8,128)S(1)}, u32[]{:S(2)}, u32[]{:S(2)}) %collective-permute-start.6) | collective-permute-done | bytes 8224 | tf_op jit(solution)/shard_map/ppermute | solution.py:362
  46.8 0.0 collective-permute-done.5
  46.8 1.2 %update.1 = (f32[16,2048]{1,0:T(8,128)}, f32[16,2048]{1,0:T(8,128)}, f32[16,2048]{1,0:T(8,128)}) custom-call(f32[16,128]{1,0:T(8,128)S(1)} %add_add_fusion.sums_ref, f32[1,2048]{1,0:T(1,128)S(1)} %get-tuple-element.23.noise_ref, f32[16,2048]{1,0:T(8,128)S(1)} %get-tuple-element.24.vec_ref, f32[16,2048]{1,0:T(8,128)S(1)} %get-tuple-element.27.image_ref, ...), custom_call_target="tpu_custom_call" | custom-call | flops 1000000000 | bytes 10000000 | tf_op jit(solution)/shard_map/update/pallas_call | solution.py:394
  (2 shorter events, 0.0 us)
Async XLA Ops:
  1.7 11.5 %collective-permute-start.1 = (bf16[48,2048]{1,0:T(8,128)(2,1)S(1)}, bf16[48,2048]{1,0:T(8,128)(2,1)S(1)}, u32[]{:S(2)}, u32[]{:S(2)}) collective-permute-start(bf16[48,2048]{1,0:T(8,128)(2,1)S(1)} %get-tuple-element.19.own_ref), channel_id=1, source_target_pairs={{4,8},{8,4},{12,16},{16,12},{20,24},{24,20},{5,9},{9,5},{13,17},{1... | collective-permute-start | bytes 589832 | tf_op jit(solution)/shard_map/ppermute | solution.py:340
  2.3 13.4 %collective-permute-start = (bf16[48,2048]{1,0:T(8,128)(2,1)S(1)}, bf16[48,2048]{1,0:T(8,128)(2,1)S(1)}, u32[]{:S(2)}, u32[]{:S(2)}) collective-permute-start(bf16[48,2048]{1,0:T(8,128)(2,1)S(1)} %get-tuple-element.19.own_ref), channel_id=1, source_target_pairs={{0,4},{4,0},{8,12},{12,8},{16,20},{20,16},{24,28},{28,24},{1,5},{5... | collective-permute-start | bytes 589832 | tf_op jit(solution)/shard_map/ppermute | solution.py:336
  20.2 8.9 %collective-permute-start.3 = (bf16[16,2048]{1,0:T(8,128)(2,1)S(1)}, bf16[16,2048]{1,0:T(8,128)(2,1)S(1)}, u32[]{:S(2)}, u32[]{:S(2)}) collective-permute-start(bf16[16,2048]{1,0:T(8,128)(2,1)S(1)} %get-tuple-element.25.own_ref), channel_id=1, source_target_pairs={{4,8},{8,4},{12,16},{16,12},{20,24},{24,20},{5,9},{9,5},{13,17},{1... | collective-permute-start | bytes 196616 | tf_op jit(solution)/shard_map/ppermute | solution.py:340
  21.1 9.1 %collective-permute-start.2 = (bf16[16,2048]{1,0:T(8,128)(2,1)S(1)}, bf16[16,2048]{1,0:T(8,128)(2,1)S(1)}, u32[]{:S(2)}, u32[]{:S(2)}) collective-permute-start(bf16[16,2048]{1,0:T(8,128)(2,1)S(1)} %get-tuple-element.25.own_ref), channel_id=1, source_target_pairs={{0,4},{4,0},{8,12},{12,8},{16,20},{20,16},{24,28},{28,24},{1,5},{5... | collective-permute-start | bytes 196616 | tf_op jit(solution)/shard_map/ppermute | solution.py:336
  31.6 4.5 %collective-permute-start.4 = (bf16[16,2432]{1,0:T(8,128)(2,1)S(1)}, bf16[16,2432]{1,0:T(8,128)(2,1)S(1)}, u32[]{:S(2)}, u32[]{:S(2)}) collective-permute-start(bf16[16,2432]{1,0:T(8,128)(2,1)S(1)} %get-tuple-element.31.own_ref), channel_id=1, source_target_pairs={{0,4},{4,0},{8,12},{12,8},{16,20},{20,16},{24,28},{28,24},{1,5},{5... | collective-permute-start | bytes 233480 | tf_op jit(solution)/shard_map/ppermute | solution.py:336
  34.9 8.0 %collective-permute-start.8 = (bf16[16,2432]{1,0:T(8,128)(2,1)S(1)}, bf16[16,2432]{1,0:T(8,128)(2,1)S(1)}, u32[]{:S(2)}, u32[]{:S(2)}) collective-permute-start(bf16[16,2432]{1,0:T(8,128)(2,1)S(1)} %get-tuple-element.31.own_ref), channel_id=1, source_target_pairs={{4,8},{8,4},{12,16},{16,12},{20,24},{24,20},{5,9},{9,5},{13,17},{1... | collective-permute-start | bytes 233480 | tf_op jit(solution)/shard_map/ppermute | solution.py:340
  36.1 8.6 %collective-permute-start.7 = (f32[16,128]{1,0:T(8,128)S(1)}, f32[16,128]{1,0:T(8,128)S(1)}, u32[]{:S(2)}, u32[]{:S(2)}) collective-permute-start(f32[16,128]{1,0:T(8,128)S(1)} %add_add_fusion.1), channel_id=1, source_target_pairs={{0,24},{4,28},{8,16},{12,20},{16,8},{20,12},{24,0},{28,4},{1,25},{... | collective-permute-start | bytes 24584 | tf_op jit(solution)/shard_map/ppermute | solution.py:362
  42.2 4.5 %collective-permute-start.6 = (f32[16,128]{1,0:T(8,128)S(1)}, f32[16,128]{1,0:T(8,128)S(1)}, u32[]{:S(2)}, u32[]{:S(2)}) collective-permute-start(f32[16,128]{1,0:T(8,128)S(1)} %add_add_fusion.1), channel_id=1, source_target_pairs={{0,16},{4,20},{8,24},{12,28},{16,0},{20,4},{24,8},{28,12},{1,17},{... | collective-permute-start | bytes 24584 | tf_op jit(solution)/shard_map/ppermute | solution.py:362
  42.2 4.5 %collective-permute-start.5 = (f32[16,128]{1,0:T(8,128)S(1)}, f32[16,128]{1,0:T(8,128)S(1)}, u32[]{:S(2)}, u32[]{:S(2)}) collective-permute-start(f32[16,128]{1,0:T(8,128)S(1)} %add_add_fusion.1), channel_id=1, source_target_pairs={{0,8},{4,12},{8,0},{12,4},{16,24},{20,28},{24,16},{28,20},{1,9},{5... | collective-permute-start | bytes 24584 | tf_op jit(solution)/shard_map/ppermute | solution.py:362

commit v7 on v6

--- a/solution.py
+++ b/solution.py
@@ -19,7 +19,7 @@
 SCALE = 1.0 / (4 * BLK)
 SHIFT = 2.0 / (0.5 + 0.6)
 SUMS = 9
-STEPS = (32, 16, 8)
+STEPS = (48, 16, 8)
 FIELD = 10
 MIB = 1 << 20
 
@@ -131,16 +131,17 @@
         list_ref[count + k] = jnp.int32(entry(spare, spare, 0, 0))
 
 
-def clear_tiles(count, list_ref, tiles_ref):
+def clear_tiles(first, last, list_ref, tiles_ref, mirrored):
     mask = (1 << FIELD) - 1
 
     def step(at, carry):
         code = list_ref[at]
         tiles_ref[code & mask] = jnp.zeros((BLK, BLK), bf16)
-        tiles_ref[(code >> FIELD) & mask] = jnp.zeros((BLK, BLK), bf16)
+        if mirrored:
+            tiles_ref[(code >> FIELD) & mask] = jnp.zeros((BLK, BLK), bf16)
         return carry
 
-    lax.fori_loop(0, count, step, 0)
+    lax.fori_loop(first, last, step, 0)
 
 
 def products(vec, tiles_ref, first, wide):
@@ -191,7 +192,7 @@
     pattern_copy.wait()
 
 
-def local_kernel(blocks, listed_ref, own_ref, tiles_ref, right_ref, part_ref, left_ref, list_ref, dead_ref):
+def local_kernel(blocks, listed_ref, own_ref, tiles_ref, right_ref, part_ref, left_ref, list_ref):
     fill_features(own_ref[:F, :], left_ref, 0, right_ref)
     for pair in range(blocks // 2):
         first = blocks * blocks + pair * 2 * (blocks + 2)
@@ -201,26 +202,24 @@
         (entry(local_slot(blocks, home, other), local_slot(blocks, other, home), other, home), home, column)
         for home, other, column in local_entries(blocks)
     ]
-    count, dead = scan_entries(entries, listed_ref, list_ref, dead_ref)
+    count = scan_entries(entries, listed_ref, list_ref)
+    clear_tiles(count + STEPS[-1], list_ref.shape[0], list_ref, tiles_ref, True)
     pad_list(count, list_ref, spare_slot(blocks))
-    clear_tiles(dead, dead_ref, tiles_ref)
     make_tiles(count, list_ref, left_ref, right_ref, tiles_ref, True)
     local_products(blocks, own_ref[F:, :], tiles_ref, part_ref)
 
 
-def scan_entries(entries, listed_ref, list_ref, dead_ref):
+def scan_entries(entries, listed_ref, list_ref):
+    size = list_ref.shape[0]
     count = jnp.int32(0)
-    dead = jnp.int32(0)
-    for code, home, column in entries:
+    for at, (code, home, column) in enumerate(entries):
         live = listed_ref[home, column]
-        list_ref[count] = jnp.int32(code)
-        dead_ref[dead] = jnp.int32(code)
+        list_ref[jnp.where(live == 1, count, size - 1 - at + count)] = jnp.int32(code)
         count = count + live
-        dead = dead + (1 - live)
-    return count, dead
-
-
-def make_side(blocks, before, listed_ref, points, right_ref, tiles_ref, left_ref, list_ref, dead_ref, count_ref):
+    return count
+
+
+def make_side(blocks, before, listed_ref, points, right_ref, tiles_ref, left_ref, list_ref, count_ref):
     fill_features(points, left_ref, 0)
     for after in (False, True):
 
@@ -230,33 +229,31 @@
             for home, other, column in side_entries(blocks, after):
                 slot = side_slot(blocks, home, other, after)
                 entries.append((entry(slot, slot, other, home), home, column))
-            count, dead = scan_entries(entries, listed_ref, list_ref, dead_ref)
-            count_ref[0] = count
-            count_ref[1] = dead
+            count_ref[0] = scan_entries(entries, listed_ref, list_ref)
 
     count = count_ref[0]
+    clear_tiles(count + STEPS[-1], list_ref.shape[0], list_ref, tiles_ref, False)
     pad_list(count, list_ref, spare_slot(blocks))
-    clear_tiles(count_ref[1], dead_ref, tiles_ref)
     make_tiles(count, list_ref, left_ref, right_ref, tiles_ref, False)
 
 
 def side_kernel(
-    blocks, listed_ref, b_ref, right_ref, tiles_in, tiles_ref, left_ref, list_ref, dead_ref, count_ref
+    blocks, listed_ref, b_ref, right_ref, tiles_in, tiles_ref, left_ref, list_ref, count_ref
 ):
     del tiles_in
     make_side(
-        blocks, 1 - odd_place(), listed_ref, b_ref[:F, :], right_ref, tiles_ref, left_ref, list_ref, dead_ref, count_ref
+        blocks, 1 - odd_place(), listed_ref, b_ref[:F, :], right_ref, tiles_ref, left_ref, list_ref, count_ref
     )
 
 
 def first_kernel(
     blocks, listed_ref, a_ref, b_ref, right_ref, tiles_in, part_ref, noise_ref, vec_ref,
-    tiles_ref, image_ref, low_ref, left_ref, list_ref, dead_ref, count_ref, wide_ref,
+    tiles_ref, image_ref, low_ref, left_ref, list_ref, count_ref, wide_ref,
 ):
     del tiles_in
     before = odd_place()
     make_side(
-        blocks, before, listed_ref, a_ref[:F, :], right_ref, tiles_ref, left_ref, list_ref, dead_ref, count_ref
+        blocks, before, listed_ref, a_ref[:F, :], right_ref, tiles_ref, left_ref, list_ref, count_ref
     )
     gather_sides(blocks, before, a_ref[F:, :], b_ref[F:, :], wide_ref)
     for pair in range(blocks // 2):
@@ -269,6 +266,10 @@
 
 def own_kernel(blocks, own_ref, tiles_ref, part_ref):
     local_products(blocks, own_ref[:, : blocks * BLK], tiles_ref, part_ref)
+
+
+def copy_kernel(columns, from_ref, to_ref):
+    to_ref[...] = from_ref[:, :columns]
 
 
 def second_kernel(
@@ -301,7 +302,7 @@
 
 def third_kernel(blocks, a_ref, b_ref, tiles_ref, part_ref, out_ref, wide_ref):
     points = blocks * BLK
-    gather_sides(blocks, odd_place(), a_ref[:, :points], b_ref[:, :points], wide_ref)
+    gather_sides(blocks, odd_place(), a_ref[:, :points], b_ref[...], wide_ref)
     for pair in range(blocks // 2):
         cols = pair_cols(pair)
         out_ref[:, cols] = (part_ref[:, cols] + side_products(blocks, pair, wide_ref, tiles_ref)) * SCALE
@@ -385,7 +386,6 @@
     lists = (
         pltpu.VMEM((blocks, BLK, LANES), bf16),
         numbers(pairs + STEPS[-1]),
-        numbers(pairs + 1),
     )
     wide = pltpu.VMEM((width, 2 * local_rows), bf16)
 
@@ -461,10 +461,12 @@
         (wide,),
     )
     low_a = first_side(low)
+    low_b = second_side(
+        call(functools.partial(copy_kernel, local_rows), "second_message", (low,), pltpu.VMEM(full, bf16))
+    )
+    low, low_a = lax.optimization_barrier((low, low_a))
+    sums = total_over_points(sums, low_a)
     part = call(functools.partial(own_kernel, blocks), "own_products_last", (low, tiles), pltpu.VMEM(full, f32))
-    low, part = lax.optimization_barrier((low, part))
-    low_b = second_side(low)
-    sums = total_over_points(sums, low_a)
     prods = call(
         functools.partial(third_kernel, blocks),
         "products",

time: 47.6 us -> 45.4 us (0.954); the launches traced: 47.9 us -> 45 us
  starting transfers between devices: 23.6 us -> 21.8 us
  waiting for transfers between devices: 4.44 us -> 3.71 us
    ppermute x3, waiting for transfers between devices: 2.55 us -> 0.01 us  [total_over_points(): lax.ppermute(x, 'pts', [(i, i ^ k * step) for i in range(count)])]
    ppermute x3, starting transfers between devices: 6.78 us -> 4.39 us  [total_over_points(): lax.ppermute(x, 'pts', [(i, i ^ k * step) for i in range(count)])]
    ppermute x3, waiting for transfers between devices: 1.89 us -> 3.69 us  [first_side(): return lax.ppermute(x, 'pts', swap_pairs(lax.axis_size('pts'), 0))]
    ppermute x3, starting transfers between devices: 14.7 us -> 15.4 us  [first_side(): return lax.ppermute(x, 'pts', swap_pairs(lax.axis_size('pts'), 0))]
    pallas_call x9 -> x10, Pallas kernels: 19.1 us -> 18.8 us  [call(): pl.pallas_call(kernel, out_shape=outs, in_specs=list(spaces), out_specs=j...]
  transfers between devices with their start and end apart: 9 -> 9, of which waited for: 5 -> 3; matrix products, arithmetic and copies ran while one was open for 0% -> 0% of each run, Pallas kernels for 23% -> 24%
where the time goes in v7:
time: 45.4 us; the launch traced here: 45 us
  starting transfers between devices  21.8 us (48%)
  Pallas kernels  18.8 us (41%)
  waiting for transfers between devices  3.71 us (8%)
  between operations  0.71 us (2%)
    pallas_call x10, Pallas kernels, call(): pl.pallas_call(kernel, out_shape=outs, in_specs=list(spaces), out_specs=j...  18.8 us
    ppermute x3, starting transfers between devices, first_side(): return lax.ppermute(x, 'pts', swap_pairs(lax.axis_size('pts'), 0))  15.4 us
    ppermute x3, starting transfers between devices, total_over_points(): lax.ppermute(x, 'pts', [(i, i ^ k * step) for i in range(count)])  4.39 us
    ppermute x3, waiting for transfers between devices, first_side(): return lax.ppermute(x, 'pts', swap_pairs(lax.axis_size('pts'), 0))  3.69 us
    ppermute x3, starting transfers between devices, second_side(): return lax.ppermute(x, 'pts', swap_pairs(lax.axis_size('pts'), 1))  1.99 us
  transfers between devices with their start and end apart: 9, of which 3 were waited for; matrix products, arithmetic and copies ran while one was open for 0% of the time, Pallas kernels for 24%

profile of v7, /device:TPU:0, one launch (start us, length us, event | category | flops | bytes accessed | tf_op | source)
XLA Modules:
  0.0 45.0 jit_solution(9259096271555092219)
XLA Ops:
  0.6 1.0 %prep.1 = (bf16[48,2048]{1,0:T(8,128)(2,1)S(1)}, f32[16,2048]{1,0:T(8,128)S(1)}, f32[1,2048]{1,0:T(1,128)S(1)}, s32[16,33]{1,0:T(8,128)S(4)}) custom-call(bf16[32,2048]{1,0:T(8,128)(2,1)} %bitcast.2, f32[16,2048]{1,0:T(8,128)} %vec_ref.1, f32[1,2048]{1,0:T(1,128)} %bitcast.3, s32[16,33]{1,0:T(8,128)} %pattern_ref.1), custom_call_target="tpu_custom_call" | custom-call | flops 1000000000 | bytes 10000000 | tf_op jit(solution)/shard_map/prep/pallas_call | solution.py:394
  1.7 0.7 %collective-permute-start.1 = (bf16[48,2048]{1,0:T(8,128)(2,1)S(1)}, bf16[48,2048]{1,0:T(8,128)(2,1)S(1)}, u32[]{:S(2)}, u32[]{:S(2)}) collective-permute-start(bf16[48,2048]{1,0:T(8,128)(2,1)S(1)} %get-tuple-element.19.own_ref), channel_id=1, source_target_pairs={{4,8},{8,4},{12,16},{16,12},{20,24},{24,20},{5,9},{9,5},{13,17},{1... | collective-permute-start | bytes 589832 | tf_op jit(solution)/shard_map/ppermute | solution.py:341
  2.3 5.8 %collective-permute-start = (bf16[48,2048]{1,0:T(8,128)(2,1)S(1)}, bf16[48,2048]{1,0:T(8,128)(2,1)S(1)}, u32[]{:S(2)}, u32[]{:S(2)}) collective-permute-start(bf16[48,2048]{1,0:T(8,128)(2,1)S(1)} %get-tuple-element.19.own_ref), channel_id=1, source_target_pairs={{0,4},{4,0},{8,12},{12,8},{16,20},{20,16},{24,28},{28,24},{1,5},{5... | collective-permute-start | bytes 589832 | tf_op jit(solution)/shard_map/ppermute | solution.py:337
  8.1 5.1 %local_tiles.1 = (bf16[545,128,128]{2,1,0:T(8,128)(2,1)S(1)}, bf16[16,128,128]{2,1,0:T(8,128)(2,1)S(1)}, f32[16,2048]{1,0:T(8,128)S(1)}) custom-call(s32[16,33]{1,0:T(8,128)S(4)} %get-tuple-element.18.listed_ref, bf16[48,2048]{1,0:T(8,128)(2,1)S(1)} %get-tuple-element.19.own_ref), custom_call_target="tpu_custom_call" | custom-call | flops 1000000000 | bytes 10000000 | tf_op jit(solution)/shard_map/local_tiles/pallas_call | solution.py:394
  13.3 0.0 collective-permute-done.1.b_ref
  13.3 1.8 %side_tiles.1.tiles_in = bf16[545,128,128]{2,1,0:T(8,128)(2,1)S(1)} custom-call(s32[16,33]{1,0:T(8,128)S(4)} %get-tuple-element.18.listed_ref, bf16[48,2048]{1,0:T(8,128)(2,1)S(1)} %collective-permute-done.1.b_ref, bf16[16,128,128]{2,1,0:T(8,128)(2,1)S(1)} %get-tuple-element.20.right_ref, ...), custom_call_target="tpu_custom_call", output_to_operand_aliasing={{}: (3, {})} | custom-call | flops 1000000000 | bytes 10000000 | tf_op jit(solution)/shard_map/side_tiles/pallas_call | solution.py:394
  15.1 0.7 %collective-permute-done.a_ref = bf16[48,2048]{1,0:T(8,128)(2,1)S(1)} collective-permute-done((bf16[48,2048]{1,0:T(8,128)(2,1)S(1)}, bf16[48,2048]{1,0:T(8,128)(2,1)S(1)}, u32[]{:S(2)}, u32[]{:S(2)}) %collective-permute-start) | collective-permute-done | bytes 196640 | tf_op jit(solution)/shard_map/ppermute | solution.py:337
  15.8 4.5 %image.1 = (bf16[545,128,128]{2,1,0:T(8,128)(2,1)S(1)}, f32[16,2048]{1,0:T(8,128)S(1)}, bf16[16,2048]{1,0:T(8,128)(2,1)S(1)}) custom-call(s32[16,33]{1,0:T(8,128)S(4)} %get-tuple-element.18.listed_ref, bf16[48,2048]{1,0:T(8,128)(2,1)S(1)} %collective-permute-done.a_ref, ...), custom_call_target="tpu_custom_call", output_to_operand_aliasing={{0}: (4, {})} | custom-call | flops 1000000000 | bytes 10000000 | tf_op jit(solution)/shard_map/image/pallas_call | solution.py:394
  20.2 0.7 %collective-permute-start.3 = (bf16[16,2048]{1,0:T(8,128)(2,1)S(1)}, bf16[16,2048]{1,0:T(8,128)(2,1)S(1)}, u32[]{:S(2)}, u32[]{:S(2)}) collective-permute-start(bf16[16,2048]{1,0:T(8,128)(2,1)S(1)} %get-tuple-element.25.own_ref), channel_id=1, source_target_pairs={{4,8},{8,4},{12,16},{16,12},{20,24},{24,20},{5,9},{9,5},{13,17},{1... | collective-permute-start | bytes 196616 | tf_op jit(solution)/shard_map/ppermute | solution.py:341
  20.9 7.5 %collective-permute-start.2 = (bf16[16,2048]{1,0:T(8,128)(2,1)S(1)}, bf16[16,2048]{1,0:T(8,128)(2,1)S(1)}, u32[]{:S(2)}, u32[]{:S(2)}) collective-permute-start(bf16[16,2048]{1,0:T(8,128)(2,1)S(1)} %get-tuple-element.25.own_ref), channel_id=1, source_target_pairs={{0,4},{4,0},{8,12},{12,8},{16,20},{20,16},{24,28},{28,24},{1,5},{5... | collective-permute-start | bytes 196616 | tf_op jit(solution)/shard_map/ppermute | solution.py:337
  28.4 1.2 %own_products.1.part_ref = f32[16,2048]{1,0:T(8,128)S(1)} custom-call(bf16[16,2048]{1,0:T(8,128)(2,1)S(1)} %get-tuple-element.25.own_ref, bf16[545,128,128]{2,1,0:T(8,128)(2,1)S(1)} %get-tuple-element.26.tiles_ref), custom_call_target="tpu_custom_call" | custom-call | flops 1000000000 | bytes 10000000 | tf_op jit(solution)/shard_map/own_products/pallas_call | solution.py:394
  29.6 0.0 collective-permute-done.3.b_ref
  29.6 1.0 %collective-permute-done.2.a_ref = bf16[16,2048]{1,0:T(8,128)(2,1)S(1)} collective-permute-done((bf16[16,2048]{1,0:T(8,128)(2,1)S(1)}, bf16[16,2048]{1,0:T(8,128)(2,1)S(1)}, u32[]{:S(2)}, u32[]{:S(2)}) %collective-permute-start.2) | collective-permute-done | bytes 65568 | tf_op jit(solution)/shard_map/ppermute | solution.py:337
  30.7 1.5 %twice.1 = (f32[16,2048]{1,0:T(8,128)S(1)}, bf16[16,2432]{1,0:T(8,128)(2,1)S(1)}, f32[16,128]{1,0:T(8,128)S(1)}) custom-call(bf16[16,2048]{1,0:T(8,128)(2,1)S(1)} %collective-permute-done.2.a_ref, bf16[16,2048]{1,0:T(8,128)(2,1)S(1)} %collective-permute-done.3.b_ref, bf16[545,128,128]{2,1,0:T(8,128)(2,1)S(1)} %get-tuple-element.26.tiles_ref, ...), custom_call_target="tpu_custom_call" | custom-call | flops 1000000000 | bytes 10000000 | tf_op jit(solution)/shard_map/twice/pallas_call | solution.py:394
  32.2 2.1 %collective-permute-start.4 = (bf16[16,2432]{1,0:T(8,128)(2,1)S(1)}, bf16[16,2432]{1,0:T(8,128)(2,1)S(1)}, u32[]{:S(2)}, u32[]{:S(2)}) collective-permute-start(bf16[16,2432]{1,0:T(8,128)(2,1)S(1)} %get-tuple-element.32.from_ref.own_ref), channel_id=1, source_target_pairs={{0,4},{4,0},{8,12},{12,8},{16,20},{20,16},{24,28},{28,24},{1,5},{5... | collective-permute-start | bytes 233480 | tf_op jit(solution)/shard_map/ppermute | solution.py:337
  34.2 0.7 %collective-permute-start.8 = (bf16[16,2048]{1,0:T(8,128)(2,1)S(1)}, bf16[16,2048]{1,0:T(8,128)(2,1)S(1)}, u32[]{:S(2)}, u32[]{:S(2)}) collective-permute-start(bf16[16,2048]{1,0:T(8,128)(2,1)S(1)} %second_message.1), channel_id=1, source_target_pairs={{4,8},{8,4},{12,16},{16,12},{20,24},{24,20},{5,9},{9,5},{13,17},{1... | collective-permute-start | bytes 196616 | tf_op jit(solution)/shard_map/ppermute | solution.py:341
  34.9 2.0 %collective-permute-done.4.a_ref = bf16[16,2432]{1,0:T(8,128)(2,1)S(1)} collective-permute-done((bf16[16,2432]{1,0:T(8,128)(2,1)S(1)}, bf16[16,2432]{1,0:T(8,128)(2,1)S(1)}, u32[]{:S(2)}, u32[]{:S(2)}) %collective-permute-start.4) | collective-permute-done | bytes 77856 | tf_op jit(solution)/shard_map/ppermute | solution.py:337
  36.9 2.3 %collective-permute-start.7 = (f32[16,128]{1,0:T(8,128)S(1)}, f32[16,128]{1,0:T(8,128)S(1)}, u32[]{:S(2)}, u32[]{:S(2)}) collective-permute-start(f32[16,128]{1,0:T(8,128)S(1)} %add_add_fusion.1), channel_id=1, source_target_pairs={{0,24},{4,28},{8,16},{12,20},{16,8},{20,12},{24,0},{28,4},{1,25},{... | collective-permute-start | bytes 24584 | tf_op jit(solution)/shard_map/ppermute | solution.py:363
  39.2 0.3 collective-permute-start.6
  39.5 1.8 %collective-permute-start.5 = (f32[16,128]{1,0:T(8,128)S(1)}, f32[16,128]{1,0:T(8,128)S(1)}, u32[]{:S(2)}, u32[]{:S(2)}) collective-permute-start(f32[16,128]{1,0:T(8,128)S(1)} %add_add_fusion.1), channel_id=1, source_target_pairs={{0,8},{4,12},{8,0},{12,4},{16,24},{20,28},{24,16},{28,20},{1,9},{5... | collective-permute-start | bytes 24584 | tf_op jit(solution)/shard_map/ppermute | solution.py:363
  41.3 1.2 %own_products_last.1.part_ref = f32[16,2048]{1,0:T(8,128)S(1)} custom-call(bf16[16,2432]{1,0:T(8,128)(2,1)S(1)} %get-tuple-element.32.from_ref.own_ref, bf16[545,128,128]{2,1,0:T(8,128)(2,1)S(1)} %get-tuple-element.26.tiles_ref), custom_call_target="tpu_custom_call" | custom-call | flops 1000000000 | bytes 10000000 | tf_op jit(solution)/shard_map/own_products_last/pallas_call | solution.py:394
  42.5 0.0 collective-permute-done.8.b_ref
  42.5 1.4 %products.1.prod_ref = f32[16,2048]{1,0:T(8,128)S(1)} custom-call(bf16[16,2432]{1,0:T(8,128)(2,1)S(1)} %collective-permute-done.4.a_ref, bf16[16,2048]{1,0:T(8,128)(2,1)S(1)} %collective-permute-done.8.b_ref, bf16[545,128,128]{2,1,0:T(8,128)(2,1)S(1)} %get-tuple-element.26.tiles_ref, f32[16,2048]{1,0:T(8,128)S(1)} %own_products_last.1.part_ref), custom_call_target="tpu_custom_call" | custom-call | flops 1000000000 | bytes 10000000 | tf_op jit(solution)/shard_map/products/pallas_call | solution.py:394
  43.8 0.0 collective-permute-done.7
  43.8 0.0 collective-permute-done.6
  43.9 0.0 collective-permute-done.5
  43.9 1.2 %update.1 = (f32[16,2048]{1,0:T(8,128)}, f32[16,2048]{1,0:T(8,128)}, f32[16,2048]{1,0:T(8,128)}) custom-call(f32[16,128]{1,0:T(8,128)S(1)} %add_add_fusion.sums_ref, f32[1,2048]{1,0:T(1,128)S(1)} %get-tuple-element.23.noise_ref, f32[16,2048]{1,0:T(8,128)S(1)} %get-tuple-element.24.vec_ref, f32[16,2048]{1,0:T(8,128)S(1)} %get-tuple-element.27.image_ref, ...), custom_call_target="tpu_custom_call" | custom-call | flops 1000000000 | bytes 10000000 | tf_op jit(solution)/shard_map/update/pallas_call | solution.py:394
  (3 shorter events, 0.0 us)
Async XLA Ops:
  1.7 11.6 %collective-permute-start.1 = (bf16[48,2048]{1,0:T(8,128)(2,1)S(1)}, bf16[48,2048]{1,0:T(8,128)(2,1)S(1)}, u32[]{:S(2)}, u32[]{:S(2)}) collective-permute-start(bf16[48,2048]{1,0:T(8,128)(2,1)S(1)} %get-tuple-element.19.own_ref), channel_id=1, source_target_pairs={{4,8},{8,4},{12,16},{16,12},{20,24},{24,20},{5,9},{9,5},{13,17},{1... | collective-permute-start | bytes 589832 | tf_op jit(solution)/shard_map/ppermute | solution.py:341
  2.3 13.4 %collective-permute-start = (bf16[48,2048]{1,0:T(8,128)(2,1)S(1)}, bf16[48,2048]{1,0:T(8,128)(2,1)S(1)}, u32[]{:S(2)}, u32[]{:S(2)}) collective-permute-start(bf16[48,2048]{1,0:T(8,128)(2,1)S(1)} %get-tuple-element.19.own_ref), channel_id=1, source_target_pairs={{0,4},{4,0},{8,12},{12,8},{16,20},{20,16},{24,28},{28,24},{1,5},{5... | collective-permute-start | bytes 589832 | tf_op jit(solution)/shard_map/ppermute | solution.py:337
  20.2 9.4 %collective-permute-start.3 = (bf16[16,2048]{1,0:T(8,128)(2,1)S(1)}, bf16[16,2048]{1,0:T(8,128)(2,1)S(1)}, u32[]{:S(2)}, u32[]{:S(2)}) collective-permute-start(bf16[16,2048]{1,0:T(8,128)(2,1)S(1)} %get-tuple-element.25.own_ref), channel_id=1, source_target_pairs={{4,8},{8,4},{12,16},{16,12},{20,24},{24,20},{5,9},{9,5},{13,17},{1... | collective-permute-start | bytes 196616 | tf_op jit(solution)/shard_map/ppermute | solution.py:341
  20.9 9.8 %collective-permute-start.2 = (bf16[16,2048]{1,0:T(8,128)(2,1)S(1)}, bf16[16,2048]{1,0:T(8,128)(2,1)S(1)}, u32[]{:S(2)}, u32[]{:S(2)}) collective-permute-start(bf16[16,2048]{1,0:T(8,128)(2,1)S(1)} %get-tuple-element.25.own_ref), channel_id=1, source_target_pairs={{0,4},{4,0},{8,12},{12,8},{16,20},{20,16},{24,28},{28,24},{1,5},{5... | collective-permute-start | bytes 196616 | tf_op jit(solution)/shard_map/ppermute | solution.py:337
  32.2 4.7 %collective-permute-start.4 = (bf16[16,2432]{1,0:T(8,128)(2,1)S(1)}, bf16[16,2432]{1,0:T(8,128)(2,1)S(1)}, u32[]{:S(2)}, u32[]{:S(2)}) collective-permute-start(bf16[16,2432]{1,0:T(8,128)(2,1)S(1)} %get-tuple-element.32.from_ref.own_ref), channel_id=1, source_target_pairs={{0,4},{4,0},{8,12},{12,8},{16,20},{20,16},{24,28},{28,24},{1,5},{5... | collective-permute-start | bytes 233480 | tf_op jit(solution)/shard_map/ppermute | solution.py:337
  34.2 8.2 %collective-permute-start.8 = (bf16[16,2048]{1,0:T(8,128)(2,1)S(1)}, bf16[16,2048]{1,0:T(8,128)(2,1)S(1)}, u32[]{:S(2)}, u32[]{:S(2)}) collective-permute-start(bf16[16,2048]{1,0:T(8,128)(2,1)S(1)} %second_message.1), channel_id=1, source_target_pairs={{4,8},{8,4},{12,16},{16,12},{20,24},{24,20},{5,9},{9,5},{13,17},{1... | collective-permute-start | bytes 196616 | tf_op jit(solution)/shard_map/ppermute | solution.py:341
  36.9 7.0 %collective-permute-start.7 = (f32[16,128]{1,0:T(8,128)S(1)}, f32[16,128]{1,0:T(8,128)S(1)}, u32[]{:S(2)}, u32[]{:S(2)}) collective-permute-start(f32[16,128]{1,0:T(8,128)S(1)} %add_add_fusion.1), channel_id=1, source_target_pairs={{0,24},{4,28},{8,16},{12,20},{16,8},{20,12},{24,0},{28,4},{1,25},{... | collective-permute-start | bytes 24584 | tf_op jit(solution)/shard_map/ppermute | solution.py:363
  39.2 4.6 %collective-permute-start.6 = (f32[16,128]{1,0:T(8,128)S(1)}, f32[16,128]{1,0:T(8,128)S(1)}, u32[]{:S(2)}, u32[]{:S(2)}) collective-permute-start(f32[16,128]{1,0:T(8,128)S(1)} %add_add_fusion.1), channel_id=1, source_target_pairs={{0,16},{4,20},{8,24},{12,28},{16,0},{20,4},{24,8},{28,12},{1,17},{... | collective-permute-start | bytes 24584 | tf_op jit(solution)/shard_map/ppermute | solution.py:363
  39.5 4.4 %collective-permute-start.5 = (f32[16,128]{1,0:T(8,128)S(1)}, f32[16,128]{1,0:T(8,128)S(1)}, u32[]{:S(2)}, u32[]{:S(2)}) collective-permute-start(f32[16,128]{1,0:T(8,128)S(1)} %add_add_fusion.1), channel_id=1, source_target_pairs={{0,8},{4,12},{8,0},{12,4},{16,24},{20,28},{24,16},{28,20},{1,9},{5... | collective-permute-start | bytes 24584 | tf_op jit(solution)/shard_map/ppermute | solution.py:363
